TPU v7x, 32 devices: a whole 2x2x4 slice. The times are simulated.
32 devices in a mesh: row: 16 (over z, x, core), col: 2 (over y).
Axes of the slice: x: 2, y: 2, z: 4, core: 2. Of those that a mesh axis runs over, the one named last changes fastest.
Arguments:
- pair: bfloat16 [512, 512, 128], P('row', 'col'), may hold values from -6 to 6
- cotangent: bfloat16 [64, 512, 512], P(None, 'row', 'col'), may hold values from -0.59765625 to 0.59765625
- w_left: bfloat16 [128, 64], replicated, may hold values from -0.5 to 0.5
- w_left_gate: bfloat16 [128, 64], replicated, may hold values from -0.5 to 0.5
- w_right: bfloat16 [128, 64], replicated, may hold values from -0.5 to 0.5
- w_right_gate: bfloat16 [128, 64], replicated, may hold values from -0.5 to 0.5
Outputs:
- pair_gradient: bfloat16 [512, 512, 128], P('row', 'col')
- grad_left: float32 [128, 64], replicated
- grad_left_gate: float32 [128, 64], replicated
- grad_right: float32 [128, 64], replicated
- grad_right_gate: float32 [128, 64], replicated
All inputs are finite; a program needn't handle non-finite values.
Results may differ from a plain program's by a relative error of at most 0.0082.
Values may be sent and summed in bfloat16 or wider, within the bound.
No kernel may reach another device: no remote copies, remote signals or barrier semaphores. Data moves between devices by JAX's collectives and lax.ppermute only.
A program may use at most 128 MiB of HBM per device.

v0:
```python
import functools

import jax
import jax.numpy as jnp
from jax import lax
from jax.experimental import pallas as pl
from jax.experimental.pallas import tpu as pltpu
from jax.sharding import PartitionSpec as P

BF16, F32 = jnp.bfloat16, jnp.float32


def gathered_shards(pair, cotangent, w_left, w_left_gate, w_right, w_right_gate):
    pair_f = pair.astype(jnp.float32)
    average = jnp.mean(pair_f, axis=-1, keepdims=True)
    centered_input = pair_f - average
    variance = jnp.mean(centered_input * centered_input, axis=-1, keepdims=True)
    inverse_scale = 1.0 / jnp.sqrt(variance + 1e-05)
    standardized_input = centered_input * inverse_scale
    normalized_input = standardized_input.astype(jnp.bfloat16)
    stacked = jnp.concatenate([w_left, w_left_gate, w_right, w_right_gate], axis=1)
    projected = jnp.einsum(
        "rcd,dh->hrc", normalized_input, stacked, preferred_element_type=jnp.float32
    )
    q_left, p_left, q_right, p_right = jnp.split(projected, 4, axis=0)
    s_left = jax.nn.sigmoid(p_left)
    s_right = jax.nn.sigmoid(p_right)
    left = (s_left * q_left).astype(jnp.bfloat16)
    right = (s_right * q_right).astype(jnp.bfloat16)
    g_chan, left_chan, right_chan = (
        lax.all_to_all(cotangent, "col", split_axis=0, concat_axis=2, tiled=True),
        lax.all_to_all(left, "col", split_axis=0, concat_axis=2, tiled=True),
        lax.all_to_all(right, "col", split_axis=0, concat_axis=2, tiled=True),
    )
    residues = g_chan.shape[2]
    g_columns = lax.all_to_all(g_chan, "row", split_axis=2, concat_axis=1, tiled=True)
    d_left = jnp.einsum(
        "hij,hjk->hik",
        g_chan,
        lax.all_gather(right_chan, "row", axis=1, tiled=True),
        preferred_element_type=jnp.float32,
    )
    d_right = jnp.einsum(
        "hij,hik->hjk",
        g_columns,
        lax.all_gather(left_chan, "row", axis=1, tiled=True),
        preferred_element_type=jnp.float32,
    )
    d_left_tile, d_right_tile = (
        lax.all_to_all(d_left.astype(jnp.bfloat16), "col", split_axis=2, concat_axis=0, tiled=True),
        lax.all_to_all(
            d_right.astype(jnp.bfloat16), "col", split_axis=2, concat_axis=0, tiled=True
        ),
    )
    grad_l = d_left_tile.astype(jnp.float32)
    grad_r = d_right_tile.astype(jnp.float32)
    e_left = grad_l * s_left
    f_left = grad_l * q_left * s_left * (1.0 - s_left)
    e_right = grad_r * s_right
    f_right = grad_r * q_right * s_right * (1.0 - s_right)
    grads = jnp.concatenate([e_left, f_left, e_right, f_right], axis=0).astype(jnp.bfloat16)
    local_weights = jnp.einsum(
        "rcd,hrc->dh", normalized_input, grads, preferred_element_type=jnp.float32
    )
    total_weights = lax.psum(local_weights, ("row", "col")) / residues
    normalized_gradient = jnp.einsum(
        "hrc,dh->rcd", grads, stacked, preferred_element_type=jnp.float32
    )
    gradient_mean = jnp.mean(normalized_gradient, axis=-1, keepdims=True)
    gradient_input_mean = jnp.mean(normalized_gradient * standardized_input, axis=-1, keepdims=True)
    pair_gradient = (
        (normalized_gradient - gradient_mean - standardized_input * gradient_input_mean)
        * inverse_scale
    ).astype(jnp.bfloat16)
    pieces_w = jnp.split(total_weights, 4, axis=1)
    return (pair_gradient, pieces_w[0], pieces_w[1], pieces_w[2], pieces_w[3])


NT = (((1,), (1,)), ((), ()))
TN = (((0,), (0,)), ((), ()))
NN = (((1,), (0,)), ((), ()))


def dot(a, b, dims=NN):
    return lax.dot_general(a, b, dims, preferred_element_type=F32)


def stack_weights(w_refs, w_ref):
    h = w_refs[0].shape[0]
    for i, ref in enumerate(w_refs):
        w_ref[pl.ds(i * h, h), :] = ref[...]


def layer_norm(x):
    x = x.T.astype(F32)
    centered = x - jnp.mean(x, axis=0, keepdims=True)
    variance = jnp.mean(centered * centered, axis=0, keepdims=True)
    inverse_scale = lax.rsqrt(variance + 1e-05)
    return centered * inverse_scale, inverse_scale


def project(w_ref, normed):
    projected = dot(w_ref[...], normed)
    h = projected.shape[0] // 4
    q_left, p_left, q_right, p_right = (projected[i * h : (i + 1) * h] for i in range(4))
    return q_left, jax.nn.sigmoid(p_left), q_right, jax.nn.sigmoid(p_right)


def put_lanes(ref, at, value):
    lanes = ref.shape[2]
    for i in range(ref.shape[0]):
        ref[i, at, :] = value[:, i * lanes : (i + 1) * lanes]


def get_lanes(ref, at):
    return jnp.concatenate([ref[i, at, :] for i in range(ref.shape[0])], axis=1)


def before_kernel(own, pair_ref, wl, wlg, wr, wrg, out_ref, gates_ref, normed_ref, w_ref, rows_ref):
    stack_weights((wl, wlg, wr, wrg), w_ref)
    h = wl.shape[0]
    rows = pair_ref.shape[0]

    def one_row(r, carry):
        normed = layer_norm(pair_ref[r])[0].astype(BF16)
        normed_ref[r] = normed
        projected = dot(w_ref[...], normed)
        for side in range(2):
            q = projected[2 * side * h : (2 * side + 1) * h]
            s = jax.nn.sigmoid(projected[(2 * side + 1) * h : (2 * side + 2) * h])
            value = s * q
            start = pl.multiple_of(r * 2 * h + side * h, h)
            put_lanes(rows_ref, pl.ds(start, h), value)
            gates_ref[r, pl.ds(2 * side * h, h), :] = s
            gates_ref[r, pl.ds((2 * side + 1) * h, h), :] = value * (1.0 - s)
        return carry

    lax.fori_loop(0, rows, one_row, 0, unroll=4)
    for channel in range(h):
        to, slot = channel // own, (channel % own) * 2
        for side in range(2):
            line = get_lanes(rows_ref, pl.ds(side * h + channel, rows, stride=2 * h))
            out_ref[to, slot + side] = line.astype(BF16)


def triangle_kernel(rows, cols, cot_ref, in_ref, out_ref, g_ref, l_ref, r_ref):
    r, c = in_ref.shape[2:]
    for a in range(rows):
        for b in range(cols):
            at = (pl.ds(a * r, r), pl.ds(b * c, c))
            g_ref[at] = cot_ref[a * cols + b, 0]
            l_ref[at] = in_ref[a * cols + b, 0]
            r_ref[at] = in_ref[a * cols + b, 1]
    for i, (dims, ref) in enumerate(((NN, r_ref), (TN, l_ref))):
        d = dot(g_ref[...], ref[...], dims).astype(BF16)
        for a in range(rows):
            for b in range(cols):
                out_ref[a * cols + b, i] = d[a * r : (a + 1) * r, b * c : (b + 1) * c]


def gates_kernel(own, bit_ref, d_ref, gates_ref, normed_ref, grads_ref, kept_ref, sent_ref, sums_ref, rows_ref):
    rows, h = gates_ref.shape[0], gates_ref.shape[1] // 4

    @pl.when(pl.program_id(0) == 0)
    def _():
        sums_ref[...] = jnp.zeros_like(sums_ref)

    for channel in range(h):
        to, slot = channel // own, (channel % own) * 2
        for side in range(2):
            line = d_ref[to, slot + side].astype(F32)
            put_lanes(rows_ref, pl.ds(side * h + channel, rows, stride=2 * h), line)

    def one_row(r, carry):
        parts = []
        for side in range(2):
            d = get_lanes(rows_ref, pl.ds(pl.multiple_of(r * 2 * h + side * h, h), h))
            parts.append(d * gates_ref[r, pl.ds(2 * side * h, h), :])
            parts.append(d * gates_ref[r, pl.ds((2 * side + 1) * h, h), :])
        grads = jnp.concatenate(parts, axis=0).astype(BF16)
        grads_ref[r] = grads
        sums_ref[...] += dot(grads, normed_ref[r], NT)
        return carry

    lax.fori_loop(0, rows, one_row, 0, unroll=4)

    @pl.when(pl.program_id(0) == pl.num_programs(0) - 1)
    def _():
        bit = bit_ref[0]
        kept_ref[...] = sums_ref[pl.ds(pl.multiple_of(bit * 2 * h, 2 * h), 2 * h), :]
        sent_ref[...] = sums_ref[pl.ds(pl.multiple_of((1 - bit) * 2 * h, 2 * h), 2 * h), :]


def input_kernel(pair_ref, grads_ref, wl, wlg, wr, wrg, *refs):
    out_ref, back_ref = refs[-2:]
    h = wl.shape[0]
    for i, ref in enumerate((wl, wlg, wr, wrg)):
        back_ref[:, pl.ds(i * h, h)] = ref[...].T

    def one_row(r, carry):
        standardized, inverse_scale = layer_norm(pair_ref[r])
        d_normed = dot(back_ref[...], grads_ref[r])
        mean = jnp.mean(d_normed, axis=0, keepdims=True)
        input_mean = jnp.mean(d_normed * standardized, axis=0, keepdims=True)
        moved = (d_normed - mean - standardized * input_mean) * inverse_scale
        out_ref[r] = moved.astype(BF16).T
        return carry

    lax.fori_loop(0, pair_ref.shape[0], one_row, 0, unroll=4)


def finish_kernel(scale, bit_ref, mine_ref, other_ref, *out_refs):
    h = out_refs[0].shape[0]
    for i, out_ref in enumerate(out_refs):
        at = pl.ds(i % 2 * h, h)
        mine = bit_ref[0] == i // 2
        out_ref[...] = jnp.where(mine, mine_ref[at, :], other_ref[at, :]) * scale


def channel_shards(sizes, pair, cotangent, *weights):
    rows, cols = sizes
    devices = rows * cols
    hidden, r, c = cotangent.shape
    dim = pair.shape[2]
    own = hidden // devices
    block = 16 if r % 16 == 0 else r
    pieces = 4 if r % 4 == 0 else 1
    weights = [w.T for w in weights]
    whole = pl.BlockSpec((hidden, dim), lambda i: (0, 0))
    tile = pl.BlockSpec((block, c, dim), lambda i: (i, 0, 0))
    exchange = functools.partial(
        lax.all_to_all, axis_name=("row", "col"), split_axis=0, concat_axis=0, tiled=True
    )
    stacked = pltpu.VMEM((4 * hidden, dim), BF16)
    lanes = min(c, 128)
    rows_scratch = pltpu.VMEM((c // lanes, 2 * hidden * block, lanes), F32)

    def cost(flops, *arrays):
        moved = sum(a.size * a.dtype.itemsize for a in arrays)
        return pl.CostEstimate(flops=flops, bytes_accessed=moved, transcendentals=0)

    def memory(mib):
        return pltpu.CompilerParams(vmem_limit_bytes=mib * 2**20)

    columns = r * c
    lr_shape = jax.ShapeDtypeStruct((devices, 2 * own, r, c), BF16)
    gates_shape = jax.ShapeDtypeStruct((r, 4 * hidden, c), F32)
    normed_shape = jax.ShapeDtypeStruct((r, dim, c), BF16)
    by_hidden = pl.BlockSpec((block, 4 * hidden, c), lambda i: (i, 0, 0))
    by_dim = pl.BlockSpec((block, dim, c), lambda i: (i, 0, 0))
    g_all = exchange(cotangent.reshape(devices, own, r, c))
    sent, gates, normed = pl.pallas_call(
        functools.partial(before_kernel, own),
        grid=(r // block,),
        in_specs=[tile] + [whole] * 4,
        out_specs=[
            pl.BlockSpec((devices, 2 * own, block, c), lambda i: (0, 0, i, 0)),
            by_hidden,
            by_dim,
        ],
        out_shape=[lr_shape, gates_shape, normed_shape],
        scratch_shapes=[stacked, rows_scratch],
        compiler_params=memory(60),
        cost_estimate=cost(8 * hidden * dim * columns, pair, lr_shape, gates_shape),
        name="before",
    )(pair, *weights)

    n_i, n_k = rows * r, cols * c
    sent = pl.pallas_call(
        functools.partial(triangle_kernel, rows, cols),
        grid=(own,),
        in_specs=[
            pl.BlockSpec((devices, 1, r, c), lambda i: (0, i, 0, 0)),
            pl.BlockSpec((devices, 2, r, c), lambda i: (0, i, 0, 0)),
        ],
        out_specs=pl.BlockSpec((devices, 2, r, c), lambda i: (0, i, 0, 0)),
        out_shape=lr_shape,
        scratch_shapes=[pltpu.VMEM((n_i, n_k), BF16)] * 3,
        compiler_params=memory(32),
        name="triangle",
    )(g_all, exchange(sent))

    bit = (lax.axis_index("row") % 2).astype(jnp.int32).reshape(1)
    smem = pl.BlockSpec(memory_space=pltpu.SMEM)
    half_shape = jax.ShapeDtypeStruct((2 * hidden, dim), F32)
    half = pl.BlockSpec(half_shape.shape, lambda i: (0, 0))
    grads, kept, given = pl.pallas_call(
        functools.partial(gates_kernel, own),
        grid=(r // block,),
        in_specs=[
            smem,
            pl.BlockSpec((devices, 2 * own, block, c), lambda i: (0, 0, i, 0)),
            by_hidden,
            by_dim,
        ],
        out_specs=[by_hidden, half, half],
        out_shape=[jax.ShapeDtypeStruct((r, 4 * hidden, c), BF16), half_shape, half_shape],
        scratch_shapes=[pltpu.VMEM((4 * hidden, dim), F32), rows_scratch],
        compiler_params=memory(28),
        name="gates",
    )(bit, exchange(sent), gates, normed)

    def input_piece(piece, pair_gradient):
        held = [] if pair_gradient is None else [pair_gradient]
        at = pl.BlockSpec((r // pieces, c, dim), lambda i: (piece, 0, 0))
        return pl.pallas_call(
            input_kernel,
            grid=(1,),
            in_specs=[at, pl.BlockSpec((r // pieces, 4 * hidden, c), lambda i: (piece, 0, 0))]
            + [whole] * 4
            + [pl.BlockSpec(memory_space=pl.ANY)] * len(held),
            out_specs=at,
            out_shape=jax.ShapeDtypeStruct(pair.shape, BF16),
            scratch_shapes=[pltpu.VMEM((dim, 4 * hidden), BF16)],
            input_output_aliases={6: 0} if held else {},
            compiler_params=memory(16),
            cost_estimate=cost(8 * hidden * dim * columns // pieces, pair),
            name="input",
        )(pair, grads, *weights, *held)

    steps = [("row", rows, 1 << i) for i in range(1, rows.bit_length() - 1)][::-1]
    steps += [("col", cols, 1 << i) for i in range(cols.bit_length() - 1)]
    neighbours = [(i, i ^ 1) for i in range(rows)]
    pair_gradient = None
    mine = kept + lax.ppermute(given, "row", neighbours)
    for n, (axis, size, step) in enumerate(steps):
        other = lax.ppermute(mine, axis, [(i, i ^ step) for i in range(size)])
        for piece in range(n * pieces // len(steps), (n + 1) * pieces // len(steps)):
            pair_gradient = input_piece(piece, pair_gradient)
        if pair_gradient is not None:
            other, pair_gradient = lax.optimization_barrier((other, pair_gradient))
        mine = mine + other
    weight_grads = pl.pallas_call(
        functools.partial(finish_kernel, 1.0 / n_i),
        in_specs=[smem, pl.BlockSpec(memory_space=pltpu.VMEM), pl.BlockSpec(memory_space=pltpu.VMEM)],
        out_shape=[jax.ShapeDtypeStruct((hidden, dim), F32)] * 4,
        name="finish",
    )(bit, mine, lax.ppermute(mine, "row", neighbours))
    return (pair_gradient, *(g.T for g in weight_grads))


def solution(mesh):
    in_specs = (P("row", "col", None), P(None, "row", "col"), P(), P(), P(), P())
    out_specs = (P("row", "col", None), P(), P(), P(), P())
    sizes = (mesh.shape["row"], mesh.shape["col"])

    def shards(pair, cotangent, *weights):
        plain = all(size > 1 and size & (size - 1) == 0 for size in sizes)
        if plain and cotangent.shape[0] % (sizes[0] * sizes[1]) == 0:
            return channel_shards(sizes, pair, cotangent, *weights)
        return gathered_shards(pair, cotangent, *weights)

    return jax.shard_map(shards, mesh=mesh, in_specs=in_specs, out_specs=out_specs, check_vma=False)
```

profile of v0, /device:TPU:0, one launch (start us, length us, event | category | flops | bytes accessed | tf_op | source)
XLA Modules:
  0.0 178.4 jit_solution(15112355512830760134)
XLA Ops:
  0.6 7.3 %all-to-all-start = ((bf16[32,2,32,256]{3,2,1,0:T(8,128)(2,1)}), bf16[32,2,32,256]{3,2,1,0:T(8,128)(2,1)S(1)}, u32[]{:S(2)}, u32[]{:S(2)}) async-start(bf16[32,2,32,256]{3,2,1,0:T(8,128)(2,1)} %bitcast.30), calls=%async_computation | async-start | bytes 2097152 | tf_op jit(solution)/shard_map/all_to_all | solution.py:251
  7.9 10.5 %before.1 = (bf16[32,4,32,256]{3,2,1,0:T(8,128)(2,1)}, f32[32,256,256]{2,1,0:T(8,128)}, bf16[32,128,256]{2,1,0:T(8,128)(2,1)}) custom-call(bf16[32,256,128]{2,1,0:T(8,128)(2,1)} %pair_ref.9, bf16[64,128]{1,0:T(8,128)(2,1)} %bitcast.10, bf16[64,128]{1,0:T(8,128)(2,1)} %bitcast.15, bf16[64,128]{1,0:T(8,128)(2,1)} %bitcast.20, bf16[64,128]{1,0:T(8,128)(2,1)} %bitcast.25), custom_call_target="tpu_custom_call" | custom-call | flops 536870912 | bytes 12582912 | tf_op jit(solution)/shard_map/before/pallas_call | solution.py:252
  18.4 15.8 %all-to-all-done.cot_ref = bf16[32,2,32,256]{3,2,1,0:T(8,128)(2,1)S(1)} async-done(((bf16[32,2,32,256]{3,2,1,0:T(8,128)(2,1)}), bf16[32,2,32,256]{3,2,1,0:T(8,128)(2,1)S(1)}, u32[]{:S(2)}, u32[]{:S(2)}) %all-to-all-start) | async-done | bytes 1048608 | tf_op jit(solution)/shard_map/all_to_all | solution.py:251
  34.2 52.3 %all_to_all.15.in_ref = bf16[32,4,32,256]{3,2,1,0:T(8,128)(2,1)S(1)} all-to-all(bf16[32,4,32,256]{3,2,1,0:T(8,128)(2,1)} %get-tuple-element.23), channel_id=1, replica_groups=mesh['row'=16,'col'=2] {'row','col'}, dimensions={0} | all-to-all | bytes 4194304 | tf_op jit(solution)/shard_map/all_to_all | solution.py:281
  86.5 1.8 triangle.1
  88.3 0.0 copy-start.2
  88.3 1.3 copy-done.2
  89.6 3.7 %all-to-all-start.2 = ((bf16[32,4,32,256]{3,2,1,0:T(8,128)(2,1)}), bf16[32,4,32,256]{3,2,1,0:T(8,128)(2,1)S(1)}, u32[]{:S(2)}, u32[]{:S(2)}) async-start(bf16[32,4,32,256]{3,2,1,0:T(8,128)(2,1)} %copy-done.2), calls=%async_computation.2 | async-start | bytes 4194304 | tf_op jit(solution)/shard_map/all_to_all | solution.py:301
  93.3 48.7 %all-to-all-done.2.d_ref = bf16[32,4,32,256]{3,2,1,0:T(8,128)(2,1)S(1)} async-done(((bf16[32,4,32,256]{3,2,1,0:T(8,128)(2,1)}), bf16[32,4,32,256]{3,2,1,0:T(8,128)(2,1)S(1)}, u32[]{:S(2)}, u32[]{:S(2)}) %all-to-all-start.2) | async-done | bytes 2097184 | tf_op jit(solution)/shard_map/all_to_all | solution.py:301
  142.0 0.0 copy-start.1
  142.0 3.4 %copy-done.1 = f32[32,256,256]{2,1,0:T(8,128)S(1)} copy-done((f32[32,256,256]{2,1,0:T(8,128)S(1)}, f32[32,256,256]{2,1,0:T(8,128)}, u32[]{:S(2)}) %copy-start.1) | copy-done | bytes 8388632
  145.4 0.0 copy-start.3
  145.4 1.6 copy-done.3
  147.0 0.0 copy-start
  147.0 0.0 copy-start.4
  147.0 0.0 copy-start.5
  147.0 0.0 copy-start.6
  147.0 0.0 copy-start.7
  147.0 7.0 %gates.1 = (bf16[32,256,256]{2,1,0:T(8,128)(2,1)S(1)}, f32[128,128]{1,0:T(8,128)S(1)}, f32[128,128]{1,0:T(8,128)S(1)}) custom-call(s32[1]{0:T(128)} %bitcast.bit_ref, bf16[32,4,32,256]{3,2,1,0:T(8,128)(2,1)S(1)} %all-to-all-done.2.d_ref, f32[32,256,256]{2,1,0:T(8,128)S(1)} %copy-done.1, bf16[32,128,256]{2,1,0:T(8,128)(2,1)S(1)} %copy-done.3), custom_call_target="tpu_custom_call" | custom-call | tf_op jit(solution)/shard_map/gates/pallas_call | solution.py:287
  154.0 0.1 collective-permute-start
  154.1 1.2 collective-permute-done
  155.4 1.1 collective-permute-start.1
  156.5 0.0 copy-done
  156.5 0.0 copy-done.4
  156.5 0.0 copy-done.5
  156.5 0.0 copy-done.6
  156.5 0.0 copy-done.7
  156.5 1.9 %input.4.refs_0_ = bf16[32,256,128]{2,1,0:T(8,128)(2,1)} custom-call(bf16[32,256,128]{2,1,0:T(8,128)(2,1)S(1)} %copy-done, bf16[32,256,256]{2,1,0:T(8,128)(2,1)S(1)} %get-tuple-element.28.grads_ref, bf16[64,128]{1,0:T(8,128)(2,1)S(1)} %bitcast.11, bf16[64,128]{1,0:T(8,128)(2,1)S(1)} %bitcast.16, bf16[64,128]{1,0:T(8,128)(2,1)S(1)} %bitcast.21, ...), custom_call_target="tpu_custom_call" | custom-call | flops 134217728 | bytes 2097152 | tf_op jit(solution)/shard_map/input/pallas_call | solution.py:306
  158.4 3.5 %collective-permute-done.1 = f32[128,128]{1,0:T(8,128)S(1)} collective-permute-done((f32[128,128]{1,0:T(8,128)S(1)}, f32[128,128]{1,0:T(8,128)S(1)}, u32[]{:S(2)}, u32[]{:S(2)}) %collective-permute-start.1) | collective-permute-done | bytes 65568 | tf_op jit(solution)/shard_map/ppermute | solution.py:327
  161.9 0.1 collective-permute-start.2
  162.0 1.9 %input.5.refs_0_ = bf16[32,256,128]{2,1,0:T(8,128)(2,1)} custom-call(bf16[32,256,128]{2,1,0:T(8,128)(2,1)S(1)} %copy-done, bf16[32,256,256]{2,1,0:T(8,128)(2,1)S(1)} %get-tuple-element.28.grads_ref, bf16[64,128]{1,0:T(8,128)(2,1)S(1)} %bitcast.12, bf16[64,128]{1,0:T(8,128)(2,1)S(1)} %bitcast.17, ...), custom_call_target="tpu_custom_call", output_to_operand_aliasing={{}: (6, {})} | custom-call | flops 134217728 | bytes 2097152 | tf_op jit(solution)/shard_map/input/pallas_call | solution.py:306
  163.9 2.3 %collective-permute-done.2 = f32[128,128]{1,0:T(8,128)S(1)} collective-permute-done((f32[128,128]{1,0:T(8,128)S(1)}, f32[128,128]{1,0:T(8,128)S(1)}, u32[]{:S(2)}, u32[]{:S(2)}) %collective-permute-start.2) | collective-permute-done | bytes 65568 | tf_op jit(solution)/shard_map/ppermute | solution.py:327
  166.2 0.7 collective-permute-start.3
  167.0 1.9 %input.6.refs_0_ = bf16[32,256,128]{2,1,0:T(8,128)(2,1)} custom-call(bf16[32,256,128]{2,1,0:T(8,128)(2,1)S(1)} %copy-done, bf16[32,256,256]{2,1,0:T(8,128)(2,1)S(1)} %get-tuple-element.28.grads_ref, bf16[64,128]{1,0:T(8,128)(2,1)S(1)} %bitcast.13, bf16[64,128]{1,0:T(8,128)(2,1)S(1)} %bitcast.18, ...), custom_call_target="tpu_custom_call", output_to_operand_aliasing={{}: (6, {})} | custom-call | flops 134217728 | bytes 2097152 | tf_op jit(solution)/shard_map/input/pallas_call | solution.py:306
  168.9 1.7 collective-permute-done.3
  170.6 1.5 collective-permute-start.4
  172.1 1.9 %input.7 = bf16[32,256,128]{2,1,0:T(8,128)(2,1)} custom-call(bf16[32,256,128]{2,1,0:T(8,128)(2,1)S(1)} %copy-done, bf16[32,256,256]{2,1,0:T(8,128)(2,1)S(1)} %get-tuple-element.28.grads_ref, bf16[64,128]{1,0:T(8,128)(2,1)S(1)} %bitcast.14, bf16[64,128]{1,0:T(8,128)(2,1)S(1)} %bitcast.19, ...), custom_call_target="tpu_custom_call", output_to_operand_aliasing={{}: (6, {})} | custom-call | flops 134217728 | bytes 2097152 | tf_op jit(solution)/shard_map/input/pallas_call | solution.py:306
  174.0 0.9 collective-permute-done.4
  174.9 0.0 copy-start.8
  174.9 0.1 collective-permute-start.5
  175.0 1.2 collective-permute-done.5.other_ref
  176.3 0.0 copy-done.8
  176.3 0.0 copy-start.9
  176.3 0.6 copy-done.9
  176.9 1.5 finish.1
  (5 shorter events, 0.0 us)
Async XLA Ops:
  0.6 33.5 %all-to-all-start = ((bf16[32,2,32,256]{3,2,1,0:T(8,128)(2,1)}), bf16[32,2,32,256]{3,2,1,0:T(8,128)(2,1)S(1)}, u32[]{:S(2)}, u32[]{:S(2)}) async-start(bf16[32,2,32,256]{3,2,1,0:T(8,128)(2,1)} %bitcast.30), calls=%async_computation | async-start | bytes 2097152 | tf_op jit(solution)/shard_map/all_to_all | solution.py:251
  88.3 1.3 copy-start.2
  89.6 52.4 %all-to-all-start.2 = ((bf16[32,4,32,256]{3,2,1,0:T(8,128)(2,1)}), bf16[32,4,32,256]{3,2,1,0:T(8,128)(2,1)S(1)}, u32[]{:S(2)}, u32[]{:S(2)}) async-start(bf16[32,4,32,256]{3,2,1,0:T(8,128)(2,1)} %copy-done.2), calls=%async_computation.2 | async-start | bytes 4194304 | tf_op jit(solution)/shard_map/all_to_all | solution.py:301
  142.0 3.4 %copy-start.1 = (f32[32,256,256]{2,1,0:T(8,128)S(1)}, f32[32,256,256]{2,1,0:T(8,128)}, u32[]{:S(2)}) copy-start(f32[32,256,256]{2,1,0:T(8,128)} %get-tuple-element.24.gates_ref) | copy-start | bytes 25165828
  145.4 1.6 copy-start.3
  147.0 9.5 %copy-start = (bf16[32,256,128]{2,1,0:T(8,128)(2,1)S(1)}, bf16[32,256,128]{2,1,0:T(8,128)(2,1)}, u32[]{:S(2)}) copy-start(bf16[32,256,128]{2,1,0:T(8,128)(2,1)} %pair_ref.9) | copy-start | bytes 6291460
  147.0 9.5 %copy-start.4 = (bf16[128,64]{0,1:T(8,128)(2,1)S(1)}, bf16[128,64]{0,1:T(8,128)(2,1)}, u32[]{:S(2)}) copy-start(bf16[128,64]{0,1:T(8,128)(2,1)} %param.8) | copy-start | bytes 49156
  147.0 9.5 %copy-start.5 = (bf16[128,64]{0,1:T(8,128)(2,1)S(1)}, bf16[128,64]{0,1:T(8,128)(2,1)}, u32[]{:S(2)}) copy-start(bf16[128,64]{0,1:T(8,128)(2,1)} %param.9) | copy-start | bytes 49156
  147.0 9.5 %copy-start.6 = (bf16[128,64]{0,1:T(8,128)(2,1)S(1)}, bf16[128,64]{0,1:T(8,128)(2,1)}, u32[]{:S(2)}) copy-start(bf16[128,64]{0,1:T(8,128)(2,1)} %param.10) | copy-start | bytes 49156
  147.0 9.5 %copy-start.7 = (bf16[128,64]{0,1:T(8,128)(2,1)S(1)}, bf16[128,64]{0,1:T(8,128)(2,1)}, u32[]{:S(2)}) copy-start(bf16[128,64]{0,1:T(8,128)(2,1)} %param.11) | copy-start | bytes 49156
  154.0 1.3 collective-permute-start
  155.4 6.5 %collective-permute-start.1 = (f32[128,128]{1,0:T(8,128)S(1)}, f32[128,128]{1,0:T(8,128)S(1)}, u32[]{:S(2)}, u32[]{:S(2)}) collective-permute-start(f32[128,128]{1,0:T(8,128)S(1)} %add.20), channel_id=1, source_target_pairs={{0,16},{2,18},{4,20},{6,22},{8,24},{10,26},{12,28},{14,30},{16,0},... | collective-permute-start | bytes 196616 | tf_op jit(solution)/shard_map/ppermute | solution.py:327
  161.9 4.3 %collective-permute-start.2 = (f32[128,128]{1,0:T(8,128)S(1)}, f32[128,128]{1,0:T(8,128)S(1)}, u32[]{:S(2)}, u32[]{:S(2)}) collective-permute-start(f32[128,128]{1,0:T(8,128)S(1)} %add.21), channel_id=1, source_target_pairs={{0,8},{2,10},{4,12},{6,14},{8,0},{10,2},{12,4},{14,6},{16,24},{18,... | collective-permute-start | bytes 196616 | tf_op jit(solution)/shard_map/ppermute | solution.py:327
  166.2 4.3 %collective-permute-start.3 = (f32[128,128]{1,0:T(8,128)S(1)}, f32[128,128]{1,0:T(8,128)S(1)}, u32[]{:S(2)}, u32[]{:S(2)}) collective-permute-start(f32[128,128]{1,0:T(8,128)S(1)} %add.22), channel_id=1, source_target_pairs={{0,4},{2,6},{4,0},{6,2},{8,12},{10,14},{12,8},{14,10},{16,20},{18,... | collective-permute-start | bytes 196616 | tf_op jit(solution)/shard_map/ppermute | solution.py:327
  170.6 4.3 %collective-permute-start.4 = (f32[128,128]{1,0:T(8,128)S(1)}, f32[128,128]{1,0:T(8,128)S(1)}, u32[]{:S(2)}, u32[]{:S(2)}) collective-permute-start(f32[128,128]{1,0:T(8,128)S(1)} %add.23), channel_id=1, source_target_pairs={{0,1},{1,0},{2,3},{3,2},{4,5},{5,4},{6,7},{7,6},{8,9},{9,8},{10,11... | collective-permute-start | bytes 196616 | tf_op jit(solution)/shard_map/ppermute | solution.py:327
  174.9 1.3 copy-start.8
  174.9 1.3 collective-permute-start.5
  176.3 0.6 copy-start.9
where the time goes:
time: 179 us; the launch traced here: 178 us
  waiting for transfers between devices  75.4 us (42%)
  blocking collectives  52.3 us (29%)
  Pallas kernels  28.5 us (16%)
  starting transfers between devices  14.5 us (8%)
  local copies, waits for them, and re-layouts  6.94 us (4%)
    all_to_all x1, blocking collectives, channel_shards(): exchange(sent)  52.3 us
    all_to_all x1, waiting for transfers between devices, channel_shards(): exchange(sent)  48.7 us
    all_to_all x1, waiting for transfers between devices, channel_shards(): g_all = exchange(cotangent.reshape(devices, own, r, c))  15.8 us
    pallas_call x1, Pallas kernels, channel_shards(): pl.pallas_call(functools.partial(before_kernel, own), grid=(r // block,),...  10.5 us
    ppermute x4, waiting for transfers between devices, channel_shards(): other = lax.ppermute(mine, axis, [(i, i ^ step) for i in range(size)])  8.39 us
    pallas_call x4, Pallas kernels, input_piece(): pl.pallas_call(input_kernel, grid=(1,), in_specs=[at, pl.BlockSpec((r //...  7.73 us
    all_to_all x1, starting transfers between devices, channel_shards(): g_all = exchange(cotangent.reshape(devices, own, r, c))  7.3 us
    pallas_call x1, Pallas kernels, channel_shards(): pl.pallas_call(functools.partial(gates_kernel, own), grid=(r // block,),...  7 us
  transfers between devices with their start and end apart: 8, of which 8 were waited for; matrix products, arithmetic and copies ran while one was open for 0% of the time, Pallas kernels for 10%

commit v1 on v0

--- a/solution.py
+++ b/solution.py
@@ -161,7 +161,9 @@
 def gates_kernel(own, bit_ref, d_ref, gates_ref, normed_ref, grads_ref, kept_ref, sent_ref, sums_ref, rows_ref):
     rows, h = gates_ref.shape[0], gates_ref.shape[1] // 4
 
-    @pl.when(pl.program_id(0) == 0)
+    step = pl.program_id(0) * pl.num_programs(1) + pl.program_id(1)
+
+    @pl.when(step == 0)
     def _():
         sums_ref[...] = jnp.zeros_like(sums_ref)
 
@@ -184,7 +186,7 @@
 
     lax.fori_loop(0, rows, one_row, 0, unroll=4)
 
-    @pl.when(pl.program_id(0) == pl.num_programs(0) - 1)
+    @pl.when(step == pl.num_programs(0) * pl.num_programs(1) - 1)
     def _():
         bit = bit_ref[0]
         kept_ref[...] = sums_ref[pl.ds(pl.multiple_of(bit * 2 * h, 2 * h), 2 * h), :]
@@ -283,20 +285,20 @@
     bit = (lax.axis_index("row") % 2).astype(jnp.int32).reshape(1)
     smem = pl.BlockSpec(memory_space=pltpu.SMEM)
     half_shape = jax.ShapeDtypeStruct((2 * hidden, dim), F32)
-    half = pl.BlockSpec(half_shape.shape, lambda i: (0, 0))
+    half = pl.BlockSpec(half_shape.shape, lambda i, j: (0, 0))
     grads, kept, given = pl.pallas_call(
         functools.partial(gates_kernel, own),
-        grid=(r // block,),
+        grid=(r // block, c // lanes),
         in_specs=[
             smem,
-            pl.BlockSpec((devices, 2 * own, block, c), lambda i: (0, 0, i, 0)),
-            by_hidden,
-            by_dim,
+            pl.BlockSpec((devices, 2 * own, block, lanes), lambda i, j: (0, 0, i, j)),
+            pl.BlockSpec((block, 4 * hidden, lanes), lambda i, j: (i, 0, j)),
+            pl.BlockSpec((block, dim, lanes), lambda i, j: (i, 0, j)),
         ],
-        out_specs=[by_hidden, half, half],
+        out_specs=[pl.BlockSpec((block, 4 * hidden, lanes), lambda i, j: (i, 0, j)), half, half],
         out_shape=[jax.ShapeDtypeStruct((r, 4 * hidden, c), BF16), half_shape, half_shape],
-        scratch_shapes=[pltpu.VMEM((4 * hidden, dim), F32), rows_scratch],
-        compiler_params=memory(28),
+        scratch_shapes=[pltpu.VMEM((4 * hidden, dim), F32), pltpu.VMEM((1, 2 * hidden * block, lanes), F32)],
+        compiler_params=memory(60),
         name="gates",
     )(bit, exchange(sent), gates, normed)
 
@@ -313,7 +315,7 @@
             out_shape=jax.ShapeDtypeStruct(pair.shape, BF16),
             scratch_shapes=[pltpu.VMEM((dim, 4 * hidden), BF16)],
             input_output_aliases={6: 0} if held else {},
-            compiler_params=memory(16),
+            compiler_params=memory(60),
             cost_estimate=cost(8 * hidden * dim * columns // pieces, pair),
             name="input",
         )(pair, grads, *weights, *held)

time: 179 us -> 180 us (level)
  Pallas kernels: 28.5 us -> 38.9 us
  local copies, waits for them, and re-layouts: 6.94 us -> 1.95 us
  waiting for transfers between devices: 75.4 us -> 70.6 us
    pallas_call x4, Pallas kernels: 7.73 us -> 13.2 us  [input_piece(): pl.pallas_call(input_kernel, grid=(1,), in_specs=[at, pl.BlockSpec((r //...]
    ppermute x4, waiting for transfers between devices: 8.39 us -> 3.37 us  [channel_shards(): other = lax.ppermute(mine, axis, [(i, i ^ step) for i in range(size)])]
    unnamed x20 -> x6, local copies, waits for them, and re-layouts: 6.94 us -> 1.95 us
    pallas_call x1, Pallas kernels: 7 us -> 11 us  [channel_shards(): pl.pallas_call(functools.partial(gates_kernel, own), grid=(r // block, c...]
  transfers between devices with their start and end apart: 8 -> 8, of which waited for: 8 -> 7; matrix products, arithmetic and copies ran while one was open for 0% -> 0% of each run, Pallas kernels for 10% -> 13%
where the time goes in v1:
time: 180 us
  waiting for transfers between devices  70.6 us (39%)
  blocking collectives  52.3 us (29%)
  Pallas kernels  38.9 us (22%)
  starting transfers between devices  14.4 us (8%)
  local copies, waits for them, and re-layouts  1.95 us (1%)
    all_to_all x1, blocking collectives, channel_shards(): exchange(sent)  52.3 us
    all_to_all x1, waiting for transfers between devices, channel_shards(): exchange(sent)  48.7 us
    all_to_all x1, waiting for transfers between devices, channel_shards(): g_all = exchange(cotangent.reshape(devices, own, r, c))  15.8 us
    pallas_call x4, Pallas kernels, input_piece(): pl.pallas_call(input_kernel, grid=(1,), in_specs=[at, pl.BlockSpec((r //...  13.2 us
    pallas_call x1, Pallas kernels, channel_shards(): pl.pallas_call(functools.partial(gates_kernel, own), grid=(r // block, c...  11 us
    pallas_call x1, Pallas kernels, channel_shards(): pl.pallas_call(functools.partial(before_kernel, own), grid=(r // block,),...  10.4 us
    all_to_all x1, starting transfers between devices, channel_shards(): g_all = exchange(cotangent.reshape(devices, own, r, c))  7.3 us
    all_to_all x1, starting transfers between devices, channel_shards(): exchange(sent)  3.67 us
  transfers between devices with their start and end apart: 8, of which 7 were waited for; matrix products, arithmetic and copies ran while one was open for 0% of the time, Pallas kernels for 13%

profile of v1, /device:TPU:0, one launch (start us, length us, event | category | flops | bytes accessed | tf_op | source)
XLA Modules:
  0.0 179.8 jit_solution(11802200555881715322)
XLA Ops:
  0.6 7.3 %all-to-all-start = ((bf16[32,2,32,256]{3,2,1,0:T(8,128)(2,1)}), bf16[32,2,32,256]{3,2,1,0:T(8,128)(2,1)S(1)}, u32[]{:S(2)}, u32[]{:S(2)}) async-start(bf16[32,2,32,256]{3,2,1,0:T(8,128)(2,1)} %bitcast.10), calls=%async_computation | async-start | bytes 2097152 | tf_op jit(solution)/shard_map/all_to_all | solution.py:253
  7.9 10.4 %before.1 = (bf16[32,4,32,256]{3,2,1,0:T(8,128)(2,1)}, f32[32,256,256]{2,1,0:T(8,128)}, bf16[32,128,256]{2,1,0:T(8,128)(2,1)}) custom-call(bf16[32,256,128]{2,1,0:T(8,128)(2,1)} %pair_ref.9, bf16[64,128]{1,0:T(8,128)(2,1)} %bitcast.11, bf16[64,128]{1,0:T(8,128)(2,1)} %bitcast.16, bf16[64,128]{1,0:T(8,128)(2,1)} %bitcast.21, bf16[64,128]{1,0:T(8,128)(2,1)} %bitcast.26), custom_call_target="tpu_custom_call" | custom-call | flops 536870912 | bytes 12582912 | tf_op jit(solution)/shard_map/before/pallas_call | solution.py:254
  18.4 15.8 %all-to-all-done.cot_ref = bf16[32,2,32,256]{3,2,1,0:T(8,128)(2,1)S(1)} async-done(((bf16[32,2,32,256]{3,2,1,0:T(8,128)(2,1)}), bf16[32,2,32,256]{3,2,1,0:T(8,128)(2,1)S(1)}, u32[]{:S(2)}, u32[]{:S(2)}) %all-to-all-start) | async-done | bytes 1048608 | tf_op jit(solution)/shard_map/all_to_all | solution.py:253
  34.2 52.3 %all_to_all.15.in_ref = bf16[32,4,32,256]{3,2,1,0:T(8,128)(2,1)S(1)} all-to-all(bf16[32,4,32,256]{3,2,1,0:T(8,128)(2,1)} %get-tuple-element.23), channel_id=1, replica_groups=mesh['row'=16,'col'=2] {'row','col'}, dimensions={0} | all-to-all | bytes 4194304 | tf_op jit(solution)/shard_map/all_to_all | solution.py:283
  86.5 2.6 %triangle.1 = bf16[32,4,32,256]{3,2,1,0:T(8,128)(2,1)} custom-call(bf16[32,2,32,256]{3,2,1,0:T(8,128)(2,1)S(1)} %all-to-all-done.cot_ref, bf16[32,4,32,256]{3,2,1,0:T(8,128)(2,1)S(1)} %all_to_all.15.in_ref), custom_call_target="tpu_custom_call" | custom-call | tf_op jit(solution)/shard_map/triangle/pallas_call | solution.py:271
  89.2 3.7 %all-to-all-start.2 = ((bf16[32,4,32,256]{3,2,1,0:T(8,128)(2,1)}), bf16[32,4,32,256]{3,2,1,0:T(8,128)(2,1)S(1)}, u32[]{:S(2)}, u32[]{:S(2)}) async-start(bf16[32,4,32,256]{3,2,1,0:T(8,128)(2,1)} %triangle.1), calls=%async_computation.2 | async-start | bytes 4194304 | tf_op jit(solution)/shard_map/all_to_all | solution.py:303
  92.8 48.7 %all-to-all-done.2.d_ref = bf16[32,4,32,256]{3,2,1,0:T(8,128)(2,1)S(1)} async-done(((bf16[32,4,32,256]{3,2,1,0:T(8,128)(2,1)}), bf16[32,4,32,256]{3,2,1,0:T(8,128)(2,1)S(1)}, u32[]{:S(2)}, u32[]{:S(2)}) %all-to-all-start.2) | async-done | bytes 2097184 | tf_op jit(solution)/shard_map/all_to_all | solution.py:303
  141.6 0.0 copy-start
  141.6 1.3 copy-done
  142.9 11.0 %gates.1 = (bf16[32,256,256]{2,1,0:T(8,128)(2,1)}, f32[128,128]{1,0:T(8,128)}, f32[128,128]{1,0:T(8,128)}) custom-call(s32[1]{0:T(128)} %bitcast.bit_ref, bf16[32,4,32,256]{3,2,1,0:T(8,128)(2,1)} %copy-done, f32[32,256,256]{2,1,0:T(8,128)} %get-tuple-element.24.gates_ref, bf16[32,128,256]{2,1,0:T(8,128)(2,1)} %get-tuple-element.25.normed_ref), custom_call_target="tpu_custom_call" | custom-call | tf_op jit(solution)/shard_map/gates/pallas_call | solution.py:289
  153.9 0.0 collective-permute-start
  153.9 1.5 collective-permute-done
  155.4 0.9 add.20
  156.2 1.1 collective-permute-start.1
  157.3 3.3 %input.4.refs_0_ = bf16[32,256,128]{2,1,0:T(8,128)(2,1)} custom-call(bf16[32,256,128]{2,1,0:T(8,128)(2,1)} %pair_ref.9, bf16[32,256,256]{2,1,0:T(8,128)(2,1)} %get-tuple-element.28.grads_ref, bf16[64,128]{1,0:T(8,128)(2,1)} %bitcast.12, bf16[64,128]{1,0:T(8,128)(2,1)} %bitcast.17, bf16[64,128]{1,0:T(8,128)(2,1)} %bitcast.22, bf16[64,128]{1,0:T(8,128)(2,1)} %bitcast.27), custom_call_target="tpu_custom_call" | custom-call | flops 134217728 | bytes 2097152 | tf_op jit(solution)/shard_map/input/pallas_call | solution.py:308
  160.6 2.1 %collective-permute-done.1 = f32[128,128]{1,0:T(8,128)S(1)} collective-permute-done((f32[128,128]{1,0:T(8,128)S(1)}, f32[128,128]{1,0:T(8,128)S(1)}, u32[]{:S(2)}, u32[]{:S(2)}) %collective-permute-start.1) | collective-permute-done | bytes 65568 | tf_op jit(solution)/shard_map/ppermute | solution.py:329
  162.8 0.1 collective-permute-start.2
  162.9 3.3 %input.5.refs_0_ = bf16[32,256,128]{2,1,0:T(8,128)(2,1)} custom-call(bf16[32,256,128]{2,1,0:T(8,128)(2,1)} %pair_ref.9, bf16[32,256,256]{2,1,0:T(8,128)(2,1)} %get-tuple-element.28.grads_ref, bf16[64,128]{1,0:T(8,128)(2,1)} %bitcast.13, bf16[64,128]{1,0:T(8,128)(2,1)} %bitcast.18, bf16[64,128]{1,0:T(8,128)(2,1)} %bitcast.23, ...), custom_call_target="tpu_custom_call", output_to_operand_aliasing={{}: (6, {})} | custom-call | flops 134217728 | bytes 2097152 | tf_op jit(solution)/shard_map/input/pallas_call | solution.py:308
  166.2 0.9 collective-permute-done.2
  167.1 0.7 collective-permute-start.3
  167.8 3.3 %input.6.refs_0_ = bf16[32,256,128]{2,1,0:T(8,128)(2,1)} custom-call(bf16[32,256,128]{2,1,0:T(8,128)(2,1)} %pair_ref.9, bf16[32,256,256]{2,1,0:T(8,128)(2,1)} %get-tuple-element.28.grads_ref, bf16[64,128]{1,0:T(8,128)(2,1)} %bitcast.14, bf16[64,128]{1,0:T(8,128)(2,1)} %bitcast.19, bf16[64,128]{1,0:T(8,128)(2,1)} %bitcast.24, ...), custom_call_target="tpu_custom_call", output_to_operand_aliasing={{}: (6, {})} | custom-call | flops 134217728 | bytes 2097152 | tf_op jit(solution)/shard_map/input/pallas_call | solution.py:308
  171.1 0.3 collective-permute-done.3
  171.5 1.5 collective-permute-start.4
  172.9 3.3 %input.7 = bf16[32,256,128]{2,1,0:T(8,128)(2,1)} custom-call(bf16[32,256,128]{2,1,0:T(8,128)(2,1)} %pair_ref.9, bf16[32,256,256]{2,1,0:T(8,128)(2,1)} %get-tuple-element.28.grads_ref, bf16[64,128]{1,0:T(8,128)(2,1)} %bitcast.15, bf16[64,128]{1,0:T(8,128)(2,1)} %bitcast.20, bf16[64,128]{1,0:T(8,128)(2,1)} %bitcast.25, ...), custom_call_target="tpu_custom_call", output_to_operand_aliasing={{}: (6, {})} | custom-call | flops 134217728 | bytes 2097152 | tf_op jit(solution)/shard_map/input/pallas_call | solution.py:308
  176.2 0.0 collective-permute-done.4
  176.3 0.0 copy-start.1
  176.3 0.1 collective-permute-start.5
  176.4 1.2 collective-permute-done.5.other_ref
  177.6 0.0 copy-done.1
  177.6 0.0 copy-start.2
  177.6 0.6 copy-done.2
  178.2 1.5 finish.1
  (4 shorter events, 0.0 us)
Async XLA Ops:
  0.6 33.5 %all-to-all-start = ((bf16[32,2,32,256]{3,2,1,0:T(8,128)(2,1)}), bf16[32,2,32,256]{3,2,1,0:T(8,128)(2,1)S(1)}, u32[]{:S(2)}, u32[]{:S(2)}) async-start(bf16[32,2,32,256]{3,2,1,0:T(8,128)(2,1)} %bitcast.10), calls=%async_computation | async-start | bytes 2097152 | tf_op jit(solution)/shard_map/all_to_all | solution.py:253
  89.2 52.4 %all-to-all-start.2 = ((bf16[32,4,32,256]{3,2,1,0:T(8,128)(2,1)}), bf16[32,4,32,256]{3,2,1,0:T(8,128)(2,1)S(1)}, u32[]{:S(2)}, u32[]{:S(2)}) async-start(bf16[32,4,32,256]{3,2,1,0:T(8,128)(2,1)} %triangle.1), calls=%async_computation.2 | async-start | bytes 4194304 | tf_op jit(solution)/shard_map/all_to_all | solution.py:303
  141.6 1.3 copy-start
  153.9 1.5 collective-permute-start
  156.2 6.5 %collective-permute-start.1 = (f32[128,128]{1,0:T(8,128)S(1)}, f32[128,128]{1,0:T(8,128)S(1)}, u32[]{:S(2)}, u32[]{:S(2)}) collective-permute-start(f32[128,128]{1,0:T(8,128)S(1)} %add.20), channel_id=1, source_target_pairs={{0,16},{2,18},{4,20},{6,22},{8,24},{10,26},{12,28},{14,30},{16,0},... | collective-permute-start | bytes 196616 | tf_op jit(solution)/shard_map/ppermute | solution.py:329
  162.8 4.3 %collective-permute-start.2 = (f32[128,128]{1,0:T(8,128)S(1)}, f32[128,128]{1,0:T(8,128)S(1)}, u32[]{:S(2)}, u32[]{:S(2)}) collective-permute-start(f32[128,128]{1,0:T(8,128)S(1)} %add.21), channel_id=1, source_target_pairs={{0,8},{2,10},{4,12},{6,14},{8,0},{10,2},{12,4},{14,6},{16,24},{18,... | collective-permute-start | bytes 196616 | tf_op jit(solution)/shard_map/ppermute | solution.py:329
  167.1 4.3 %collective-permute-start.3 = (f32[128,128]{1,0:T(8,128)S(1)}, f32[128,128]{1,0:T(8,128)S(1)}, u32[]{:S(2)}, u32[]{:S(2)}) collective-permute-start(f32[128,128]{1,0:T(8,128)S(1)} %add.22), channel_id=1, source_target_pairs={{0,4},{2,6},{4,0},{6,2},{8,12},{10,14},{12,8},{14,10},{16,20},{18,... | collective-permute-start | bytes 196616 | tf_op jit(solution)/shard_map/ppermute | solution.py:329
  171.5 4.8 %collective-permute-start.4 = (f32[128,128]{1,0:T(8,128)S(1)}, f32[128,128]{1,0:T(8,128)S(1)}, u32[]{:S(2)}, u32[]{:S(2)}) collective-permute-start(f32[128,128]{1,0:T(8,128)S(1)} %add.23), channel_id=1, source_target_pairs={{0,1},{1,0},{2,3},{3,2},{4,5},{5,4},{6,7},{7,6},{8,9},{9,8},{10,11... | collective-permute-start | bytes 196616 | tf_op jit(solution)/shard_map/ppermute | solution.py:329
  176.3 1.3 copy-start.1
  176.3 1.3 collective-permute-start.5
  177.6 0.6 copy-start.2

commit v2 on v0

--- a/solution.py
+++ b/solution.py
@@ -260,7 +260,7 @@
         ],
         out_shape=[lr_shape, gates_shape, normed_shape],
         scratch_shapes=[stacked, rows_scratch],
-        compiler_params=memory(60),
+        compiler_params=memory(20),
         cost_estimate=cost(8 * hidden * dim * columns, pair, lr_shape, gates_shape),
         name="before",
     )(pair, *weights)
@@ -296,7 +296,7 @@
         out_specs=[by_hidden, half, half],
         out_shape=[jax.ShapeDtypeStruct((r, 4 * hidden, c), BF16), half_shape, half_shape],
         scratch_shapes=[pltpu.VMEM((4 * hidden, dim), F32), rows_scratch],
-        compiler_params=memory(28),
+        compiler_params=memory(22),
         name="gates",
     )(bit, exchange(sent), gates, normed)
 

time: 179 us -> 180 us (level)
  local copies, waits for them, and re-layouts: 6.94 us -> 15.7 us
  waiting for transfers between devices: 75.4 us -> 70.4 us
  Pallas kernels: 28.5 us -> 25.8 us
    unnamed x20 -> x34, local copies, waits for them, and re-layouts: 6.94 us -> 15.7 us
    all_to_all x1, waiting for transfers between devices: 15.8 us -> 10.8 us  [channel_shards(): g_all = exchange(cotangent.reshape(devices, own, r, c))]
    pallas_call x1, Pallas kernels: 10.5 us -> 6.6 us  [channel_shards(): pl.pallas_call(functools.partial(before_kernel, own), grid=(r // block,),...]
  transfers between devices with their start and end apart: 8 -> 8, of which waited for: 8 -> 8; matrix products, arithmetic and copies ran while one was open for 0% -> 0% of each run, Pallas kernels for 10% -> 8%
where the time goes in v2:
time: 180 us
  waiting for transfers between devices  70.4 us (39%)
  blocking collectives  52.3 us (29%)
  Pallas kernels  25.8 us (14%)
  local copies, waits for them, and re-layouts  15.7 us (9%)
  starting transfers between devices  14.6 us (8%)
    all_to_all x1, blocking collectives, channel_shards(): exchange(sent)  52.3 us
    all_to_all x1, waiting for transfers between devices, channel_shards(): exchange(sent)  48.7 us
    unnamed x34, local copies, waits for them, and re-layouts  15.7 us
    all_to_all x1, waiting for transfers between devices, channel_shards(): g_all = exchange(cotangent.reshape(devices, own, r, c))  10.8 us
    ppermute x4, waiting for transfers between devices, channel_shards(): other = lax.ppermute(mine, axis, [(i, i ^ step) for i in range(size)])  8.4 us
    pallas_call x1, Pallas kernels, channel_shards(): pl.pallas_call(functools.partial(gates_kernel, own), grid=(r // block,),...  8.13 us
    pallas_call x4, Pallas kernels, input_piece(): pl.pallas_call(input_kernel, grid=(1,), in_specs=[at, pl.BlockSpec((r //...  7.74 us
    all_to_all x1, starting transfers between devices, channel_shards(): g_all = exchange(cotangent.reshape(devices, own, r, c))  7.3 us
  transfers between devices with their start and end apart: 8, of which 8 were waited for; matrix products, arithmetic and copies ran while one was open for 0% of the time, Pallas kernels for 8%

profile of v2, /device:TPU:0, one launch (start us, length us, event | category | flops | bytes accessed | tf_op | source)
XLA Modules:
  0.0 179.7 jit_solution(8227578834327405695)
XLA Ops:
  0.6 0.0 copy-start
  0.6 7.3 %all-to-all-start = ((bf16[32,2,32,256]{3,2,1,0:T(8,128)(2,1)}), bf16[32,2,32,256]{3,2,1,0:T(8,128)(2,1)S(1)}, u32[]{:S(2)}, u32[]{:S(2)}) async-start(bf16[32,2,32,256]{3,2,1,0:T(8,128)(2,1)} %bitcast.30), calls=%async_computation | async-start | bytes 2097152 | tf_op jit(solution)/shard_map/all_to_all | solution.py:251
  8.0 0.0 copy-done
  8.0 0.0 copy-start.7
  8.0 0.7 copy-done.7
  8.7 0.0 copy-start.9
  8.7 0.7 copy-done.9
  9.4 0.7 copy-done.11
  10.1 0.7 copy-done.13
  10.8 6.6 %before.1 = (bf16[32,4,32,256]{3,2,1,0:T(8,128)(2,1)S(1)}, f32[32,256,256]{2,1,0:T(8,128)S(1)}, bf16[32,128,256]{2,1,0:T(8,128)(2,1)S(1)}) custom-call(bf16[32,256,128]{2,1,0:T(8,128)(2,1)S(1)} %copy-done, bf16[64,128]{1,0:T(8,128)(2,1)S(1)} %bitcast.10, bf16[64,128]{1,0:T(8,128)(2,1)S(1)} %bitcast.15, bf16[64,128]{1,0:T(8,128)(2,1)S(1)} %bitcast.20, ...), custom_call_target="tpu_custom_call" | custom-call | flops 536870912 | bytes 12582912 | tf_op jit(solution)/shard_map/before/pallas_call | solution.py:252
  17.4 0.0 copy-start.1
  17.5 3.3 %copy-done.1 = f32[32,256,256]{2,1,0:T(8,128)} copy-done((f32[32,256,256]{2,1,0:T(8,128)}, f32[32,256,256]{2,1,0:T(8,128)S(1)}, u32[]{:S(2)}) %copy-start.1) | copy-done | bytes 8388632
  20.7 1.3 copy-done.4
  22.1 1.3 copy-done.6
  23.4 10.8 %all-to-all-done.cot_ref = bf16[32,2,32,256]{3,2,1,0:T(8,128)(2,1)S(1)} async-done(((bf16[32,2,32,256]{3,2,1,0:T(8,128)(2,1)}), bf16[32,2,32,256]{3,2,1,0:T(8,128)(2,1)S(1)}, u32[]{:S(2)}, u32[]{:S(2)}) %all-to-all-start) | async-done | bytes 1048608 | tf_op jit(solution)/shard_map/all_to_all | solution.py:251
  34.2 52.3 %all_to_all.15.in_ref = bf16[32,4,32,256]{3,2,1,0:T(8,128)(2,1)S(1)} all-to-all(bf16[32,4,32,256]{3,2,1,0:T(8,128)(2,1)} %copy-done.6), channel_id=1, replica_groups=mesh['row'=16,'col'=2] {'row','col'}, dimensions={0} | all-to-all | bytes 4194304 | tf_op jit(solution)/shard_map/all_to_all | solution.py:281
  86.5 1.8 triangle.1
  88.3 0.0 copy-start.3
  88.3 1.3 copy-done.3
  89.6 3.8 %all-to-all-start.2 = ((bf16[32,4,32,256]{3,2,1,0:T(8,128)(2,1)}), bf16[32,4,32,256]{3,2,1,0:T(8,128)(2,1)}, u32[]{:S(2)}, u32[]{:S(2)}) async-start(bf16[32,4,32,256]{3,2,1,0:T(8,128)(2,1)} %copy-done.3), calls=%async_computation.2 | async-start | bytes 4194304 | tf_op jit(solution)/shard_map/all_to_all | solution.py:301
  93.5 48.7 %all-to-all-done.2.d_ref = bf16[32,4,32,256]{3,2,1,0:T(8,128)(2,1)} async-done(((bf16[32,4,32,256]{3,2,1,0:T(8,128)(2,1)}), bf16[32,4,32,256]{3,2,1,0:T(8,128)(2,1)}, u32[]{:S(2)}, u32[]{:S(2)}) %all-to-all-start.2) | async-done | bytes 2097184 | tf_op jit(solution)/shard_map/all_to_all | solution.py:301
  142.1 3.4 %copy-done.2 = f32[32,256,256]{2,1,0:T(8,128)S(1)} copy-done((f32[32,256,256]{2,1,0:T(8,128)S(1)}, f32[32,256,256]{2,1,0:T(8,128)}, u32[]{:S(2)}) %copy-start.2) | copy-done | bytes 8388632
  145.5 1.6 copy-done.5
  147.1 8.1 %gates.1 = (bf16[32,256,256]{2,1,0:T(8,128)(2,1)S(1)}, f32[128,128]{1,0:T(8,128)S(1)}, f32[128,128]{1,0:T(8,128)S(1)}) custom-call(s32[1]{0:T(128)} %bitcast.bit_ref, bf16[32,4,32,256]{3,2,1,0:T(8,128)(2,1)} %all-to-all-done.2.d_ref, f32[32,256,256]{2,1,0:T(8,128)S(1)} %copy-done.2, bf16[32,128,256]{2,1,0:T(8,128)(2,1)S(1)} %copy-done.5), custom_call_target="tpu_custom_call" | custom-call | tf_op jit(solution)/shard_map/gates/pallas_call | solution.py:287
  155.3 0.1 collective-permute-start
  155.3 1.2 collective-permute-done
  156.6 1.1 collective-permute-start.1
  157.7 0.0 copy-done.8
  157.7 0.0 copy-done.10
  157.7 0.0 copy-done.12
  157.7 0.0 copy-done.14
  157.7 1.9 %input.4.refs_0_ = bf16[32,256,128]{2,1,0:T(8,128)(2,1)} custom-call(bf16[32,256,128]{2,1,0:T(8,128)(2,1)S(1)} %copy-done, bf16[32,256,256]{2,1,0:T(8,128)(2,1)S(1)} %get-tuple-element.28.grads_ref, bf16[64,128]{1,0:T(8,128)(2,1)S(1)} %bitcast.11, bf16[64,128]{1,0:T(8,128)(2,1)S(1)} %bitcast.16, bf16[64,128]{1,0:T(8,128)(2,1)S(1)} %bitcast.21, ...), custom_call_target="tpu_custom_call" | custom-call | flops 134217728 | bytes 2097152 | tf_op jit(solution)/shard_map/input/pallas_call | solution.py:306
  159.6 3.5 %collective-permute-done.1 = f32[128,128]{1,0:T(8,128)S(1)} collective-permute-done((f32[128,128]{1,0:T(8,128)S(1)}, f32[128,128]{1,0:T(8,128)S(1)}, u32[]{:S(2)}, u32[]{:S(2)}) %collective-permute-start.1) | collective-permute-done | bytes 65568 | tf_op jit(solution)/shard_map/ppermute | solution.py:327
  163.1 0.1 collective-permute-start.2
  163.2 1.9 %input.5.refs_0_ = bf16[32,256,128]{2,1,0:T(8,128)(2,1)} custom-call(bf16[32,256,128]{2,1,0:T(8,128)(2,1)S(1)} %copy-done, bf16[32,256,256]{2,1,0:T(8,128)(2,1)S(1)} %get-tuple-element.28.grads_ref, bf16[64,128]{1,0:T(8,128)(2,1)S(1)} %bitcast.12, bf16[64,128]{1,0:T(8,128)(2,1)S(1)} %bitcast.17, ...), custom_call_target="tpu_custom_call", output_to_operand_aliasing={{}: (6, {})} | custom-call | flops 134217728 | bytes 2097152 | tf_op jit(solution)/shard_map/input/pallas_call | solution.py:306
  165.2 2.3 %collective-permute-done.2 = f32[128,128]{1,0:T(8,128)S(1)} collective-permute-done((f32[128,128]{1,0:T(8,128)S(1)}, f32[128,128]{1,0:T(8,128)S(1)}, u32[]{:S(2)}, u32[]{:S(2)}) %collective-permute-start.2) | collective-permute-done | bytes 65568 | tf_op jit(solution)/shard_map/ppermute | solution.py:327
  167.5 0.7 collective-permute-start.3
  168.2 1.9 %input.6.refs_0_ = bf16[32,256,128]{2,1,0:T(8,128)(2,1)} custom-call(bf16[32,256,128]{2,1,0:T(8,128)(2,1)S(1)} %copy-done, bf16[32,256,256]{2,1,0:T(8,128)(2,1)S(1)} %get-tuple-element.28.grads_ref, bf16[64,128]{1,0:T(8,128)(2,1)S(1)} %bitcast.13, bf16[64,128]{1,0:T(8,128)(2,1)S(1)} %bitcast.18, ...), custom_call_target="tpu_custom_call", output_to_operand_aliasing={{}: (6, {})} | custom-call | flops 134217728 | bytes 2097152 | tf_op jit(solution)/shard_map/input/pallas_call | solution.py:306
  170.1 1.7 collective-permute-done.3
  171.8 1.5 collective-permute-start.4
  173.3 1.9 %input.7 = bf16[32,256,128]{2,1,0:T(8,128)(2,1)} custom-call(bf16[32,256,128]{2,1,0:T(8,128)(2,1)S(1)} %copy-done, bf16[32,256,256]{2,1,0:T(8,128)(2,1)S(1)} %get-tuple-element.28.grads_ref, bf16[64,128]{1,0:T(8,128)(2,1)S(1)} %bitcast.14, bf16[64,128]{1,0:T(8,128)(2,1)S(1)} %bitcast.19, ...), custom_call_target="tpu_custom_call", output_to_operand_aliasing={{}: (6, {})} | custom-call | flops 134217728 | bytes 2097152 | tf_op jit(solution)/shard_map/input/pallas_call | solution.py:306
  175.2 0.9 collective-permute-done.4
  176.2 0.0 copy-start.15
  176.2 0.1 collective-permute-start.5
  176.3 1.2 collective-permute-done.5.other_ref
  177.5 0.0 copy-done.15
  177.5 0.6 copy-done.16
  178.1 1.5 finish.1
  (16 shorter events, 0.1 us)
Async XLA Ops:
  0.6 7.3 %copy-start = (bf16[32,256,128]{2,1,0:T(8,128)(2,1)S(1)}, bf16[32,256,128]{2,1,0:T(8,128)(2,1)}, u32[]{:S(2)}) copy-start(bf16[32,256,128]{2,1,0:T(8,128)(2,1)} %pair_ref.9) | copy-start | bytes 6291460
  0.6 33.5 %all-to-all-start = ((bf16[32,2,32,256]{3,2,1,0:T(8,128)(2,1)}), bf16[32,2,32,256]{3,2,1,0:T(8,128)(2,1)S(1)}, u32[]{:S(2)}, u32[]{:S(2)}) async-start(bf16[32,2,32,256]{3,2,1,0:T(8,128)(2,1)} %bitcast.30), calls=%async_computation | async-start | bytes 2097152 | tf_op jit(solution)/shard_map/all_to_all | solution.py:251
  8.0 0.7 copy-start.7
  8.7 0.7 copy-start.9
  9.4 0.7 copy-start.11
  10.1 0.7 copy-start.13
  17.4 3.3 %copy-start.1 = (f32[32,256,256]{2,1,0:T(8,128)}, f32[32,256,256]{2,1,0:T(8,128)S(1)}, u32[]{:S(2)}) copy-start(f32[32,256,256]{2,1,0:T(8,128)S(1)} %get-tuple-element.24.gates_ref) | copy-start | bytes 25165828
  20.7 1.3 copy-start.4
  22.1 1.3 copy-start.6
  88.3 1.3 copy-start.3
  89.6 52.5 %all-to-all-start.2 = ((bf16[32,4,32,256]{3,2,1,0:T(8,128)(2,1)}), bf16[32,4,32,256]{3,2,1,0:T(8,128)(2,1)}, u32[]{:S(2)}, u32[]{:S(2)}) async-start(bf16[32,4,32,256]{3,2,1,0:T(8,128)(2,1)} %copy-done.3), calls=%async_computation.2 | async-start | bytes 4194304 | tf_op jit(solution)/shard_map/all_to_all | solution.py:301
  142.1 3.4 %copy-start.2 = (f32[32,256,256]{2,1,0:T(8,128)S(1)}, f32[32,256,256]{2,1,0:T(8,128)}, u32[]{:S(2)}) copy-start(f32[32,256,256]{2,1,0:T(8,128)} %copy-done.1) | copy-start | bytes 25165828
  145.5 1.6 copy-start.5
  147.1 10.6 %copy-start.8 = (bf16[128,64]{0,1:T(8,128)(2,1)S(1)}, bf16[128,64]{0,1:T(8,128)(2,1)}, u32[]{:S(2)}) copy-start(bf16[128,64]{0,1:T(8,128)(2,1)} %param.8) | copy-start | bytes 49156
  147.1 10.6 %copy-start.10 = (bf16[128,64]{0,1:T(8,128)(2,1)S(1)}, bf16[128,64]{0,1:T(8,128)(2,1)}, u32[]{:S(2)}) copy-start(bf16[128,64]{0,1:T(8,128)(2,1)} %param.9) | copy-start | bytes 49156
  147.1 10.6 %copy-start.12 = (bf16[128,64]{0,1:T(8,128)(2,1)S(1)}, bf16[128,64]{0,1:T(8,128)(2,1)}, u32[]{:S(2)}) copy-start(bf16[128,64]{0,1:T(8,128)(2,1)} %param.10) | copy-start | bytes 49156
  147.1 10.6 %copy-start.14 = (bf16[128,64]{0,1:T(8,128)(2,1)S(1)}, bf16[128,64]{0,1:T(8,128)(2,1)}, u32[]{:S(2)}) copy-start(bf16[128,64]{0,1:T(8,128)(2,1)} %param.11) | copy-start | bytes 49156
  155.3 1.3 collective-permute-start
  156.6 6.5 %collective-permute-start.1 = (f32[128,128]{1,0:T(8,128)S(1)}, f32[128,128]{1,0:T(8,128)S(1)}, u32[]{:S(2)}, u32[]{:S(2)}) collective-permute-start(f32[128,128]{1,0:T(8,128)S(1)} %add.20), channel_id=1, source_target_pairs={{0,16},{2,18},{4,20},{6,22},{8,24},{10,26},{12,28},{14,30},{16,0},... | collective-permute-start | bytes 196616 | tf_op jit(solution)/shard_map/ppermute | solution.py:327
  163.1 4.3 %collective-permute-start.2 = (f32[128,128]{1,0:T(8,128)S(1)}, f32[128,128]{1,0:T(8,128)S(1)}, u32[]{:S(2)}, u32[]{:S(2)}) collective-permute-start(f32[128,128]{1,0:T(8,128)S(1)} %add.21), channel_id=1, source_target_pairs={{0,8},{2,10},{4,12},{6,14},{8,0},{10,2},{12,4},{14,6},{16,24},{18,... | collective-permute-start | bytes 196616 | tf_op jit(solution)/shard_map/ppermute | solution.py:327
  167.5 4.3 %collective-permute-start.3 = (f32[128,128]{1,0:T(8,128)S(1)}, f32[128,128]{1,0:T(8,128)S(1)}, u32[]{:S(2)}, u32[]{:S(2)}) collective-permute-start(f32[128,128]{1,0:T(8,128)S(1)} %add.22), channel_id=1, source_target_pairs={{0,4},{2,6},{4,0},{6,2},{8,12},{10,14},{12,8},{14,10},{16,20},{18,... | collective-permute-start | bytes 196616 | tf_op jit(solution)/shard_map/ppermute | solution.py:327
  171.8 4.3 %collective-permute-start.4 = (f32[128,128]{1,0:T(8,128)S(1)}, f32[128,128]{1,0:T(8,128)S(1)}, u32[]{:S(2)}, u32[]{:S(2)}) collective-permute-start(f32[128,128]{1,0:T(8,128)S(1)} %add.23), channel_id=1, source_target_pairs={{0,1},{1,0},{2,3},{3,2},{4,5},{5,4},{6,7},{7,6},{8,9},{9,8},{10,11... | collective-permute-start | bytes 196616 | tf_op jit(solution)/shard_map/ppermute | solution.py:327
  176.2 1.3 copy-start.15
  176.2 1.3 collective-permute-start.5
  177.5 0.6 copy-start.16

commit v3 on v0

--- a/solution.py
+++ b/solution.py
@@ -116,30 +116,24 @@
     return jnp.concatenate([ref[i, at, :] for i in range(ref.shape[0])], axis=1)
 
 
-def before_kernel(own, pair_ref, wl, wlg, wr, wrg, out_ref, gates_ref, normed_ref, w_ref, rows_ref):
+def before_kernel(own, pair_ref, wl, wlg, wr, wrg, out_ref, w_ref, rows_ref):
     stack_weights((wl, wlg, wr, wrg), w_ref)
     h = wl.shape[0]
     rows = pair_ref.shape[0]
+    pitch = rows + 1
 
     def one_row(r, carry):
         normed = layer_norm(pair_ref[r])[0].astype(BF16)
-        normed_ref[r] = normed
-        projected = dot(w_ref[...], normed)
-        for side in range(2):
-            q = projected[2 * side * h : (2 * side + 1) * h]
-            s = jax.nn.sigmoid(projected[(2 * side + 1) * h : (2 * side + 2) * h])
-            value = s * q
-            start = pl.multiple_of(r * 2 * h + side * h, h)
-            put_lanes(rows_ref, pl.ds(start, h), value)
-            gates_ref[r, pl.ds(2 * side * h, h), :] = s
-            gates_ref[r, pl.ds((2 * side + 1) * h, h), :] = value * (1.0 - s)
+        q_left, s_left, q_right, s_right = project(w_ref, normed)
+        put_lanes(rows_ref, pl.ds(r, h, stride=pitch), s_left * q_left)
+        put_lanes(rows_ref, pl.ds(r + h * pitch, h, stride=pitch), s_right * q_right)
         return carry
 
     lax.fori_loop(0, rows, one_row, 0, unroll=4)
     for channel in range(h):
         to, slot = channel // own, (channel % own) * 2
         for side in range(2):
-            line = get_lanes(rows_ref, pl.ds(side * h + channel, rows, stride=2 * h))
+            line = get_lanes(rows_ref, pl.ds((side * h + channel) * pitch, rows))
             out_ref[to, slot + side] = line.astype(BF16)
 
 
@@ -158,8 +152,11 @@
                 out_ref[a * cols + b, i] = d[a * r : (a + 1) * r, b * c : (b + 1) * c]
 
 
-def gates_kernel(own, bit_ref, d_ref, gates_ref, normed_ref, grads_ref, kept_ref, sent_ref, sums_ref, rows_ref):
-    rows, h = gates_ref.shape[0], gates_ref.shape[1] // 4
+def gates_kernel(own, bit_ref, pair_ref, d_ref, wl, wlg, wr, wrg, grads_ref, kept_ref, sent_ref, w_ref, sums_ref, rows_ref):
+    stack_weights((wl, wlg, wr, wrg), w_ref)
+    h = wl.shape[0]
+    rows = pair_ref.shape[0]
+    pitch = rows + 1
 
     @pl.when(pl.program_id(0) == 0)
     def _():
@@ -169,17 +166,18 @@
         to, slot = channel // own, (channel % own) * 2
         for side in range(2):
             line = d_ref[to, slot + side].astype(F32)
-            put_lanes(rows_ref, pl.ds(side * h + channel, rows, stride=2 * h), line)
+            put_lanes(rows_ref, pl.ds((side * h + channel) * pitch, rows), line)
 
     def one_row(r, carry):
-        parts = []
-        for side in range(2):
-            d = get_lanes(rows_ref, pl.ds(pl.multiple_of(r * 2 * h + side * h, h), h))
-            parts.append(d * gates_ref[r, pl.ds(2 * side * h, h), :])
-            parts.append(d * gates_ref[r, pl.ds((2 * side + 1) * h, h), :])
-        grads = jnp.concatenate(parts, axis=0).astype(BF16)
+        normed = layer_norm(pair_ref[r])[0].astype(BF16)
+        q_left, s_left, q_right, s_right = project(w_ref, normed)
+        e_left = get_lanes(rows_ref, pl.ds(r, h, stride=pitch)) * s_left
+        e_right = get_lanes(rows_ref, pl.ds(r + h * pitch, h, stride=pitch)) * s_right
+        f_left = e_left * q_left * (1.0 - s_left)
+        f_right = e_right * q_right * (1.0 - s_right)
+        grads = jnp.concatenate([e_left, f_left, e_right, f_right], axis=0).astype(BF16)
         grads_ref[r] = grads
-        sums_ref[...] += dot(grads, normed_ref[r], NT)
+        sums_ref[...] += dot(grads, normed, NT)
         return carry
 
     lax.fori_loop(0, rows, one_row, 0, unroll=4)
@@ -233,7 +231,7 @@
     )
     stacked = pltpu.VMEM((4 * hidden, dim), BF16)
     lanes = min(c, 128)
-    rows_scratch = pltpu.VMEM((c // lanes, 2 * hidden * block, lanes), F32)
+    rows_scratch = pltpu.VMEM((c // lanes, 2 * hidden * (block + 1), lanes), F32)
 
     def cost(flops, *arrays):
         moved = sum(a.size * a.dtype.itemsize for a in arrays)
@@ -244,24 +242,17 @@
 
     columns = r * c
     lr_shape = jax.ShapeDtypeStruct((devices, 2 * own, r, c), BF16)
-    gates_shape = jax.ShapeDtypeStruct((r, 4 * hidden, c), F32)
-    normed_shape = jax.ShapeDtypeStruct((r, dim, c), BF16)
     by_hidden = pl.BlockSpec((block, 4 * hidden, c), lambda i: (i, 0, 0))
-    by_dim = pl.BlockSpec((block, dim, c), lambda i: (i, 0, 0))
     g_all = exchange(cotangent.reshape(devices, own, r, c))
-    sent, gates, normed = pl.pallas_call(
+    sent = pl.pallas_call(
         functools.partial(before_kernel, own),
         grid=(r // block,),
         in_specs=[tile] + [whole] * 4,
-        out_specs=[
-            pl.BlockSpec((devices, 2 * own, block, c), lambda i: (0, 0, i, 0)),
-            by_hidden,
-            by_dim,
-        ],
-        out_shape=[lr_shape, gates_shape, normed_shape],
+        out_specs=pl.BlockSpec((devices, 2 * own, block, c), lambda i: (0, 0, i, 0)),
+        out_shape=lr_shape,
         scratch_shapes=[stacked, rows_scratch],
         compiler_params=memory(60),
-        cost_estimate=cost(8 * hidden * dim * columns, pair, lr_shape, gates_shape),
+        cost_estimate=cost(8 * hidden * dim * columns, pair, lr_shape),
         name="before",
     )(pair, *weights)
 
@@ -289,16 +280,16 @@
         grid=(r // block,),
         in_specs=[
             smem,
+            tile,
             pl.BlockSpec((devices, 2 * own, block, c), lambda i: (0, 0, i, 0)),
-            by_hidden,
-            by_dim,
-        ],
+        ]
+        + [whole] * 4,
         out_specs=[by_hidden, half, half],
         out_shape=[jax.ShapeDtypeStruct((r, 4 * hidden, c), BF16), half_shape, half_shape],
-        scratch_shapes=[pltpu.VMEM((4 * hidden, dim), F32), rows_scratch],
+        scratch_shapes=[stacked, pltpu.VMEM((4 * hidden, dim), F32), rows_scratch],
         compiler_params=memory(28),
         name="gates",
-    )(bit, exchange(sent), gates, normed)
+    )(bit, pair, exchange(sent), *weights)
 
     def input_piece(piece, pair_gradient):
         held = [] if pair_gradient is None else [pair_gradient]

time: 179 us -> 174 us (0.972)
  local copies, waits for them, and re-layouts: 6.94 us -> 1.96 us
  waiting for transfers between devices: 75.4 us -> 79.3 us
  Pallas kernels: 28.5 us -> 24.9 us
    unnamed x20 -> x16, local copies, waits for them, and re-layouts: 6.94 us -> 1.96 us
    pallas_call x1, Pallas kernels: 10.5 us -> 6.52 us  [channel_shards(): pl.pallas_call(functools.partial(before_kernel, own), grid=(r // block,),...]
    all_to_all x1, waiting for transfers between devices: 15.8 us -> 19.7 us  [channel_shards(): g_all = exchange(cotangent.reshape(devices, own, r, c))]
  transfers between devices with their start and end apart: 8 -> 8, of which waited for: 8 -> 8; matrix products, arithmetic and copies ran while one was open for 0% -> 0% of each run, Pallas kernels for 10% -> 8%
where the time goes in v3:
time: 174 us
  waiting for transfers between devices  79.3 us (46%)
  blocking collectives  52.3 us (30%)
  Pallas kernels  24.9 us (14%)
  starting transfers between devices  14.6 us (8%)
  local copies, waits for them, and re-layouts  1.96 us (1%)
    all_to_all x1, blocking collectives, channel_shards(): exchange(sent)  52.3 us
    all_to_all x1, waiting for transfers between devices, channel_shards(): exchange(sent)  48.7 us
    all_to_all x1, waiting for transfers between devices, channel_shards(): g_all = exchange(cotangent.reshape(devices, own, r, c))  19.7 us
    ppermute x4, waiting for transfers between devices, channel_shards(): other = lax.ppermute(mine, axis, [(i, i ^ step) for i in range(size)])  8.42 us
    pallas_call x4, Pallas kernels, input_piece(): pl.pallas_call(input_kernel, grid=(1,), in_specs=[at, pl.BlockSpec((r //...  7.74 us
    pallas_call x1, Pallas kernels, channel_shards(): pl.pallas_call(functools.partial(gates_kernel, own), grid=(r // block,),...  7.34 us
    all_to_all x1, starting transfers between devices, channel_shards(): g_all = exchange(cotangent.reshape(devices, own, r, c))  7.3 us
    pallas_call x1, Pallas kernels, channel_shards(): pl.pallas_call(functools.partial(before_kernel, own), grid=(r // block,),...  6.52 us
  transfers between devices with their start and end apart: 8, of which 8 were waited for; matrix products, arithmetic and copies ran while one was open for 0% of the time, Pallas kernels for 8%

profile of v3, /device:TPU:0, one launch (start us, length us, event | category | flops | bytes accessed | tf_op | source)
XLA Modules:
  0.0 173.9 jit_solution(3988685753038964899)
XLA Ops:
  0.6 7.3 %all-to-all-start = ((bf16[32,2,32,256]{3,2,1,0:T(8,128)(2,1)}), bf16[32,2,32,256]{3,2,1,0:T(8,128)(2,1)S(1)}, u32[]{:S(2)}, u32[]{:S(2)}) async-start(bf16[32,2,32,256]{3,2,1,0:T(8,128)(2,1)} %bitcast.34), calls=%async_computation | async-start | bytes 2097152 | tf_op jit(solution)/shard_map/all_to_all | solution.py:246
  7.9 6.5 %before.1 = bf16[32,4,32,256]{3,2,1,0:T(8,128)(2,1)} custom-call(bf16[32,256,128]{2,1,0:T(8,128)(2,1)} %pair_ref.11, bf16[64,128]{1,0:T(8,128)(2,1)} %bitcast.10, bf16[64,128]{1,0:T(8,128)(2,1)} %bitcast.16, bf16[64,128]{1,0:T(8,128)(2,1)} %bitcast.22, bf16[64,128]{1,0:T(8,128)(2,1)} %bitcast.28), custom_call_target="tpu_custom_call" | custom-call | flops 536870912 | bytes 4194304 | tf_op jit(solution)/shard_map/before/pallas_call | solution.py:247
  14.5 19.7 %all-to-all-done.cot_ref = bf16[32,2,32,256]{3,2,1,0:T(8,128)(2,1)S(1)} async-done(((bf16[32,2,32,256]{3,2,1,0:T(8,128)(2,1)}), bf16[32,2,32,256]{3,2,1,0:T(8,128)(2,1)S(1)}, u32[]{:S(2)}, u32[]{:S(2)}) %all-to-all-start) | async-done | bytes 1048608 | tf_op jit(solution)/shard_map/all_to_all | solution.py:246
  34.2 52.3 %all_to_all.15.in_ref = bf16[32,4,32,256]{3,2,1,0:T(8,128)(2,1)S(1)} all-to-all(bf16[32,4,32,256]{3,2,1,0:T(8,128)(2,1)} %before.1), channel_id=1, replica_groups=mesh['row'=16,'col'=2] {'row','col'}, dimensions={0} | all-to-all | bytes 4194304 | tf_op jit(solution)/shard_map/all_to_all | solution.py:272
  86.5 1.8 %triangle.1 = bf16[32,4,32,256]{3,2,1,0:T(8,128)(2,1)S(1)} custom-call(bf16[32,2,32,256]{3,2,1,0:T(8,128)(2,1)S(1)} %all-to-all-done.cot_ref, bf16[32,4,32,256]{3,2,1,0:T(8,128)(2,1)S(1)} %all_to_all.15.in_ref), custom_call_target="tpu_custom_call" | custom-call | tf_op jit(solution)/shard_map/triangle/pallas_call | solution.py:260
  88.3 0.0 copy-start.1
  88.3 1.3 copy-done.1
  89.6 0.0 copy-start
  89.6 0.0 copy-start.2
  89.6 0.0 copy-start.3
  89.6 0.0 copy-start.4
  89.6 0.0 copy-start.5
  89.7 3.8 %all-to-all-start.2 = ((bf16[32,4,32,256]{3,2,1,0:T(8,128)(2,1)}), bf16[32,4,32,256]{3,2,1,0:T(8,128)(2,1)}, u32[]{:S(2)}, u32[]{:S(2)}) async-start(bf16[32,4,32,256]{3,2,1,0:T(8,128)(2,1)} %copy-done.1), calls=%async_computation.2 | async-start | bytes 4194304 | tf_op jit(solution)/shard_map/all_to_all | solution.py:292
  93.5 48.7 %all-to-all-done.2.d_ref = bf16[32,4,32,256]{3,2,1,0:T(8,128)(2,1)} async-done(((bf16[32,4,32,256]{3,2,1,0:T(8,128)(2,1)}), bf16[32,4,32,256]{3,2,1,0:T(8,128)(2,1)}, u32[]{:S(2)}, u32[]{:S(2)}) %all-to-all-start.2) | async-done | bytes 2097184 | tf_op jit(solution)/shard_map/all_to_all | solution.py:292
  142.2 0.0 copy-done
  142.2 0.0 copy-done.2
  142.2 0.0 copy-done.3
  142.2 0.0 copy-done.4
  142.2 0.0 copy-done.5
  142.2 7.3 %gates.1 = (bf16[32,256,256]{2,1,0:T(8,128)(2,1)S(1)}, f32[128,128]{1,0:T(8,128)S(1)}, f32[128,128]{1,0:T(8,128)S(1)}) custom-call(s32[1]{0:T(128)} %bitcast.bit_ref, bf16[32,256,128]{2,1,0:T(8,128)(2,1)S(1)} %copy-done, bf16[32,4,32,256]{3,2,1,0:T(8,128)(2,1)} %all-to-all-done.2.d_ref, bf16[64,128]{1,0:T(8,128)(2,1)S(1)} %bitcast.11, ...), custom_call_target="tpu_custom_call" | custom-call | tf_op jit(solution)/shard_map/gates/pallas_call | solution.py:278
  149.5 0.1 collective-permute-start
  149.6 1.2 collective-permute-done
  150.9 1.1 collective-permute-start.1
  152.0 1.9 %input.4.refs_0_ = bf16[32,256,128]{2,1,0:T(8,128)(2,1)} custom-call(bf16[32,256,128]{2,1,0:T(8,128)(2,1)S(1)} %copy-done, bf16[32,256,256]{2,1,0:T(8,128)(2,1)S(1)} %get-tuple-element.22.grads_ref, bf16[64,128]{1,0:T(8,128)(2,1)S(1)} %bitcast.12, bf16[64,128]{1,0:T(8,128)(2,1)S(1)} %bitcast.18, bf16[64,128]{1,0:T(8,128)(2,1)S(1)} %bitcast.24, ...), custom_call_target="tpu_custom_call" | custom-call | flops 134217728 | bytes 2097152 | tf_op jit(solution)/shard_map/input/pallas_call | solution.py:297
  153.9 3.5 %collective-permute-done.1 = f32[128,128]{1,0:T(8,128)S(1)} collective-permute-done((f32[128,128]{1,0:T(8,128)S(1)}, f32[128,128]{1,0:T(8,128)S(1)}, u32[]{:S(2)}, u32[]{:S(2)}) %collective-permute-start.1) | collective-permute-done | bytes 65568 | tf_op jit(solution)/shard_map/ppermute | solution.py:318
  157.4 0.1 collective-permute-start.2
  157.5 1.9 %input.5.refs_0_ = bf16[32,256,128]{2,1,0:T(8,128)(2,1)} custom-call(bf16[32,256,128]{2,1,0:T(8,128)(2,1)S(1)} %copy-done, bf16[32,256,256]{2,1,0:T(8,128)(2,1)S(1)} %get-tuple-element.22.grads_ref, bf16[64,128]{1,0:T(8,128)(2,1)S(1)} %bitcast.13, bf16[64,128]{1,0:T(8,128)(2,1)S(1)} %bitcast.19, ...), custom_call_target="tpu_custom_call", output_to_operand_aliasing={{}: (6, {})} | custom-call | flops 134217728 | bytes 2097152 | tf_op jit(solution)/shard_map/input/pallas_call | solution.py:297
  159.4 2.3 %collective-permute-done.2 = f32[128,128]{1,0:T(8,128)S(1)} collective-permute-done((f32[128,128]{1,0:T(8,128)S(1)}, f32[128,128]{1,0:T(8,128)S(1)}, u32[]{:S(2)}, u32[]{:S(2)}) %collective-permute-start.2) | collective-permute-done | bytes 65568 | tf_op jit(solution)/shard_map/ppermute | solution.py:318
  161.8 0.7 collective-permute-start.3
  162.5 1.9 %input.6.refs_0_ = bf16[32,256,128]{2,1,0:T(8,128)(2,1)} custom-call(bf16[32,256,128]{2,1,0:T(8,128)(2,1)S(1)} %copy-done, bf16[32,256,256]{2,1,0:T(8,128)(2,1)S(1)} %get-tuple-element.22.grads_ref, bf16[64,128]{1,0:T(8,128)(2,1)S(1)} %bitcast.14, bf16[64,128]{1,0:T(8,128)(2,1)S(1)} %bitcast.20, ...), custom_call_target="tpu_custom_call", output_to_operand_aliasing={{}: (6, {})} | custom-call | flops 134217728 | bytes 2097152 | tf_op jit(solution)/shard_map/input/pallas_call | solution.py:297
  164.4 1.7 collective-permute-done.3
  166.1 1.5 collective-permute-start.4
  167.6 1.9 %input.7 = bf16[32,256,128]{2,1,0:T(8,128)(2,1)} custom-call(bf16[32,256,128]{2,1,0:T(8,128)(2,1)S(1)} %copy-done, bf16[32,256,256]{2,1,0:T(8,128)(2,1)S(1)} %get-tuple-element.22.grads_ref, bf16[64,128]{1,0:T(8,128)(2,1)S(1)} %bitcast.15, bf16[64,128]{1,0:T(8,128)(2,1)S(1)} %bitcast.21, ...), custom_call_target="tpu_custom_call", output_to_operand_aliasing={{}: (6, {})} | custom-call | flops 134217728 | bytes 2097152 | tf_op jit(solution)/shard_map/input/pallas_call | solution.py:297
  169.5 0.9 collective-permute-done.4
  170.4 0.0 copy-start.6
  170.5 0.1 collective-permute-start.5
  170.5 1.2 collective-permute-done.5.other_ref
  171.8 0.0 copy-done.6
  171.8 0.0 copy-start.7
  171.8 0.6 copy-done.7
  172.4 1.5 finish.1
  (5 shorter events, 0.0 us)
Async XLA Ops:
  0.6 33.5 %all-to-all-start = ((bf16[32,2,32,256]{3,2,1,0:T(8,128)(2,1)}), bf16[32,2,32,256]{3,2,1,0:T(8,128)(2,1)S(1)}, u32[]{:S(2)}, u32[]{:S(2)}) async-start(bf16[32,2,32,256]{3,2,1,0:T(8,128)(2,1)} %bitcast.34), calls=%async_computation | async-start | bytes 2097152 | tf_op jit(solution)/shard_map/all_to_all | solution.py:246
  88.3 1.3 copy-start.1
  89.6 52.5 %copy-start = (bf16[32,256,128]{2,1,0:T(8,128)(2,1)S(1)}, bf16[32,256,128]{2,1,0:T(8,128)(2,1)}, u32[]{:S(2)}) copy-start(bf16[32,256,128]{2,1,0:T(8,128)(2,1)} %pair_ref.11) | copy-start | bytes 6291460
  89.6 52.5 %copy-start.2 = (bf16[128,64]{0,1:T(8,128)(2,1)S(1)}, bf16[128,64]{0,1:T(8,128)(2,1)}, u32[]{:S(2)}) copy-start(bf16[128,64]{0,1:T(8,128)(2,1)} %param.8) | copy-start | bytes 49156
  89.6 52.5 %copy-start.3 = (bf16[128,64]{0,1:T(8,128)(2,1)S(1)}, bf16[128,64]{0,1:T(8,128)(2,1)}, u32[]{:S(2)}) copy-start(bf16[128,64]{0,1:T(8,128)(2,1)} %param.9) | copy-start | bytes 49156
  89.6 52.5 %copy-start.4 = (bf16[128,64]{0,1:T(8,128)(2,1)S(1)}, bf16[128,64]{0,1:T(8,128)(2,1)}, u32[]{:S(2)}) copy-start(bf16[128,64]{0,1:T(8,128)(2,1)} %param.10) | copy-start | bytes 49156
  89.6 52.5 %copy-start.5 = (bf16[128,64]{0,1:T(8,128)(2,1)S(1)}, bf16[128,64]{0,1:T(8,128)(2,1)}, u32[]{:S(2)}) copy-start(bf16[128,64]{0,1:T(8,128)(2,1)} %param.11) | copy-start | bytes 49156
  89.7 52.5 %all-to-all-start.2 = ((bf16[32,4,32,256]{3,2,1,0:T(8,128)(2,1)}), bf16[32,4,32,256]{3,2,1,0:T(8,128)(2,1)}, u32[]{:S(2)}, u32[]{:S(2)}) async-start(bf16[32,4,32,256]{3,2,1,0:T(8,128)(2,1)} %copy-done.1), calls=%async_computation.2 | async-start | bytes 4194304 | tf_op jit(solution)/shard_map/all_to_all | solution.py:292
  149.5 1.3 collective-permute-start
  150.9 6.5 %collective-permute-start.1 = (f32[128,128]{1,0:T(8,128)S(1)}, f32[128,128]{1,0:T(8,128)S(1)}, u32[]{:S(2)}, u32[]{:S(2)}) collective-permute-start(f32[128,128]{1,0:T(8,128)S(1)} %add.20), channel_id=1, source_target_pairs={{0,16},{2,18},{4,20},{6,22},{8,24},{10,26},{12,28},{14,30},{16,0},... | collective-permute-start | bytes 196616 | tf_op jit(solution)/shard_map/ppermute | solution.py:318
  157.4 4.3 %collective-permute-start.2 = (f32[128,128]{1,0:T(8,128)S(1)}, f32[128,128]{1,0:T(8,128)S(1)}, u32[]{:S(2)}, u32[]{:S(2)}) collective-permute-start(f32[128,128]{1,0:T(8,128)S(1)} %add.21), channel_id=1, source_target_pairs={{0,8},{2,10},{4,12},{6,14},{8,0},{10,2},{12,4},{14,6},{16,24},{18,... | collective-permute-start | bytes 196616 | tf_op jit(solution)/shard_map/ppermute | solution.py:318
  161.8 4.3 %collective-permute-start.3 = (f32[128,128]{1,0:T(8,128)S(1)}, f32[128,128]{1,0:T(8,128)S(1)}, u32[]{:S(2)}, u32[]{:S(2)}) collective-permute-start(f32[128,128]{1,0:T(8,128)S(1)} %add.22), channel_id=1, source_target_pairs={{0,4},{2,6},{4,0},{6,2},{8,12},{10,14},{12,8},{14,10},{16,20},{18,... | collective-permute-start | bytes 196616 | tf_op jit(solution)/shard_map/ppermute | solution.py:318
  166.1 4.3 %collective-permute-start.4 = (f32[128,128]{1,0:T(8,128)S(1)}, f32[128,128]{1,0:T(8,128)S(1)}, u32[]{:S(2)}, u32[]{:S(2)}) collective-permute-start(f32[128,128]{1,0:T(8,128)S(1)} %add.23), channel_id=1, source_target_pairs={{0,1},{1,0},{2,3},{3,2},{4,5},{5,4},{6,7},{7,6},{8,9},{9,8},{10,11... | collective-permute-start | bytes 196616 | tf_op jit(solution)/shard_map/ppermute | solution.py:318
  170.4 1.3 copy-start.6
  170.5 1.3 collective-permute-start.5
  171.8 0.6 copy-start.7

commit v4 on v3

--- a/solution.py
+++ b/solution.py
@@ -116,7 +116,7 @@
     return jnp.concatenate([ref[i, at, :] for i in range(ref.shape[0])], axis=1)
 
 
-def before_kernel(own, pair_ref, wl, wlg, wr, wrg, out_ref, w_ref, rows_ref):
+def before_kernel(own, pair_ref, wl, wlg, wr, wrg, out_ref, normed_ref, w_ref, rows_ref):
     stack_weights((wl, wlg, wr, wrg), w_ref)
     h = wl.shape[0]
     rows = pair_ref.shape[0]
@@ -124,6 +124,7 @@
 
     def one_row(r, carry):
         normed = layer_norm(pair_ref[r])[0].astype(BF16)
+        normed_ref[r] = normed
         q_left, s_left, q_right, s_right = project(w_ref, normed)
         put_lanes(rows_ref, pl.ds(r, h, stride=pitch), s_left * q_left)
         put_lanes(rows_ref, pl.ds(r + h * pitch, h, stride=pitch), s_right * q_right)
@@ -152,15 +153,23 @@
                 out_ref[a * cols + b, i] = d[a * r : (a + 1) * r, b * c : (b + 1) * c]
 
 
-def gates_kernel(own, bit_ref, pair_ref, d_ref, wl, wlg, wr, wrg, grads_ref, kept_ref, sent_ref, w_ref, sums_ref, rows_ref):
-    stack_weights((wl, wlg, wr, wrg), w_ref)
+def gates_kernel(own, bit_ref, normed_hbm, d_ref, wl, wlg, wr, wrg, grads_ref, kept_ref, sent_ref, *scratch):
+    w_ref, sums_ref, rows_ref, normed_ref, sems = scratch
     h = wl.shape[0]
-    rows = pair_ref.shape[0]
+    rows = grads_ref.shape[0]
     pitch = rows + 1
-
-    @pl.when(pl.program_id(0) == 0)
+    step = pl.program_id(0)
+
+    def copy(block):
+        at = pl.ds(block * rows, rows)
+        return pltpu.make_async_copy(normed_hbm.at[at], normed_ref.at[at], sems.at[block])
+
+    @pl.when(step == 0)
     def _():
+        for block in range(normed_ref.shape[0] // rows):
+            copy(block).start()
         sums_ref[...] = jnp.zeros_like(sums_ref)
+        stack_weights((wl, wlg, wr, wrg), w_ref)
 
     for channel in range(h):
         to, slot = channel // own, (channel % own) * 2
@@ -168,8 +177,10 @@
             line = d_ref[to, slot + side].astype(F32)
             put_lanes(rows_ref, pl.ds((side * h + channel) * pitch, rows), line)
 
+    copy(step).wait()
+
     def one_row(r, carry):
-        normed = layer_norm(pair_ref[r])[0].astype(BF16)
+        normed = normed_ref[step * rows + r]
         q_left, s_left, q_right, s_right = project(w_ref, normed)
         e_left = get_lanes(rows_ref, pl.ds(r, h, stride=pitch)) * s_left
         e_right = get_lanes(rows_ref, pl.ds(r + h * pitch, h, stride=pitch)) * s_right
@@ -182,18 +193,22 @@
 
     lax.fori_loop(0, rows, one_row, 0, unroll=4)
 
-    @pl.when(pl.program_id(0) == pl.num_programs(0) - 1)
+    @pl.when(step == pl.num_programs(0) - 1)
     def _():
         bit = bit_ref[0]
         kept_ref[...] = sums_ref[pl.ds(pl.multiple_of(bit * 2 * h, 2 * h), 2 * h), :]
         sent_ref[...] = sums_ref[pl.ds(pl.multiple_of((1 - bit) * 2 * h, 2 * h), 2 * h), :]
 
 
-def input_kernel(pair_ref, grads_ref, wl, wlg, wr, wrg, *refs):
-    out_ref, back_ref = refs[-2:]
+def input_kernel(start, pair_hbm, grads_ref, wl, wlg, wr, wrg, *refs):
+    out_ref, back_ref, pair_ref, sem = refs[-4:]
+    copy = pltpu.make_async_copy(pair_hbm.at[pl.ds(start, pair_ref.shape[0])], pair_ref, sem)
+    copy.start()
     h = wl.shape[0]
     for i, ref in enumerate((wl, wlg, wr, wrg)):
         back_ref[:, pl.ds(i * h, h)] = ref[...].T
+
+    copy.wait()
 
     def one_row(r, carry):
         standardized, inverse_scale = layer_norm(pair_ref[r])
@@ -222,7 +237,7 @@
     dim = pair.shape[2]
     own = hidden // devices
     block = 16 if r % 16 == 0 else r
-    pieces = 4 if r % 4 == 0 else 1
+    pieces = 2 if r % 2 == 0 else 1
     weights = [w.T for w in weights]
     whole = pl.BlockSpec((hidden, dim), lambda i: (0, 0))
     tile = pl.BlockSpec((block, c, dim), lambda i: (i, 0, 0))
@@ -244,12 +259,16 @@
     lr_shape = jax.ShapeDtypeStruct((devices, 2 * own, r, c), BF16)
     by_hidden = pl.BlockSpec((block, 4 * hidden, c), lambda i: (i, 0, 0))
     g_all = exchange(cotangent.reshape(devices, own, r, c))
-    sent = pl.pallas_call(
+    normed_shape = jax.ShapeDtypeStruct((r, dim, c), BF16)
+    sent, normed = pl.pallas_call(
         functools.partial(before_kernel, own),
         grid=(r // block,),
         in_specs=[tile] + [whole] * 4,
-        out_specs=pl.BlockSpec((devices, 2 * own, block, c), lambda i: (0, 0, i, 0)),
-        out_shape=lr_shape,
+        out_specs=[
+            pl.BlockSpec((devices, 2 * own, block, c), lambda i: (0, 0, i, 0)),
+            pl.BlockSpec((block, dim, c), lambda i: (i, 0, 0)),
+        ],
+        out_shape=[lr_shape, normed_shape],
         scratch_shapes=[stacked, rows_scratch],
         compiler_params=memory(60),
         cost_estimate=cost(8 * hidden * dim * columns, pair, lr_shape),
@@ -280,45 +299,58 @@
         grid=(r // block,),
         in_specs=[
             smem,
-            tile,
+            pl.BlockSpec(memory_space=pltpu.HBM),
             pl.BlockSpec((devices, 2 * own, block, c), lambda i: (0, 0, i, 0)),
         ]
         + [whole] * 4,
         out_specs=[by_hidden, half, half],
         out_shape=[jax.ShapeDtypeStruct((r, 4 * hidden, c), BF16), half_shape, half_shape],
-        scratch_shapes=[stacked, pltpu.VMEM((4 * hidden, dim), F32), rows_scratch],
+        scratch_shapes=[
+            stacked,
+            pltpu.VMEM((4 * hidden, dim), F32),
+            rows_scratch,
+            pltpu.VMEM(normed_shape.shape, BF16),
+            pltpu.SemaphoreType.DMA((r // block,)),
+        ],
         compiler_params=memory(28),
         name="gates",
-    )(bit, pair, exchange(sent), *weights)
+    )(bit, pltpu.with_memory_space_constraint(normed, pltpu.HBM), exchange(sent), *weights)
 
     def input_piece(piece, pair_gradient):
         held = [] if pair_gradient is None else [pair_gradient]
         at = pl.BlockSpec((r // pieces, c, dim), lambda i: (piece, 0, 0))
         return pl.pallas_call(
-            input_kernel,
+            functools.partial(input_kernel, piece * r // pieces),
             grid=(1,),
-            in_specs=[at, pl.BlockSpec((r // pieces, 4 * hidden, c), lambda i: (piece, 0, 0))]
+            in_specs=[
+                pl.BlockSpec(memory_space=pltpu.HBM),
+                pl.BlockSpec((r // pieces, 4 * hidden, c), lambda i: (piece, 0, 0)),
+            ]
             + [whole] * 4
             + [pl.BlockSpec(memory_space=pl.ANY)] * len(held),
             out_specs=at,
             out_shape=jax.ShapeDtypeStruct(pair.shape, BF16),
-            scratch_shapes=[pltpu.VMEM((dim, 4 * hidden), BF16)],
+            scratch_shapes=[
+                pltpu.VMEM((dim, 4 * hidden), BF16),
+                pltpu.VMEM((r // pieces, c, dim), BF16),
+                pltpu.SemaphoreType.DMA,
+            ],
             input_output_aliases={6: 0} if held else {},
             compiler_params=memory(16),
             cost_estimate=cost(8 * hidden * dim * columns // pieces, pair),
             name="input",
-        )(pair, grads, *weights, *held)
+        )(pltpu.with_memory_space_constraint(pair, pltpu.HBM), grads, *weights, *held)
 
     steps = [("row", rows, 1 << i) for i in range(1, rows.bit_length() - 1)][::-1]
     steps += [("col", cols, 1 << i) for i in range(cols.bit_length() - 1)]
+    pieces = min(pieces, len(steps))
     neighbours = [(i, i ^ 1) for i in range(rows)]
     pair_gradient = None
     mine = kept + lax.ppermute(given, "row", neighbours)
     for n, (axis, size, step) in enumerate(steps):
         other = lax.ppermute(mine, axis, [(i, i ^ step) for i in range(size)])
-        for piece in range(n * pieces // len(steps), (n + 1) * pieces // len(steps)):
-            pair_gradient = input_piece(piece, pair_gradient)
-        if pair_gradient is not None:
+        if n < pieces:
+            pair_gradient = input_piece(n, pair_gradient)
             other, pair_gradient = lax.optimization_barrier((other, pair_gradient))
         mine = mine + other
     weight_grads = pl.pallas_call(

time: 174 us -> 173 us (level)
    pallas_call x4 -> x2, Pallas kernels: 7.74 us -> 8.21 us  [input_piece(): pl.pallas_call(functools.partial(input_kernel, piece * r // pieces), grid...]
  transfers between devices with their start and end apart: 8 -> 8, of which waited for: 8 -> 8; matrix products, arithmetic and copies ran while one was open for 0% -> 0% of each run, Pallas kernels for 8% -> 9%
where the time goes in v4:
time: 173 us; the launch traced here: 172 us
  waiting for transfers between devices  77.9 us (45%)
  blocking collectives  52.3 us (30%)
  Pallas kernels  24.5 us (14%)
  starting transfers between devices  15 us (9%)
  local copies, waits for them, and re-layouts  1.95 us (1%)
    all_to_all x1, blocking collectives, channel_shards(): exchange(sent)  52.3 us
    all_to_all x1, waiting for transfers between devices, channel_shards(): exchange(sent)  48.7 us
    all_to_all x1, waiting for transfers between devices, channel_shards(): g_all = exchange(cotangent.reshape(devices, own, r, c))  19.3 us
    pallas_call x2, Pallas kernels, input_piece(): pl.pallas_call(functools.partial(input_kernel, piece * r // pieces), grid...  8.21 us
    ppermute x4, waiting for transfers between devices, channel_shards(): other = lax.ppermute(mine, axis, [(i, i ^ step) for i in range(size)])  7.44 us
    all_to_all x1, starting transfers between devices, channel_shards(): g_all = exchange(cotangent.reshape(devices, own, r, c))  7.3 us
    pallas_call x1, Pallas kernels, channel_shards(): pl.pallas_call(functools.partial(before_kernel, own), grid=(r // block,),...  6.92 us
    pallas_call x1, Pallas kernels, channel_shards(): pl.pallas_call(functools.partial(gates_kernel, own), grid=(r // block,),...  6.01 us
  transfers between devices with their start and end apart: 8, of which 8 were waited for; matrix products, arithmetic and copies ran while one was open for 0% of the time, Pallas kernels for 9%

profile of v4, /device:TPU:0, one launch (start us, length us, event | category | flops | bytes accessed | tf_op | source)
XLA Modules:
  0.0 172.5 jit_solution(5308741451453431107)
XLA Ops:
  0.6 7.3 %all-to-all-start = ((bf16[32,2,32,256]{3,2,1,0:T(8,128)(2,1)}), bf16[32,2,32,256]{3,2,1,0:T(8,128)(2,1)S(1)}, u32[]{:S(2)}, u32[]{:S(2)}) async-start(bf16[32,2,32,256]{3,2,1,0:T(8,128)(2,1)} %bitcast.26), calls=%async_computation | async-start | bytes 2097152 | tf_op jit(solution)/shard_map/all_to_all | solution.py:261
  7.9 6.9 %before.1 = (bf16[32,4,32,256]{3,2,1,0:T(8,128)(2,1)}, bf16[32,128,256]{2,1,0:T(8,128)(2,1)}) custom-call(bf16[32,256,128]{2,1,0:T(8,128)(2,1)} %pair_hbm.3, bf16[64,128]{1,0:T(8,128)(2,1)} %bitcast.10, bf16[64,128]{1,0:T(8,128)(2,1)} %bitcast.14, bf16[64,128]{1,0:T(8,128)(2,1)} %bitcast.18, bf16[64,128]{1,0:T(8,128)(2,1)} %bitcast.22), custom_call_target="tpu_custom_call" | custom-call | flops 536870912 | bytes 4194304 | tf_op jit(solution)/shard_map/before/pallas_call | solution.py:263
  14.9 19.3 %all-to-all-done.cot_ref = bf16[32,2,32,256]{3,2,1,0:T(8,128)(2,1)S(1)} async-done(((bf16[32,2,32,256]{3,2,1,0:T(8,128)(2,1)}), bf16[32,2,32,256]{3,2,1,0:T(8,128)(2,1)S(1)}, u32[]{:S(2)}, u32[]{:S(2)}) %all-to-all-start) | async-done | bytes 1048608 | tf_op jit(solution)/shard_map/all_to_all | solution.py:261
  34.2 52.3 %all_to_all.15.in_ref = bf16[32,4,32,256]{3,2,1,0:T(8,128)(2,1)S(1)} all-to-all(bf16[32,4,32,256]{3,2,1,0:T(8,128)(2,1)} %get-tuple-element.19), channel_id=1, replica_groups=mesh['row'=16,'col'=2] {'row','col'}, dimensions={0} | all-to-all | bytes 4194304 | tf_op jit(solution)/shard_map/all_to_all | solution.py:291
  86.5 1.8 %triangle.1 = bf16[32,4,32,256]{3,2,1,0:T(8,128)(2,1)S(1)} custom-call(bf16[32,2,32,256]{3,2,1,0:T(8,128)(2,1)S(1)} %all-to-all-done.cot_ref, bf16[32,4,32,256]{3,2,1,0:T(8,128)(2,1)S(1)} %all_to_all.15.in_ref), custom_call_target="tpu_custom_call" | custom-call | tf_op jit(solution)/shard_map/triangle/pallas_call | solution.py:279
  88.3 0.0 copy-start
  88.3 1.3 copy-done
  89.6 0.0 copy-start.1
  89.6 0.0 copy-start.2
  89.6 0.0 copy-start.3
  89.6 0.0 copy-start.4
  89.6 3.7 %all-to-all-start.2 = ((bf16[32,4,32,256]{3,2,1,0:T(8,128)(2,1)}), bf16[32,4,32,256]{3,2,1,0:T(8,128)(2,1)S(1)}, u32[]{:S(2)}, u32[]{:S(2)}) async-start(bf16[32,4,32,256]{3,2,1,0:T(8,128)(2,1)} %copy-done), calls=%async_computation.2 | async-start | bytes 4194304 | tf_op jit(solution)/shard_map/all_to_all | solution.py:317
  93.3 48.7 %all-to-all-done.2.d_ref = bf16[32,4,32,256]{3,2,1,0:T(8,128)(2,1)S(1)} async-done(((bf16[32,4,32,256]{3,2,1,0:T(8,128)(2,1)}), bf16[32,4,32,256]{3,2,1,0:T(8,128)(2,1)S(1)}, u32[]{:S(2)}, u32[]{:S(2)}) %all-to-all-start.2) | async-done | bytes 2097184 | tf_op jit(solution)/shard_map/all_to_all | solution.py:317
  142.0 0.0 copy-done.1
  142.1 0.0 copy-done.2
  142.1 0.0 copy-done.3
  142.1 0.0 copy-done.4
  142.1 6.0 %gates.1 = (bf16[32,256,256]{2,1,0:T(8,128)(2,1)S(1)}, f32[128,128]{1,0:T(8,128)S(1)}, f32[128,128]{1,0:T(8,128)S(1)}) custom-call(s32[1]{0:T(128)} %bitcast.bit_ref, bf16[32,128,256]{2,1,0:T(8,128)(2,1)} %get-tuple-element.18.normed_hbm, bf16[32,4,32,256]{3,2,1,0:T(8,128)(2,1)S(1)} %all-to-all-done.2.d_ref, bf16[64,128]{1,0:T(8,128)(2,1)S(1)} %bitcast.11, ...), custom_call_target="tpu_custom_call" | custom-call | tf_op jit(solution)/shard_map/gates/pallas_call | solution.py:297
  148.1 0.1 collective-permute-start
  148.2 1.2 collective-permute-done
  149.4 1.1 collective-permute-start.1
  150.5 4.1 %input.2.refs_0_ = bf16[32,256,128]{2,1,0:T(8,128)(2,1)} custom-call(bf16[32,256,128]{2,1,0:T(8,128)(2,1)} %pair_hbm.3, bf16[32,256,256]{2,1,0:T(8,128)(2,1)S(1)} %get-tuple-element.22.grads_ref, bf16[64,128]{1,0:T(8,128)(2,1)S(1)} %bitcast.12, bf16[64,128]{1,0:T(8,128)(2,1)S(1)} %bitcast.16, bf16[64,128]{1,0:T(8,128)(2,1)S(1)} %bitcast.20, ...), custom_call_target="tpu_custom_call" | custom-call | flops 268435456 | bytes 2097152 | tf_op jit(solution)/shard_map/input/pallas_call | solution.py:322
  154.6 1.3 collective-permute-done.1
  156.0 0.1 collective-permute-start.2
  156.0 4.1 %input.3 = bf16[32,256,128]{2,1,0:T(8,128)(2,1)} custom-call(bf16[32,256,128]{2,1,0:T(8,128)(2,1)} %pair_hbm.3, bf16[32,256,256]{2,1,0:T(8,128)(2,1)S(1)} %get-tuple-element.22.grads_ref, bf16[64,128]{1,0:T(8,128)(2,1)S(1)} %bitcast.13, bf16[64,128]{1,0:T(8,128)(2,1)S(1)} %bitcast.17, bf16[64,128]{1,0:T(8,128)(2,1)S(1)} %bitcast.21, ...), custom_call_target="tpu_custom_call", output_to_operand_aliasing={{}: (6, {})} | custom-call | flops 268435456 | bytes 2097152 | tf_op jit(solution)/shard_map/input/pallas_call | solution.py:322
  160.2 0.1 collective-permute-done.2
  160.3 1.2 collective-permute-start.3
  161.5 3.1 %collective-permute-done.3 = f32[128,128]{1,0:T(8,128)S(1)} collective-permute-done((f32[128,128]{1,0:T(8,128)S(1)}, f32[128,128]{1,0:T(8,128)S(1)}, u32[]{:S(2)}, u32[]{:S(2)}) %collective-permute-start.3) | collective-permute-done | bytes 65568 | tf_op jit(solution)/shard_map/ppermute | solution.py:351
  164.6 1.5 collective-permute-start.4
  166.1 2.9 %collective-permute-done.4 = f32[128,128]{1,0:T(8,128)S(1)} collective-permute-done((f32[128,128]{1,0:T(8,128)S(1)}, f32[128,128]{1,0:T(8,128)S(1)}, u32[]{:S(2)}, u32[]{:S(2)}) %collective-permute-start.4) | collective-permute-done | bytes 65568 | tf_op jit(solution)/shard_map/ppermute | solution.py:351
  169.0 0.0 copy-start.5
  169.0 0.1 collective-permute-start.5
  169.1 1.2 collective-permute-done.5.other_ref
  170.3 0.0 copy-done.5
  170.3 0.0 copy-start.6
  170.3 0.6 copy-done.6
  170.9 1.5 finish.1
  (5 shorter events, 0.0 us)
Async XLA Ops:
  0.6 33.5 %all-to-all-start = ((bf16[32,2,32,256]{3,2,1,0:T(8,128)(2,1)}), bf16[32,2,32,256]{3,2,1,0:T(8,128)(2,1)S(1)}, u32[]{:S(2)}, u32[]{:S(2)}) async-start(bf16[32,2,32,256]{3,2,1,0:T(8,128)(2,1)} %bitcast.26), calls=%async_computation | async-start | bytes 2097152 | tf_op jit(solution)/shard_map/all_to_all | solution.py:261
  88.3 1.3 copy-start
  89.6 52.4 %copy-start.1 = (bf16[128,64]{0,1:T(8,128)(2,1)S(1)}, bf16[128,64]{0,1:T(8,128)(2,1)}, u32[]{:S(2)}) copy-start(bf16[128,64]{0,1:T(8,128)(2,1)} %param.8) | copy-start | bytes 49156
  89.6 52.4 %copy-start.2 = (bf16[128,64]{0,1:T(8,128)(2,1)S(1)}, bf16[128,64]{0,1:T(8,128)(2,1)}, u32[]{:S(2)}) copy-start(bf16[128,64]{0,1:T(8,128)(2,1)} %param.9) | copy-start | bytes 49156
  89.6 52.4 %copy-start.3 = (bf16[128,64]{0,1:T(8,128)(2,1)S(1)}, bf16[128,64]{0,1:T(8,128)(2,1)}, u32[]{:S(2)}) copy-start(bf16[128,64]{0,1:T(8,128)(2,1)} %param.10) | copy-start | bytes 49156
  89.6 52.4 %copy-start.4 = (bf16[128,64]{0,1:T(8,128)(2,1)S(1)}, bf16[128,64]{0,1:T(8,128)(2,1)}, u32[]{:S(2)}) copy-start(bf16[128,64]{0,1:T(8,128)(2,1)} %param.11) | copy-start | bytes 49156
  89.6 52.4 %all-to-all-start.2 = ((bf16[32,4,32,256]{3,2,1,0:T(8,128)(2,1)}), bf16[32,4,32,256]{3,2,1,0:T(8,128)(2,1)S(1)}, u32[]{:S(2)}, u32[]{:S(2)}) async-start(bf16[32,4,32,256]{3,2,1,0:T(8,128)(2,1)} %copy-done), calls=%async_computation.2 | async-start | bytes 4194304 | tf_op jit(solution)/shard_map/all_to_all | solution.py:317
  148.1 1.3 collective-permute-start
  149.4 6.5 %collective-permute-start.1 = (f32[128,128]{1,0:T(8,128)S(1)}, f32[128,128]{1,0:T(8,128)S(1)}, u32[]{:S(2)}, u32[]{:S(2)}) collective-permute-start(f32[128,128]{1,0:T(8,128)S(1)} %add.20), channel_id=1, source_target_pairs={{0,16},{2,18},{4,20},{6,22},{8,24},{10,26},{12,28},{14,30},{16,0},... | collective-permute-start | bytes 196616 | tf_op jit(solution)/shard_map/ppermute | solution.py:351
  156.0 4.3 %collective-permute-start.2 = (f32[128,128]{1,0:T(8,128)S(1)}, f32[128,128]{1,0:T(8,128)S(1)}, u32[]{:S(2)}, u32[]{:S(2)}) collective-permute-start(f32[128,128]{1,0:T(8,128)S(1)} %add.21), channel_id=1, source_target_pairs={{0,8},{2,10},{4,12},{6,14},{8,0},{10,2},{12,4},{14,6},{16,24},{18,... | collective-permute-start | bytes 196616 | tf_op jit(solution)/shard_map/ppermute | solution.py:351
  160.3 4.3 %collective-permute-start.3 = (f32[128,128]{1,0:T(8,128)S(1)}, f32[128,128]{1,0:T(8,128)S(1)}, u32[]{:S(2)}, u32[]{:S(2)}) collective-permute-start(f32[128,128]{1,0:T(8,128)S(1)} %add.22), channel_id=1, source_target_pairs={{0,4},{2,6},{4,0},{6,2},{8,12},{10,14},{12,8},{14,10},{16,20},{18,... | collective-permute-start | bytes 196616 | tf_op jit(solution)/shard_map/ppermute | solution.py:351
  164.6 4.3 %collective-permute-start.4 = (f32[128,128]{1,0:T(8,128)S(1)}, f32[128,128]{1,0:T(8,128)S(1)}, u32[]{:S(2)}, u32[]{:S(2)}) collective-permute-start(f32[128,128]{1,0:T(8,128)S(1)} %add.23), channel_id=1, source_target_pairs={{0,1},{1,0},{2,3},{3,2},{4,5},{5,4},{6,7},{7,6},{8,9},{9,8},{10,11... | collective-permute-start | bytes 196616 | tf_op jit(solution)/shard_map/ppermute | solution.py:351
  169.0 1.3 copy-start.5
  169.0 1.3 collective-permute-start.5
  170.3 0.6 copy-start.6

commit v5 on v4

--- a/solution.py
+++ b/solution.py
@@ -220,6 +220,18 @@
         return carry
 
     lax.fori_loop(0, pair_ref.shape[0], one_row, 0, unroll=4)
+
+
+def quarters_kernel(quarter, place_ref, a_ref, b_ref, *out_refs):
+    for m, out_ref in enumerate(out_refs):
+        at = pl.ds(pl.multiple_of((place_ref[0] ^ m) * quarter, quarter), quarter)
+        out_ref[...] = a_ref[at, :] + b_ref[at, :]
+
+
+def half_kernel(quarter, place_ref, *refs):
+    for m, ref in enumerate(refs[:4]):
+        at = pl.ds(pl.multiple_of((place_ref[0] ^ m) * quarter, quarter), quarter)
+        refs[4][at, :] = ref[...]
 
 
 def finish_kernel(scale, bit_ref, mine_ref, other_ref, *out_refs):
@@ -284,13 +296,16 @@
             pl.BlockSpec((devices, 2, r, c), lambda i: (0, i, 0, 0)),
         ],
         out_specs=pl.BlockSpec((devices, 2, r, c), lambda i: (0, i, 0, 0)),
-        out_shape=lr_shape,
+        out_shape=pltpu.HBM(lr_shape.shape, BF16),
         scratch_shapes=[pltpu.VMEM((n_i, n_k), BF16)] * 3,
         compiler_params=memory(32),
         name="triangle",
     )(g_all, exchange(sent))
 
-    bit = (lax.axis_index("row") % 2).astype(jnp.int32).reshape(1)
+    row, col = (lax.axis_index(axis).astype(jnp.int32) for axis in ("row", "col"))
+    bit = (row % 2).reshape(1)
+    place = (row // 2 % 2 * 2 + col % 2).reshape(1)
+    vmem = pl.BlockSpec(memory_space=pltpu.VMEM)
     smem = pl.BlockSpec(memory_space=pltpu.SMEM)
     half_shape = jax.ShapeDtypeStruct((2 * hidden, dim), F32)
     half = pl.BlockSpec(half_shape.shape, lambda i: (0, 0))
@@ -341,24 +356,62 @@
             name="input",
         )(pltpu.with_memory_space_constraint(pair, pltpu.HBM), grads, *weights, *held)
 
-    steps = [("row", rows, 1 << i) for i in range(1, rows.bit_length() - 1)][::-1]
-    steps += [("col", cols, 1 << i) for i in range(cols.bit_length() - 1)]
-    pieces = min(pieces, len(steps))
-    neighbours = [(i, i ^ 1) for i in range(rows)]
-    pair_gradient = None
-    mine = kept + lax.ppermute(given, "row", neighbours)
-    for n, (axis, size, step) in enumerate(steps):
-        other = lax.ppermute(mine, axis, [(i, i ^ step) for i in range(size)])
-        if n < pieces:
-            pair_gradient = input_piece(n, pair_gradient)
-            other, pair_gradient = lax.optimization_barrier((other, pair_gradient))
-        mine = mine + other
+    pair_gradient, piece = None, 0
+
+    def beside(values):
+        nonlocal pair_gradient, piece
+        if piece < pieces:
+            pair_gradient = input_piece(piece, pair_gradient)
+            piece += 1
+            *values, pair_gradient = lax.optimization_barrier((*values, pair_gradient))
+        return values
+
+    def swap(value, axis, size, step):
+        return lax.ppermute(value, axis, [(i, i ^ step) for i in range(size)])
+
+    def swap_quarter(value, m):
+        size = rows * cols
+        far = ((m >> 1) * 2 * cols) ^ (m & 1)
+        return lax.ppermute(value, ("row", "col"), [(i, i ^ far) for i in range(size)])
+
+    quarter = 2 * hidden // 4
+    quarters = pl.pallas_call(
+        functools.partial(quarters_kernel, quarter),
+        in_specs=[smem, vmem, vmem],
+        out_specs=[vmem] * 4,
+        out_shape=[jax.ShapeDtypeStruct((quarter, dim), F32)] * 4,
+        compiler_params=memory(8),
+        name="quarters",
+    )(place, kept, swap(given, "row", rows, 1))
+    got = beside([swap_quarter(quarters[m], m) for m in range(1, 4)])
+    mine = (quarters[0] + got[0]) + (got[1] + got[2])
+    step = 4
+    while step < rows:
+        if 2 * step < rows:
+            got = [swap(mine, "row", rows, m * step) for m in range(1, 4)]
+            got = beside(got)
+            mine = (mine + got[0]) + (got[1] + got[2])
+        else:
+            mine = mine + beside([swap(mine, "row", rows, step)])[0]
+        step *= 4
+    got = beside([swap_quarter(mine, m) for m in range(1, 4)])
+    while piece < pieces:
+        got = beside(got)
+    mine = pl.pallas_call(
+        functools.partial(half_kernel, quarter),
+        in_specs=[smem] + [vmem] * 4,
+        out_specs=vmem,
+        out_shape=half_shape,
+        compiler_params=memory(8),
+        name="half",
+    )(place, mine, *got)
     weight_grads = pl.pallas_call(
         functools.partial(finish_kernel, 1.0 / n_i),
-        in_specs=[smem, pl.BlockSpec(memory_space=pltpu.VMEM), pl.BlockSpec(memory_space=pltpu.VMEM)],
+        in_specs=[smem, vmem, vmem],
         out_shape=[jax.ShapeDtypeStruct((hidden, dim), F32)] * 4,
+        compiler_params=memory(8),
         name="finish",
-    )(bit, mine, lax.ppermute(mine, "row", neighbours))
+    )(bit, mine, swap(mine, "row", rows, 1))
     return (pair_gradient, *(g.T for g in weight_grads))
 
 
@@ -368,7 +421,7 @@
     sizes = (mesh.shape["row"], mesh.shape["col"])
 
     def shards(pair, cotangent, *weights):
-        plain = all(size > 1 and size & (size - 1) == 0 for size in sizes)
+        plain = sizes[0] >= 4 and sizes[1] == 2 and sizes[0] & (sizes[0] - 1) == 0
         if plain and cotangent.shape[0] % (sizes[0] * sizes[1]) == 0:
             return channel_shards(sizes, pair, cotangent, *weights)
         return gathered_shards(pair, cotangent, *weights)

time: 173 us -> 179 us (1.035)
  starting transfers between devices: 15 us -> 22.6 us
  waiting for transfers between devices: 77.9 us -> 73.8 us
  local copies, waits for them, and re-layouts: 1.95 us -> 4.14 us
    ppermute x6 -> x11, starting transfers between devices: 3.99 us -> 11.6 us  [the longest x6 7.11 us: swap_quarter(): lax.ppermute(value, ('row', 'col'), [(i, i ^ far) for i in range(size)])]
    ppermute x6 -> x11, waiting for transfers between devices: 9.92 us -> 5.79 us  [the longest x6 3.29 us: swap_quarter(): lax.ppermute(value, ('row', 'col'), [(i, i ^ far) for i in range(size)])]
    unnamed x14 -> x12, local copies, waits for them, and re-layouts: 1.95 us -> 4.14 us
  transfers between devices with their start and end apart: 8 -> 13, of which waited for: 8 -> 7; matrix products, arithmetic and copies ran while one was open for 0% -> 0% of each run, Pallas kernels for 9% -> 8%
where the time goes in v5:
time: 179 us; the launch traced here: 178 us
  waiting for transfers between devices  73.8 us (41%)
  blocking collectives  52.3 us (29%)
  Pallas kernels  24.4 us (14%)
  starting transfers between devices  22.6 us (13%)
  local copies, waits for them, and re-layouts  4.14 us (2%)
    all_to_all x1, blocking collectives, channel_shards(): exchange(sent)  52.3 us
    all_to_all x1, waiting for transfers between devices, channel_shards(): exchange(sent)  48.7 us
    all_to_all x1, waiting for transfers between devices, channel_shards(): g_all = exchange(cotangent.reshape(devices, own, r, c))  19.3 us
    pallas_call x2, Pallas kernels, input_piece(): pl.pallas_call(functools.partial(input_kernel, piece * r // pieces), grid...  8.2 us
    all_to_all x1, starting transfers between devices, channel_shards(): g_all = exchange(cotangent.reshape(devices, own, r, c))  7.3 us
    ppermute x6, starting transfers between devices, swap_quarter(): lax.ppermute(value, ('row', 'col'), [(i, i ^ far) for i in range(size)])  7.11 us
    pallas_call x1, Pallas kernels, channel_shards(): pl.pallas_call(functools.partial(before_kernel, own), grid=(r // block,),...  6.91 us
    pallas_call x1, Pallas kernels, channel_shards(): pl.pallas_call(functools.partial(gates_kernel, own), grid=(r // block,),...  6.02 us
  transfers between devices with their start and end apart: 13, of which 7 were waited for; matrix products, arithmetic and copies ran while one was open for 0% of the time, Pallas kernels for 8%

profile of v5, /device:TPU:0, one launch (start us, length us, event | category | flops | bytes accessed | tf_op | source)
XLA Modules:
  0.0 178.2 jit_solution(14716749966518994714)
XLA Ops:
  0.6 7.3 %all-to-all-start = ((bf16[32,2,32,256]{3,2,1,0:T(8,128)(2,1)}), bf16[32,2,32,256]{3,2,1,0:T(8,128)(2,1)S(1)}, u32[]{:S(2)}, u32[]{:S(2)}) async-start(bf16[32,2,32,256]{3,2,1,0:T(8,128)(2,1)} %bitcast.27), calls=%async_computation | async-start | bytes 2097152 | tf_op jit(solution)/shard_map/all_to_all | solution.py:273
  7.9 6.9 %before.1 = (bf16[32,4,32,256]{3,2,1,0:T(8,128)(2,1)}, bf16[32,128,256]{2,1,0:T(8,128)(2,1)}) custom-call(bf16[32,256,128]{2,1,0:T(8,128)(2,1)} %pair_hbm.3, bf16[64,128]{1,0:T(8,128)(2,1)} %bitcast.11, bf16[64,128]{1,0:T(8,128)(2,1)} %bitcast.15, bf16[64,128]{1,0:T(8,128)(2,1)} %bitcast.19, bf16[64,128]{1,0:T(8,128)(2,1)} %bitcast.23), custom_call_target="tpu_custom_call" | custom-call | flops 536870912 | bytes 4194304 | tf_op jit(solution)/shard_map/before/pallas_call | solution.py:275
  14.9 19.3 %all-to-all-done.cot_ref = bf16[32,2,32,256]{3,2,1,0:T(8,128)(2,1)S(1)} async-done(((bf16[32,2,32,256]{3,2,1,0:T(8,128)(2,1)}), bf16[32,2,32,256]{3,2,1,0:T(8,128)(2,1)S(1)}, u32[]{:S(2)}, u32[]{:S(2)}) %all-to-all-start) | async-done | bytes 1048608 | tf_op jit(solution)/shard_map/all_to_all | solution.py:273
  34.2 52.3 %all_to_all.15.in_ref = bf16[32,4,32,256]{3,2,1,0:T(8,128)(2,1)S(1)} all-to-all(bf16[32,4,32,256]{3,2,1,0:T(8,128)(2,1)} %get-tuple-element.27), channel_id=1, replica_groups=mesh['row'=16,'col'=2] {'row','col'}, dimensions={0} | all-to-all | bytes 4194304 | tf_op jit(solution)/shard_map/all_to_all | solution.py:303
  86.5 2.6 %triangle.1 = bf16[32,4,32,256]{3,2,1,0:T(8,128)(2,1)} custom-call(bf16[32,2,32,256]{3,2,1,0:T(8,128)(2,1)S(1)} %all-to-all-done.cot_ref, bf16[32,4,32,256]{3,2,1,0:T(8,128)(2,1)S(1)} %all_to_all.15.in_ref), custom_call_target="tpu_custom_call" | custom-call | tf_op jit(solution)/shard_map/triangle/pallas_call | solution.py:291
  89.2 0.0 copy-start.2
  89.2 0.0 copy-start.3
  89.2 0.0 copy-start.4
  89.2 0.0 copy-start.5
  89.2 3.7 %all-to-all-start.2 = ((bf16[32,4,32,256]{3,2,1,0:T(8,128)(2,1)}), bf16[32,4,32,256]{3,2,1,0:T(8,128)(2,1)S(1)}, u32[]{:S(2)}, u32[]{:S(2)}) async-start(bf16[32,4,32,256]{3,2,1,0:T(8,128)(2,1)} %triangle.1), calls=%async_computation.2 | async-start | bytes 4194304 | tf_op jit(solution)/shard_map/all_to_all | solution.py:332
  92.9 48.7 %all-to-all-done.2.d_ref = bf16[32,4,32,256]{3,2,1,0:T(8,128)(2,1)S(1)} async-done(((bf16[32,4,32,256]{3,2,1,0:T(8,128)(2,1)}), bf16[32,4,32,256]{3,2,1,0:T(8,128)(2,1)S(1)}, u32[]{:S(2)}, u32[]{:S(2)}) %all-to-all-start.2) | async-done | bytes 2097184 | tf_op jit(solution)/shard_map/all_to_all | solution.py:332
  141.6 0.0 copy-done.2
  141.6 0.0 copy-done.3
  141.6 0.0 copy-done.4
  141.6 0.0 copy-done.5
  141.6 6.0 %gates.1 = (bf16[32,256,256]{2,1,0:T(8,128)(2,1)S(1)}, f32[128,128]{1,0:T(8,128)S(1)}, f32[128,128]{1,0:T(8,128)S(1)}) custom-call(s32[1]{0:T(128)} %bitcast.1.bit_ref, bf16[32,128,256]{2,1,0:T(8,128)(2,1)} %get-tuple-element.26.normed_hbm, bf16[32,4,32,256]{3,2,1,0:T(8,128)(2,1)S(1)} %all-to-all-done.2.d_ref, bf16[64,128]{1,0:T(8,128)(2,1)S(1)} %bitcast.12, ...), custom_call_target="tpu_custom_call" | custom-call | tf_op jit(solution)/shard_map/gates/pallas_call | solution.py:312
  147.6 0.0 copy-start
  147.6 1.9 %copy-done = bf16[32,256,256]{2,1,0:T(8,128)(2,1)} copy-done((bf16[32,256,256]{2,1,0:T(8,128)(2,1)}, bf16[32,256,256]{2,1,0:T(8,128)(2,1)S(1)}, u32[]{:S(2)}) %copy-start) | copy-done | bytes 4194328
  149.6 0.0 collective-permute-start
  149.6 1.3 collective-permute-done.b_ref
  150.8 1.6 collective-permute-start.1
  152.5 1.4 collective-permute-start.2
  153.9 0.5 collective-permute-start.3
  154.4 0.0 copy-start.1
  154.4 2.2 %copy-done.1 = bf16[32,256,256]{2,1,0:T(8,128)(2,1)S(1)} copy-done((bf16[32,256,256]{2,1,0:T(8,128)(2,1)S(1)}, bf16[32,256,256]{2,1,0:T(8,128)(2,1)}, u32[]{:S(2)}) %copy-start.1) | copy-done | bytes 4194328
  156.6 4.1 %input.2.refs_0_ = bf16[32,256,128]{2,1,0:T(8,128)(2,1)} custom-call(bf16[32,256,128]{2,1,0:T(8,128)(2,1)} %pair_hbm.3, bf16[32,256,256]{2,1,0:T(8,128)(2,1)S(1)} %copy-done.1, bf16[64,128]{1,0:T(8,128)(2,1)S(1)} %bitcast.13, bf16[64,128]{1,0:T(8,128)(2,1)S(1)} %bitcast.17, bf16[64,128]{1,0:T(8,128)(2,1)S(1)} %bitcast.21, bf16[64,128]{1,0:T(8,128)(2,1)S(1)} %bitcast.25), custom_call_target="tpu_custom_call" | custom-call | flops 268435456 | bytes 2097152 | tf_op jit(solution)/shard_map/input/pallas_call | solution.py:337
  160.7 0.0 collective-permute-done.1
  160.7 0.0 collective-permute-done.2
  160.7 0.0 collective-permute-done.3
  160.7 1.3 collective-permute-start.6
  162.1 1.1 collective-permute-start.5
  163.2 2.0 %collective-permute-start.4 = (f32[32,128]{1,0:T(8,128)S(1)}, f32[32,128]{1,0:T(8,128)S(1)}, u32[]{:S(2)}, u32[]{:S(2)}) collective-permute-start(f32[32,128]{1,0:T(8,128)S(1)} %add_add_fusion.1), channel_id=1, source_target_pairs={{0,8},{2,10},{4,12},{6,14},{8,0},{10,2},{12,4},{14,6},{16,24},{18,... | collective-permute-start | bytes 49160 | tf_op jit(solution)/shard_map/ppermute | solution.py:370
  165.2 4.1 %input.3 = bf16[32,256,128]{2,1,0:T(8,128)(2,1)} custom-call(bf16[32,256,128]{2,1,0:T(8,128)(2,1)} %pair_hbm.3, bf16[32,256,256]{2,1,0:T(8,128)(2,1)S(1)} %copy-done.1, bf16[64,128]{1,0:T(8,128)(2,1)S(1)} %bitcast.14, bf16[64,128]{1,0:T(8,128)(2,1)S(1)} %bitcast.18, bf16[64,128]{1,0:T(8,128)(2,1)S(1)} %bitcast.22, ...), custom_call_target="tpu_custom_call", output_to_operand_aliasing={{}: (6, {})} | custom-call | flops 268435456 | bytes 2097152 | tf_op jit(solution)/shard_map/input/pallas_call | solution.py:337
  169.3 0.0 collective-permute-done.6
  169.3 0.0 collective-permute-done.5
  169.3 0.0 collective-permute-done.4
  169.3 2.5 %collective-permute-start.9 = (f32[32,128]{1,0:T(8,128)S(1)}, f32[32,128]{1,0:T(8,128)S(1)}, u32[]{:S(2)}, u32[]{:S(2)}) collective-permute-start(f32[32,128]{1,0:T(8,128)S(1)} %add_add_fusion.refs_0_), channel_id=1, source_target_pairs={{0,5},{1,4},{2,7},{3,6},{4,1},{5,0},{6,3},{7,2},{8,13},{9,12},{10,... | collective-permute-start | bytes 49160 | tf_op jit(solution)/shard_map/ppermute | solution.py:375
  171.8 0.6 collective-permute-start.8
  172.4 0.5 collective-permute-start.7
  172.9 1.1 collective-permute-done.9.refs_3_
  174.1 1.5 collective-permute-done.8.refs_2_
  175.6 0.6 collective-permute-done.7.refs_1_
  176.2 0.1 collective-permute-start.10
  176.3 1.2 collective-permute-done.10.other_ref
  177.5 0.7 finish.1
  (4 shorter events, 0.0 us)
Async XLA Ops:
  0.6 33.5 %all-to-all-start = ((bf16[32,2,32,256]{3,2,1,0:T(8,128)(2,1)}), bf16[32,2,32,256]{3,2,1,0:T(8,128)(2,1)S(1)}, u32[]{:S(2)}, u32[]{:S(2)}) async-start(bf16[32,2,32,256]{3,2,1,0:T(8,128)(2,1)} %bitcast.27), calls=%async_computation | async-start | bytes 2097152 | tf_op jit(solution)/shard_map/all_to_all | solution.py:273
  89.2 52.4 %copy-start.2 = (bf16[128,64]{0,1:T(8,128)(2,1)S(1)}, bf16[128,64]{0,1:T(8,128)(2,1)}, u32[]{:S(2)}) copy-start(bf16[128,64]{0,1:T(8,128)(2,1)} %param.8) | copy-start | bytes 49156
  89.2 52.4 %copy-start.3 = (bf16[128,64]{0,1:T(8,128)(2,1)S(1)}, bf16[128,64]{0,1:T(8,128)(2,1)}, u32[]{:S(2)}) copy-start(bf16[128,64]{0,1:T(8,128)(2,1)} %param.9) | copy-start | bytes 49156
  89.2 52.4 %copy-start.4 = (bf16[128,64]{0,1:T(8,128)(2,1)S(1)}, bf16[128,64]{0,1:T(8,128)(2,1)}, u32[]{:S(2)}) copy-start(bf16[128,64]{0,1:T(8,128)(2,1)} %param.10) | copy-start | bytes 49156
  89.2 52.4 %copy-start.5 = (bf16[128,64]{0,1:T(8,128)(2,1)S(1)}, bf16[128,64]{0,1:T(8,128)(2,1)}, u32[]{:S(2)}) copy-start(bf16[128,64]{0,1:T(8,128)(2,1)} %param.11) | copy-start | bytes 49156
  89.2 52.4 %all-to-all-start.2 = ((bf16[32,4,32,256]{3,2,1,0:T(8,128)(2,1)}), bf16[32,4,32,256]{3,2,1,0:T(8,128)(2,1)S(1)}, u32[]{:S(2)}, u32[]{:S(2)}) async-start(bf16[32,4,32,256]{3,2,1,0:T(8,128)(2,1)} %triangle.1), calls=%async_computation.2 | async-start | bytes 4194304 | tf_op jit(solution)/shard_map/all_to_all | solution.py:332
  147.6 1.9 %copy-start = (bf16[32,256,256]{2,1,0:T(8,128)(2,1)}, bf16[32,256,256]{2,1,0:T(8,128)(2,1)S(1)}, u32[]{:S(2)}) copy-start(bf16[32,256,256]{2,1,0:T(8,128)(2,1)S(1)} %get-tuple-element.34.grads_ref) | copy-start | bytes 12582916
  149.6 1.3 collective-permute-start
  150.8 9.9 %collective-permute-start.1 = (f32[32,128]{1,0:T(8,128)S(1)}, f32[32,128]{1,0:T(8,128)S(1)}, u32[]{:S(2)}, u32[]{:S(2)}) collective-permute-start(f32[32,128]{1,0:T(8,128)S(1)} %get-tuple-element.31), channel_id=1, source_target_pairs={{0,1},{1,0},{2,3},{3,2},{4,5},{5,4},{6,7},{7,6},{8,9},{9,8},{10,11... | collective-permute-start | bytes 49160 | tf_op jit(solution)/shard_map/ppermute | solution.py:375
  152.5 8.2 %collective-permute-start.2 = (f32[32,128]{1,0:T(8,128)S(1)}, f32[32,128]{1,0:T(8,128)S(1)}, u32[]{:S(2)}, u32[]{:S(2)}) collective-permute-start(f32[32,128]{1,0:T(8,128)S(1)} %get-tuple-element.32), channel_id=1, source_target_pairs={{0,4},{1,5},{2,6},{3,7},{4,0},{5,1},{6,2},{7,3},{8,12},{9,13},{10,... | collective-permute-start | bytes 49160 | tf_op jit(solution)/shard_map/ppermute | solution.py:375
  153.9 6.8 %collective-permute-start.3 = (f32[32,128]{1,0:T(8,128)S(1)}, f32[32,128]{1,0:T(8,128)S(1)}, u32[]{:S(2)}, u32[]{:S(2)}) collective-permute-start(f32[32,128]{1,0:T(8,128)S(1)} %get-tuple-element.33), channel_id=1, source_target_pairs={{0,5},{1,4},{2,7},{3,6},{4,1},{5,0},{6,3},{7,2},{8,13},{9,12},{10,... | collective-permute-start | bytes 49160 | tf_op jit(solution)/shard_map/ppermute | solution.py:375
  154.4 2.2 %copy-start.1 = (bf16[32,256,256]{2,1,0:T(8,128)(2,1)S(1)}, bf16[32,256,256]{2,1,0:T(8,128)(2,1)}, u32[]{:S(2)}) copy-start(bf16[32,256,256]{2,1,0:T(8,128)(2,1)} %copy-done) | copy-start | bytes 12582916
  160.7 8.6 %collective-permute-start.6 = (f32[32,128]{1,0:T(8,128)S(1)}, f32[32,128]{1,0:T(8,128)S(1)}, u32[]{:S(2)}, u32[]{:S(2)}) collective-permute-start(f32[32,128]{1,0:T(8,128)S(1)} %add_add_fusion.1), channel_id=1, source_target_pairs={{0,24},{2,26},{4,28},{6,30},{8,16},{10,18},{12,20},{14,22},{16,8},... | collective-permute-start | bytes 49160 | tf_op jit(solution)/shard_map/ppermute | solution.py:370
  162.1 7.2 %collective-permute-start.5 = (f32[32,128]{1,0:T(8,128)S(1)}, f32[32,128]{1,0:T(8,128)S(1)}, u32[]{:S(2)}, u32[]{:S(2)}) collective-permute-start(f32[32,128]{1,0:T(8,128)S(1)} %add_add_fusion.1), channel_id=1, source_target_pairs={{0,16},{2,18},{4,20},{6,22},{8,24},{10,26},{12,28},{14,30},{16,0},... | collective-permute-start | bytes 49160 | tf_op jit(solution)/shard_map/ppermute | solution.py:370
  163.2 6.1 %collective-permute-start.4 = (f32[32,128]{1,0:T(8,128)S(1)}, f32[32,128]{1,0:T(8,128)S(1)}, u32[]{:S(2)}, u32[]{:S(2)}) collective-permute-start(f32[32,128]{1,0:T(8,128)S(1)} %add_add_fusion.1), channel_id=1, source_target_pairs={{0,8},{2,10},{4,12},{6,14},{8,0},{10,2},{12,4},{14,6},{16,24},{18,... | collective-permute-start | bytes 49160 | tf_op jit(solution)/shard_map/ppermute | solution.py:370
  169.3 4.7 %collective-permute-start.9 = (f32[32,128]{1,0:T(8,128)S(1)}, f32[32,128]{1,0:T(8,128)S(1)}, u32[]{:S(2)}, u32[]{:S(2)}) collective-permute-start(f32[32,128]{1,0:T(8,128)S(1)} %add_add_fusion.refs_0_), channel_id=1, source_target_pairs={{0,5},{1,4},{2,7},{3,6},{4,1},{5,0},{6,3},{7,2},{8,13},{9,12},{10,... | collective-permute-start | bytes 49160 | tf_op jit(solution)/shard_map/ppermute | solution.py:375
  171.8 3.7 %collective-permute-start.8 = (f32[32,128]{1,0:T(8,128)S(1)}, f32[32,128]{1,0:T(8,128)S(1)}, u32[]{:S(2)}, u32[]{:S(2)}) collective-permute-start(f32[32,128]{1,0:T(8,128)S(1)} %add_add_fusion.refs_0_), channel_id=1, source_target_pairs={{0,4},{1,5},{2,6},{3,7},{4,0},{5,1},{6,2},{7,3},{8,12},{9,13},{10,... | collective-permute-start | bytes 49160 | tf_op jit(solution)/shard_map/ppermute | solution.py:375
  172.4 3.7 %collective-permute-start.7 = (f32[32,128]{1,0:T(8,128)S(1)}, f32[32,128]{1,0:T(8,128)S(1)}, u32[]{:S(2)}, u32[]{:S(2)}) collective-permute-start(f32[32,128]{1,0:T(8,128)S(1)} %add_add_fusion.refs_0_), channel_id=1, source_target_pairs={{0,1},{1,0},{2,3},{3,2},{4,5},{5,4},{6,7},{7,6},{8,9},{9,8},{10,11... | collective-permute-start | bytes 49160 | tf_op jit(solution)/shard_map/ppermute | solution.py:375
  176.2 1.3 collective-permute-start.10

commit v6 on v4

--- a/solution.py
+++ b/solution.py
@@ -284,7 +284,7 @@
             pl.BlockSpec((devices, 2, r, c), lambda i: (0, i, 0, 0)),
         ],
         out_specs=pl.BlockSpec((devices, 2, r, c), lambda i: (0, i, 0, 0)),
-        out_shape=lr_shape,
+        out_shape=pltpu.HBM(lr_shape.shape, BF16),
         scratch_shapes=[pltpu.VMEM((n_i, n_k), BF16)] * 3,
         compiler_params=memory(32),
         name="triangle",
@@ -357,6 +357,7 @@
         functools.partial(finish_kernel, 1.0 / n_i),
         in_specs=[smem, pl.BlockSpec(memory_space=pltpu.VMEM), pl.BlockSpec(memory_space=pltpu.VMEM)],
         out_shape=[jax.ShapeDtypeStruct((hidden, dim), F32)] * 4,
+        compiler_params=memory(8),
         name="finish",
     )(bit, mine, lax.ppermute(mine, "row", neighbours))
     return (pair_gradient, *(g.T for g in weight_grads))

time: 173 us -> 171 us (0.988)
  local copies, waits for them, and re-layouts: 1.95 us -> 0.01 us
    unnamed x14 -> x8, local copies, waits for them, and re-layouts: 1.95 us -> 0.01 us
where the time goes in v6:
time: 171 us; the launch traced here: 170 us
  waiting for transfers between devices  78 us (46%)
  blocking collectives  52.3 us (31%)
  Pallas kernels  24.4 us (14%)
  starting transfers between devices  14.9 us (9%)
    all_to_all x1, blocking collectives, channel_shards(): exchange(sent)  52.3 us
    all_to_all x1, waiting for transfers between devices, channel_shards(): exchange(sent)  48.7 us
    all_to_all x1, waiting for transfers between devices, channel_shards(): g_all = exchange(cotangent.reshape(devices, own, r, c))  19.3 us
    pallas_call x2, Pallas kernels, input_piece(): pl.pallas_call(functools.partial(input_kernel, piece * r // pieces), grid...  8.21 us
    ppermute x4, waiting for transfers between devices, channel_shards(): other = lax.ppermute(mine, axis, [(i, i ^ step) for i in range(size)])  7.46 us
    all_to_all x1, starting transfers between devices, channel_shards(): g_all = exchange(cotangent.reshape(devices, own, r, c))  7.3 us
    pallas_call x1, Pallas kernels, channel_shards(): pl.pallas_call(functools.partial(before_kernel, own), grid=(r // block,),...  6.93 us
    pallas_call x1, Pallas kernels, channel_shards(): pl.pallas_call(functools.partial(gates_kernel, own), grid=(r // block,),...  6.02 us
  transfers between devices with their start and end apart: 8, of which 8 were waited for; matrix products, arithmetic and copies ran while one was open for 0% of the time, Pallas kernels for 9%

profile of v6, /device:TPU:0, one launch (start us, length us, event | category | flops | bytes accessed | tf_op | source)
XLA Modules:
  0.0 170.5 jit_solution(7357720103617111991)
XLA Ops:
  0.6 7.3 %all-to-all-start = ((bf16[32,2,32,256]{3,2,1,0:T(8,128)(2,1)}), bf16[32,2,32,256]{3,2,1,0:T(8,128)(2,1)S(1)}, u32[]{:S(2)}, u32[]{:S(2)}) async-start(bf16[32,2,32,256]{3,2,1,0:T(8,128)(2,1)} %bitcast.26), calls=%async_computation | async-start | bytes 2097152 | tf_op jit(solution)/shard_map/all_to_all | solution.py:261
  7.9 6.9 %before.1 = (bf16[32,4,32,256]{3,2,1,0:T(8,128)(2,1)}, bf16[32,128,256]{2,1,0:T(8,128)(2,1)}) custom-call(bf16[32,256,128]{2,1,0:T(8,128)(2,1)} %pair_hbm.3, bf16[64,128]{1,0:T(8,128)(2,1)} %bitcast.10, bf16[64,128]{1,0:T(8,128)(2,1)} %bitcast.14, bf16[64,128]{1,0:T(8,128)(2,1)} %bitcast.18, bf16[64,128]{1,0:T(8,128)(2,1)} %bitcast.22), custom_call_target="tpu_custom_call" | custom-call | flops 536870912 | bytes 4194304 | tf_op jit(solution)/shard_map/before/pallas_call | solution.py:263
  14.9 19.3 %all-to-all-done.cot_ref = bf16[32,2,32,256]{3,2,1,0:T(8,128)(2,1)S(1)} async-done(((bf16[32,2,32,256]{3,2,1,0:T(8,128)(2,1)}), bf16[32,2,32,256]{3,2,1,0:T(8,128)(2,1)S(1)}, u32[]{:S(2)}, u32[]{:S(2)}) %all-to-all-start) | async-done | bytes 1048608 | tf_op jit(solution)/shard_map/all_to_all | solution.py:261
  34.2 52.3 %all_to_all.15.in_ref = bf16[32,4,32,256]{3,2,1,0:T(8,128)(2,1)S(1)} all-to-all(bf16[32,4,32,256]{3,2,1,0:T(8,128)(2,1)} %get-tuple-element.19), channel_id=1, replica_groups=mesh['row'=16,'col'=2] {'row','col'}, dimensions={0} | all-to-all | bytes 4194304 | tf_op jit(solution)/shard_map/all_to_all | solution.py:291
  86.5 2.6 %triangle.1 = bf16[32,4,32,256]{3,2,1,0:T(8,128)(2,1)} custom-call(bf16[32,2,32,256]{3,2,1,0:T(8,128)(2,1)S(1)} %all-to-all-done.cot_ref, bf16[32,4,32,256]{3,2,1,0:T(8,128)(2,1)S(1)} %all_to_all.15.in_ref), custom_call_target="tpu_custom_call" | custom-call | tf_op jit(solution)/shard_map/triangle/pallas_call | solution.py:279
  89.2 0.0 copy-start
  89.2 0.0 copy-start.1
  89.2 0.0 copy-start.2
  89.2 0.0 copy-start.3
  89.2 3.7 %all-to-all-start.2 = ((bf16[32,4,32,256]{3,2,1,0:T(8,128)(2,1)}), bf16[32,4,32,256]{3,2,1,0:T(8,128)(2,1)S(1)}, u32[]{:S(2)}, u32[]{:S(2)}) async-start(bf16[32,4,32,256]{3,2,1,0:T(8,128)(2,1)} %triangle.1), calls=%async_computation.2 | async-start | bytes 4194304 | tf_op jit(solution)/shard_map/all_to_all | solution.py:317
  92.9 48.7 %all-to-all-done.2.d_ref = bf16[32,4,32,256]{3,2,1,0:T(8,128)(2,1)S(1)} async-done(((bf16[32,4,32,256]{3,2,1,0:T(8,128)(2,1)}), bf16[32,4,32,256]{3,2,1,0:T(8,128)(2,1)S(1)}, u32[]{:S(2)}, u32[]{:S(2)}) %all-to-all-start.2) | async-done | bytes 2097184 | tf_op jit(solution)/shard_map/all_to_all | solution.py:317
  141.6 0.0 copy-done
  141.6 0.0 copy-done.1
  141.6 0.0 copy-done.2
  141.6 0.0 copy-done.3
  141.6 6.0 %gates.1 = (bf16[32,256,256]{2,1,0:T(8,128)(2,1)S(1)}, f32[128,128]{1,0:T(8,128)S(1)}, f32[128,128]{1,0:T(8,128)S(1)}) custom-call(s32[1]{0:T(128)} %bitcast.bit_ref, bf16[32,128,256]{2,1,0:T(8,128)(2,1)} %get-tuple-element.18.normed_hbm, bf16[32,4,32,256]{3,2,1,0:T(8,128)(2,1)S(1)} %all-to-all-done.2.d_ref, bf16[64,128]{1,0:T(8,128)(2,1)S(1)} %bitcast.11, ...), custom_call_target="tpu_custom_call" | custom-call | tf_op jit(solution)/shard_map/gates/pallas_call | solution.py:297
  147.6 0.1 collective-permute-start
  147.7 1.2 collective-permute-done
  149.0 1.1 collective-permute-start.1
  150.0 4.1 %input.2.refs_0_ = bf16[32,256,128]{2,1,0:T(8,128)(2,1)} custom-call(bf16[32,256,128]{2,1,0:T(8,128)(2,1)} %pair_hbm.3, bf16[32,256,256]{2,1,0:T(8,128)(2,1)S(1)} %get-tuple-element.22.grads_ref, bf16[64,128]{1,0:T(8,128)(2,1)S(1)} %bitcast.12, bf16[64,128]{1,0:T(8,128)(2,1)S(1)} %bitcast.16, bf16[64,128]{1,0:T(8,128)(2,1)S(1)} %bitcast.20, ...), custom_call_target="tpu_custom_call" | custom-call | flops 268435456 | bytes 2097152 | tf_op jit(solution)/shard_map/input/pallas_call | solution.py:322
  154.1 1.3 collective-permute-done.1
  155.5 0.1 collective-permute-start.2
  155.6 4.1 %input.3 = bf16[32,256,128]{2,1,0:T(8,128)(2,1)} custom-call(bf16[32,256,128]{2,1,0:T(8,128)(2,1)} %pair_hbm.3, bf16[32,256,256]{2,1,0:T(8,128)(2,1)S(1)} %get-tuple-element.22.grads_ref, bf16[64,128]{1,0:T(8,128)(2,1)S(1)} %bitcast.13, bf16[64,128]{1,0:T(8,128)(2,1)S(1)} %bitcast.17, bf16[64,128]{1,0:T(8,128)(2,1)S(1)} %bitcast.21, ...), custom_call_target="tpu_custom_call", output_to_operand_aliasing={{}: (6, {})} | custom-call | flops 268435456 | bytes 2097152 | tf_op jit(solution)/shard_map/input/pallas_call | solution.py:322
  159.7 0.1 collective-permute-done.2
  159.8 1.2 collective-permute-start.3
  161.0 3.1 %collective-permute-done.3 = f32[128,128]{1,0:T(8,128)S(1)} collective-permute-done((f32[128,128]{1,0:T(8,128)S(1)}, f32[128,128]{1,0:T(8,128)S(1)}, u32[]{:S(2)}, u32[]{:S(2)}) %collective-permute-start.3) | collective-permute-done | bytes 65568 | tf_op jit(solution)/shard_map/ppermute | solution.py:351
  164.2 1.5 collective-permute-start.4
  165.7 2.9 %collective-permute-done.4 = f32[128,128]{1,0:T(8,128)S(1)} collective-permute-done((f32[128,128]{1,0:T(8,128)S(1)}, f32[128,128]{1,0:T(8,128)S(1)}, u32[]{:S(2)}, u32[]{:S(2)}) %collective-permute-start.4) | collective-permute-done | bytes 65568 | tf_op jit(solution)/shard_map/ppermute | solution.py:351
  168.5 0.1 collective-permute-start.5
  168.6 1.2 collective-permute-done.5.other_ref
  169.8 0.7 finish.1
  (5 shorter events, 0.0 us)
Async XLA Ops:
  0.6 33.5 %all-to-all-start = ((bf16[32,2,32,256]{3,2,1,0:T(8,128)(2,1)}), bf16[32,2,32,256]{3,2,1,0:T(8,128)(2,1)S(1)}, u32[]{:S(2)}, u32[]{:S(2)}) async-start(bf16[32,2,32,256]{3,2,1,0:T(8,128)(2,1)} %bitcast.26), calls=%async_computation | async-start | bytes 2097152 | tf_op jit(solution)/shard_map/all_to_all | solution.py:261
  89.2 52.4 %copy-start = (bf16[128,64]{0,1:T(8,128)(2,1)S(1)}, bf16[128,64]{0,1:T(8,128)(2,1)}, u32[]{:S(2)}) copy-start(bf16[128,64]{0,1:T(8,128)(2,1)} %param.8) | copy-start | bytes 49156
  89.2 52.4 %copy-start.1 = (bf16[128,64]{0,1:T(8,128)(2,1)S(1)}, bf16[128,64]{0,1:T(8,128)(2,1)}, u32[]{:S(2)}) copy-start(bf16[128,64]{0,1:T(8,128)(2,1)} %param.9) | copy-start | bytes 49156
  89.2 52.4 %copy-start.2 = (bf16[128,64]{0,1:T(8,128)(2,1)S(1)}, bf16[128,64]{0,1:T(8,128)(2,1)}, u32[]{:S(2)}) copy-start(bf16[128,64]{0,1:T(8,128)(2,1)} %param.10) | copy-start | bytes 49156
  89.2 52.4 %copy-start.3 = (bf16[128,64]{0,1:T(8,128)(2,1)S(1)}, bf16[128,64]{0,1:T(8,128)(2,1)}, u32[]{:S(2)}) copy-start(bf16[128,64]{0,1:T(8,128)(2,1)} %param.11) | copy-start | bytes 49156
  89.2 52.4 %all-to-all-start.2 = ((bf16[32,4,32,256]{3,2,1,0:T(8,128)(2,1)}), bf16[32,4,32,256]{3,2,1,0:T(8,128)(2,1)S(1)}, u32[]{:S(2)}, u32[]{:S(2)}) async-start(bf16[32,4,32,256]{3,2,1,0:T(8,128)(2,1)} %triangle.1), calls=%async_computation.2 | async-start | bytes 4194304 | tf_op jit(solution)/shard_map/all_to_all | solution.py:317
  147.6 1.3 collective-permute-start
  149.0 6.5 %collective-permute-start.1 = (f32[128,128]{1,0:T(8,128)S(1)}, f32[128,128]{1,0:T(8,128)S(1)}, u32[]{:S(2)}, u32[]{:S(2)}) collective-permute-start(f32[128,128]{1,0:T(8,128)S(1)} %add.20), channel_id=1, source_target_pairs={{0,16},{2,18},{4,20},{6,22},{8,24},{10,26},{12,28},{14,30},{16,0},... | collective-permute-start | bytes 196616 | tf_op jit(solution)/shard_map/ppermute | solution.py:351
  155.5 4.3 %collective-permute-start.2 = (f32[128,128]{1,0:T(8,128)S(1)}, f32[128,128]{1,0:T(8,128)S(1)}, u32[]{:S(2)}, u32[]{:S(2)}) collective-permute-start(f32[128,128]{1,0:T(8,128)S(1)} %add.21), channel_id=1, source_target_pairs={{0,8},{2,10},{4,12},{6,14},{8,0},{10,2},{12,4},{14,6},{16,24},{18,... | collective-permute-start | bytes 196616 | tf_op jit(solution)/shard_map/ppermute | solution.py:351
  159.8 4.3 %collective-permute-start.3 = (f32[128,128]{1,0:T(8,128)S(1)}, f32[128,128]{1,0:T(8,128)S(1)}, u32[]{:S(2)}, u32[]{:S(2)}) collective-permute-start(f32[128,128]{1,0:T(8,128)S(1)} %add.22), channel_id=1, source_target_pairs={{0,4},{2,6},{4,0},{6,2},{8,12},{10,14},{12,8},{14,10},{16,20},{18,... | collective-permute-start | bytes 196616 | tf_op jit(solution)/shard_map/ppermute | solution.py:351
  164.2 4.3 %collective-permute-start.4 = (f32[128,128]{1,0:T(8,128)S(1)}, f32[128,128]{1,0:T(8,128)S(1)}, u32[]{:S(2)}, u32[]{:S(2)}) collective-permute-start(f32[128,128]{1,0:T(8,128)S(1)} %add.23), channel_id=1, source_target_pairs={{0,1},{1,0},{2,3},{3,2},{4,5},{5,4},{6,7},{7,6},{8,9},{9,8},{10,11... | collective-permute-start | bytes 196616 | tf_op jit(solution)/shard_map/ppermute | solution.py:351
  168.5 1.3 collective-permute-start.5

commit v7 on v4

--- a/solution.py
+++ b/solution.py
@@ -179,19 +179,28 @@
 
     copy(step).wait()
 
-    def one_row(r, carry):
-        normed = normed_ref[step * rows + r]
-        q_left, s_left, q_right, s_right = project(w_ref, normed)
-        e_left = get_lanes(rows_ref, pl.ds(r, h, stride=pitch)) * s_left
-        e_right = get_lanes(rows_ref, pl.ds(r + h * pitch, h, stride=pitch)) * s_right
-        f_left = e_left * q_left * (1.0 - s_left)
-        f_right = e_right * q_right * (1.0 - s_right)
-        grads = jnp.concatenate([e_left, f_left, e_right, f_right], axis=0).astype(BF16)
-        grads_ref[r] = grads
-        sums_ref[...] += dot(grads, normed, NT)
+    together = 4 if rows % 4 == 0 else 1
+
+    def some_rows(n, carry):
+        all_grads, all_normed = [], []
+        for i in range(together):
+            r = n * together + i
+            normed = normed_ref[step * rows + r]
+            q_left, s_left, q_right, s_right = project(w_ref, normed)
+            e_left = get_lanes(rows_ref, pl.ds(r, h, stride=pitch)) * s_left
+            e_right = get_lanes(rows_ref, pl.ds(r + h * pitch, h, stride=pitch)) * s_right
+            f_left = e_left * q_left * (1.0 - s_left)
+            f_right = e_right * q_right * (1.0 - s_right)
+            grads = jnp.concatenate([e_left, f_left, e_right, f_right], axis=0).astype(BF16)
+            grads_ref[r] = grads
+            all_grads.append(grads)
+            all_normed.append(normed)
+        sums_ref[...] += dot(
+            jnp.concatenate(all_grads, axis=1), jnp.concatenate(all_normed, axis=1), NT
+        )
         return carry
 
-    lax.fori_loop(0, rows, one_row, 0, unroll=4)
+    lax.fori_loop(0, rows // together, some_rows, 0)
 
     @pl.when(step == pl.num_programs(0) - 1)
     def _():
@@ -239,6 +248,7 @@
     block = 16 if r % 16 == 0 else r
     pieces = 2 if r % 2 == 0 else 1
     weights = [w.T for w in weights]
+    late_weights = [pltpu.with_memory_space_constraint(w, pltpu.HBM) for w in weights]
     whole = pl.BlockSpec((hidden, dim), lambda i: (0, 0))
     tile = pl.BlockSpec((block, c, dim), lambda i: (i, 0, 0))
     exchange = functools.partial(
@@ -314,7 +324,7 @@
         ],
         compiler_params=memory(28),
         name="gates",
-    )(bit, pltpu.with_memory_space_constraint(normed, pltpu.HBM), exchange(sent), *weights)
+    )(bit, pltpu.with_memory_space_constraint(normed, pltpu.HBM), exchange(sent), *late_weights)
 
     def input_piece(piece, pair_gradient):
         held = [] if pair_gradient is None else [pair_gradient]
@@ -339,7 +349,7 @@
             compiler_params=memory(16),
             cost_estimate=cost(8 * hidden * dim * columns // pieces, pair),
             name="input",
-        )(pltpu.with_memory_space_constraint(pair, pltpu.HBM), grads, *weights, *held)
+        )(pltpu.with_memory_space_constraint(pair, pltpu.HBM), grads, *late_weights, *held)
 
     steps = [("row", rows, 1 << i) for i in range(1, rows.bit_length() - 1)][::-1]
     steps += [("col", cols, 1 << i) for i in range(cols.bit_length() - 1)]
@@ -357,6 +367,7 @@
         functools.partial(finish_kernel, 1.0 / n_i),
         in_specs=[smem, pl.BlockSpec(memory_space=pltpu.VMEM), pl.BlockSpec(memory_space=pltpu.VMEM)],
         out_shape=[jax.ShapeDtypeStruct((hidden, dim), F32)] * 4,
+        compiler_params=memory(8),
         name="finish",
     )(bit, mine, lax.ppermute(mine, "row", neighbours))
     return (pair_gradient, *(g.T for g in weight_grads))

time: 173 us -> 172 us (level)
  waiting for transfers between devices: 77.9 us -> 76.1 us
    ppermute x4, waiting for transfers between devices: 7.44 us -> 5.59 us  [channel_shards(): other = lax.ppermute(mine, axis, [(i, i ^ step) for i in range(size)])]
  transfers between devices with their start and end apart: 8 -> 8, of which waited for: 8 -> 7; matrix products, arithmetic and copies ran while one was open for 0% -> 0% of each run, Pallas kernels for 9% -> 10%
where the time goes in v7:
time: 172 us
  waiting for transfers between devices  76.1 us (44%)
  blocking collectives  52.3 us (30%)
  Pallas kernels  25.1 us (15%)
  starting transfers between devices  16.2 us (9%)
    all_to_all x1, blocking collectives, channel_shards(): exchange(sent)  52.3 us
    all_to_all x1, waiting for transfers between devices, channel_shards(): exchange(sent)  48.7 us
    all_to_all x1, waiting for transfers between devices, channel_shards(): g_all = exchange(cotangent.reshape(devices, own, r, c))  19.3 us
    pallas_call x2, Pallas kernels, input_piece(): pl.pallas_call(functools.partial(input_kernel, piece * r // pieces), grid...  9.73 us
    all_to_all x1, starting transfers between devices, channel_shards(): g_all = exchange(cotangent.reshape(devices, own, r, c))  7.3 us
    pallas_call x1, Pallas kernels, channel_shards(): pl.pallas_call(functools.partial(before_kernel, own), grid=(r // block,),...  6.94 us
    pallas_call x1, Pallas kernels, channel_shards(): pl.pallas_call(functools.partial(gates_kernel, own), grid=(r // block,),...  5.98 us
    ppermute x4, waiting for transfers between devices, channel_shards(): other = lax.ppermute(mine, axis, [(i, i ^ step) for i in range(size)])  5.59 us
  transfers between devices with their start and end apart: 8, of which 7 were waited for; matrix products, arithmetic and copies ran while one was open for 0% of the time, Pallas kernels for 10%

profile of v7, /device:TPU:0, one launch (start us, length us, event | category | flops | bytes accessed | tf_op | source)
XLA Modules:
  0.0 171.8 jit_solution(13111013801211653946)
XLA Ops:
  0.6 7.3 %all-to-all-start = ((bf16[32,2,32,256]{3,2,1,0:T(8,128)(2,1)}), bf16[32,2,32,256]{3,2,1,0:T(8,128)(2,1)S(1)}, u32[]{:S(2)}, u32[]{:S(2)}) async-start(bf16[32,2,32,256]{3,2,1,0:T(8,128)(2,1)} %bitcast.10), calls=%async_computation | async-start | bytes 2097152 | tf_op jit(solution)/shard_map/all_to_all | solution.py:271
  7.9 6.9 %before.1 = (bf16[32,4,32,256]{3,2,1,0:T(8,128)(2,1)}, bf16[32,128,256]{2,1,0:T(8,128)(2,1)}) custom-call(bf16[32,256,128]{2,1,0:T(8,128)(2,1)} %pair_hbm.3, bf16[64,128]{1,0:T(8,128)(2,1)} %bitcast.11, bf16[64,128]{1,0:T(8,128)(2,1)} %bitcast.15, bf16[64,128]{1,0:T(8,128)(2,1)} %bitcast.19, bf16[64,128]{1,0:T(8,128)(2,1)} %bitcast.23), custom_call_target="tpu_custom_call" | custom-call | flops 536870912 | bytes 4194304 | tf_op jit(solution)/shard_map/before/pallas_call | solution.py:273
  14.9 19.3 %all-to-all-done.cot_ref = bf16[32,2,32,256]{3,2,1,0:T(8,128)(2,1)S(1)} async-done(((bf16[32,2,32,256]{3,2,1,0:T(8,128)(2,1)}), bf16[32,2,32,256]{3,2,1,0:T(8,128)(2,1)S(1)}, u32[]{:S(2)}, u32[]{:S(2)}) %all-to-all-start) | async-done | bytes 1048608 | tf_op jit(solution)/shard_map/all_to_all | solution.py:271
  34.2 52.3 %all_to_all.15.in_ref = bf16[32,4,32,256]{3,2,1,0:T(8,128)(2,1)S(1)} all-to-all(bf16[32,4,32,256]{3,2,1,0:T(8,128)(2,1)} %get-tuple-element.19), channel_id=1, replica_groups=mesh['row'=16,'col'=2] {'row','col'}, dimensions={0} | all-to-all | bytes 4194304 | tf_op jit(solution)/shard_map/all_to_all | solution.py:301
  86.5 1.8 %triangle.1 = bf16[32,4,32,256]{3,2,1,0:T(8,128)(2,1)S(1)} custom-call(bf16[32,2,32,256]{3,2,1,0:T(8,128)(2,1)S(1)} %all-to-all-done.cot_ref, bf16[32,4,32,256]{3,2,1,0:T(8,128)(2,1)S(1)} %all_to_all.15.in_ref), custom_call_target="tpu_custom_call" | custom-call | tf_op jit(solution)/shard_map/triangle/pallas_call | solution.py:289
  88.3 0.0 copy-start
  88.3 1.3 copy-done
  89.6 3.7 %all-to-all-start.2 = ((bf16[32,4,32,256]{3,2,1,0:T(8,128)(2,1)}), bf16[32,4,32,256]{3,2,1,0:T(8,128)(2,1)S(1)}, u32[]{:S(2)}, u32[]{:S(2)}) async-start(bf16[32,4,32,256]{3,2,1,0:T(8,128)(2,1)} %copy-done), calls=%async_computation.2 | async-start | bytes 4194304 | tf_op jit(solution)/shard_map/all_to_all | solution.py:327
  93.3 48.7 %all-to-all-done.2.d_ref = bf16[32,4,32,256]{3,2,1,0:T(8,128)(2,1)S(1)} async-done(((bf16[32,4,32,256]{3,2,1,0:T(8,128)(2,1)}), bf16[32,4,32,256]{3,2,1,0:T(8,128)(2,1)S(1)}, u32[]{:S(2)}, u32[]{:S(2)}) %all-to-all-start.2) | async-done | bytes 2097184 | tf_op jit(solution)/shard_map/all_to_all | solution.py:327
  142.0 6.0 %gates.1 = (bf16[32,256,256]{2,1,0:T(8,128)(2,1)S(1)}, f32[128,128]{1,0:T(8,128)S(1)}, f32[128,128]{1,0:T(8,128)S(1)}) custom-call(s32[1]{0:T(128)} %bitcast.bit_ref, bf16[32,128,256]{2,1,0:T(8,128)(2,1)} %get-tuple-element.18.normed_hbm, bf16[32,4,32,256]{3,2,1,0:T(8,128)(2,1)S(1)} %all-to-all-done.2.d_ref, bf16[64,128]{1,0:T(8,128)(2,1)} %bitcast.12, ...), custom_call_target="tpu_custom_call" | custom-call | tf_op jit(solution)/shard_map/gates/pallas_call | solution.py:307
  148.0 0.1 collective-permute-start
  148.1 1.2 collective-permute-done
  149.4 1.1 collective-permute-start.1
  150.4 4.9 %input.2.refs_0_ = bf16[32,256,128]{2,1,0:T(8,128)(2,1)} custom-call(bf16[32,256,128]{2,1,0:T(8,128)(2,1)} %pair_hbm.3, bf16[32,256,256]{2,1,0:T(8,128)(2,1)S(1)} %get-tuple-element.22.grads_ref, bf16[64,128]{1,0:T(8,128)(2,1)} %bitcast.13, bf16[64,128]{1,0:T(8,128)(2,1)} %bitcast.17, bf16[64,128]{1,0:T(8,128)(2,1)} %bitcast.21, bf16[64,128]{1,0:T(8,128)(2,1)} %bitcast.25), custom_call_target="tpu_custom_call" | custom-call | flops 268435456 | bytes 2097152 | tf_op jit(solution)/shard_map/input/pallas_call | solution.py:332
  155.3 0.6 collective-permute-done.1
  155.9 0.3 collective-permute-start.2
  156.2 4.9 %input.3 = bf16[32,256,128]{2,1,0:T(8,128)(2,1)} custom-call(bf16[32,256,128]{2,1,0:T(8,128)(2,1)} %pair_hbm.3, bf16[32,256,256]{2,1,0:T(8,128)(2,1)S(1)} %get-tuple-element.22.grads_ref, bf16[64,128]{1,0:T(8,128)(2,1)} %bitcast.14, bf16[64,128]{1,0:T(8,128)(2,1)} %bitcast.18, bf16[64,128]{1,0:T(8,128)(2,1)} %bitcast.22, ...), custom_call_target="tpu_custom_call", output_to_operand_aliasing={{}: (6, {})} | custom-call | flops 268435456 | bytes 2097152 | tf_op jit(solution)/shard_map/input/pallas_call | solution.py:332
  161.1 0.0 collective-permute-done.2
  161.1 1.8 %collective-permute-start.3 = (f32[128,128]{1,0:T(8,128)S(1)}, f32[128,128]{1,0:T(8,128)S(1)}, u32[]{:S(2)}, u32[]{:S(2)}) collective-permute-start(f32[128,128]{1,0:T(8,128)S(1)} %add.22), channel_id=1, source_target_pairs={{0,4},{2,6},{4,0},{6,2},{8,12},{10,14},{12,8},{14,10},{16,20},{18,... | collective-permute-start | bytes 196616 | tf_op jit(solution)/shard_map/ppermute | solution.py:361
  163.0 2.5 %collective-permute-done.3 = f32[128,128]{1,0:T(8,128)S(1)} collective-permute-done((f32[128,128]{1,0:T(8,128)S(1)}, f32[128,128]{1,0:T(8,128)S(1)}, u32[]{:S(2)}, u32[]{:S(2)}) %collective-permute-start.3) | collective-permute-done | bytes 65568 | tf_op jit(solution)/shard_map/ppermute | solution.py:361
  165.5 1.8 %collective-permute-start.4 = (f32[128,128]{1,0:T(8,128)S(1)}, f32[128,128]{1,0:T(8,128)S(1)}, u32[]{:S(2)}, u32[]{:S(2)}) collective-permute-start(f32[128,128]{1,0:T(8,128)S(1)} %add.23), channel_id=1, source_target_pairs={{0,1},{1,0},{2,3},{3,2},{4,5},{5,4},{6,7},{7,6},{8,9},{9,8},{10,11... | collective-permute-start | bytes 196616 | tf_op jit(solution)/shard_map/ppermute | solution.py:361
  167.3 2.5 %collective-permute-done.4 = f32[128,128]{1,0:T(8,128)S(1)} collective-permute-done((f32[128,128]{1,0:T(8,128)S(1)}, f32[128,128]{1,0:T(8,128)S(1)}, u32[]{:S(2)}, u32[]{:S(2)}) %collective-permute-start.4) | collective-permute-done | bytes 65568 | tf_op jit(solution)/shard_map/ppermute | solution.py:361
  169.8 0.1 collective-permute-start.5
  169.9 1.2 collective-permute-done.5.other_ref
  171.1 0.7 finish.1
  (5 shorter events, 0.0 us)
Async XLA Ops:
  0.6 33.5 %all-to-all-start = ((bf16[32,2,32,256]{3,2,1,0:T(8,128)(2,1)}), bf16[32,2,32,256]{3,2,1,0:T(8,128)(2,1)S(1)}, u32[]{:S(2)}, u32[]{:S(2)}) async-start(bf16[32,2,32,256]{3,2,1,0:T(8,128)(2,1)} %bitcast.10), calls=%async_computation | async-start | bytes 2097152 | tf_op jit(solution)/shard_map/all_to_all | solution.py:271
  88.3 1.3 copy-start
  89.6 52.4 %all-to-all-start.2 = ((bf16[32,4,32,256]{3,2,1,0:T(8,128)(2,1)}), bf16[32,4,32,256]{3,2,1,0:T(8,128)(2,1)S(1)}, u32[]{:S(2)}, u32[]{:S(2)}) async-start(bf16[32,4,32,256]{3,2,1,0:T(8,128)(2,1)} %copy-done), calls=%async_computation.2 | async-start | bytes 4194304 | tf_op jit(solution)/shard_map/all_to_all | solution.py:327
  148.0 1.3 collective-permute-start
  149.4 6.5 %collective-permute-start.1 = (f32[128,128]{1,0:T(8,128)S(1)}, f32[128,128]{1,0:T(8,128)S(1)}, u32[]{:S(2)}, u32[]{:S(2)}) collective-permute-start(f32[128,128]{1,0:T(8,128)S(1)} %add.20), channel_id=1, source_target_pairs={{0,16},{2,18},{4,20},{6,22},{8,24},{10,26},{12,28},{14,30},{16,0},... | collective-permute-start | bytes 196616 | tf_op jit(solution)/shard_map/ppermute | solution.py:361
  155.9 5.2 %collective-permute-start.2 = (f32[128,128]{1,0:T(8,128)S(1)}, f32[128,128]{1,0:T(8,128)S(1)}, u32[]{:S(2)}, u32[]{:S(2)}) collective-permute-start(f32[128,128]{1,0:T(8,128)S(1)} %add.21), channel_id=1, source_target_pairs={{0,8},{2,10},{4,12},{6,14},{8,0},{10,2},{12,4},{14,6},{16,24},{18,... | collective-permute-start | bytes 196616 | tf_op jit(solution)/shard_map/ppermute | solution.py:361
  161.1 4.3 %collective-permute-start.3 = (f32[128,128]{1,0:T(8,128)S(1)}, f32[128,128]{1,0:T(8,128)S(1)}, u32[]{:S(2)}, u32[]{:S(2)}) collective-permute-start(f32[128,128]{1,0:T(8,128)S(1)} %add.22), channel_id=1, source_target_pairs={{0,4},{2,6},{4,0},{6,2},{8,12},{10,14},{12,8},{14,10},{16,20},{18,... | collective-permute-start | bytes 196616 | tf_op jit(solution)/shard_map/ppermute | solution.py:361
  165.5 4.3 %collective-permute-start.4 = (f32[128,128]{1,0:T(8,128)S(1)}, f32[128,128]{1,0:T(8,128)S(1)}, u32[]{:S(2)}, u32[]{:S(2)}) collective-permute-start(f32[128,128]{1,0:T(8,128)S(1)} %add.23), channel_id=1, source_target_pairs={{0,1},{1,0},{2,3},{3,2},{4,5},{5,4},{6,7},{7,6},{8,9},{9,8},{10,11... | collective-permute-start | bytes 196616 | tf_op jit(solution)/shard_map/ppermute | solution.py:361
  169.8 1.3 collective-permute-start.5

commit v8 on v7

--- a/solution.py
+++ b/solution.py
@@ -153,23 +153,16 @@
                 out_ref[a * cols + b, i] = d[a * r : (a + 1) * r, b * c : (b + 1) * c]
 
 
-def gates_kernel(own, bit_ref, normed_hbm, d_ref, wl, wlg, wr, wrg, grads_ref, kept_ref, sent_ref, *scratch):
-    w_ref, sums_ref, rows_ref, normed_ref, sems = scratch
+def gates_kernel(own, normed_hbm, d_ref, wl, wlg, wr, wrg, grads_ref, kept_ref, sent_ref, *scratch):
+    w_ref, sums_ref, rows_ref, normed_ref, sem = scratch
+    copy = pltpu.make_async_copy(normed_hbm, normed_ref, sem)
+    copy.start()
     h = wl.shape[0]
     rows = grads_ref.shape[0]
     pitch = rows + 1
-    step = pl.program_id(0)
-
-    def copy(block):
-        at = pl.ds(block * rows, rows)
-        return pltpu.make_async_copy(normed_hbm.at[at], normed_ref.at[at], sems.at[block])
-
-    @pl.when(step == 0)
-    def _():
-        for block in range(normed_ref.shape[0] // rows):
-            copy(block).start()
-        sums_ref[...] = jnp.zeros_like(sums_ref)
-        stack_weights((wl, wlg, wr, wrg), w_ref)
+    together = 4 if rows % 4 == 0 else 1
+    stack_weights((wl, wlg, wr, wrg), w_ref)
+    sums_ref[...] = jnp.zeros_like(sums_ref)
 
     for channel in range(h):
         to, slot = channel // own, (channel % own) * 2
@@ -177,15 +170,13 @@
             line = d_ref[to, slot + side].astype(F32)
             put_lanes(rows_ref, pl.ds((side * h + channel) * pitch, rows), line)
 
-    copy(step).wait()
-
-    together = 4 if rows % 4 == 0 else 1
+    copy.wait()
 
     def some_rows(n, carry):
         all_grads, all_normed = [], []
         for i in range(together):
             r = n * together + i
-            normed = normed_ref[step * rows + r]
+            normed = normed_ref[r]
             q_left, s_left, q_right, s_right = project(w_ref, normed)
             e_left = get_lanes(rows_ref, pl.ds(r, h, stride=pitch)) * s_left
             e_right = get_lanes(rows_ref, pl.ds(r + h * pitch, h, stride=pitch)) * s_right
@@ -201,41 +192,49 @@
         return carry
 
     lax.fori_loop(0, rows // together, some_rows, 0)
-
-    @pl.when(step == pl.num_programs(0) - 1)
-    def _():
-        bit = bit_ref[0]
-        kept_ref[...] = sums_ref[pl.ds(pl.multiple_of(bit * 2 * h, 2 * h), 2 * h), :]
-        sent_ref[...] = sums_ref[pl.ds(pl.multiple_of((1 - bit) * 2 * h, 2 * h), 2 * h), :]
+    bit = lax.rem(lax.axis_index("row"), 2)
+    kept_ref[...] = sums_ref[pl.ds(pl.multiple_of(bit * 2 * h, 2 * h), 2 * h), :]
+    sent_ref[...] = sums_ref[pl.ds(pl.multiple_of((1 - bit) * 2 * h, 2 * h), 2 * h), :]
 
 
 def input_kernel(start, pair_hbm, grads_ref, wl, wlg, wr, wrg, *refs):
-    out_ref, back_ref, pair_ref, sem = refs[-4:]
-    copy = pltpu.make_async_copy(pair_hbm.at[pl.ds(start, pair_ref.shape[0])], pair_ref, sem)
-    copy.start()
+    out_hbm, back_ref, pair_ref, out_ref, in_sem, out_sems = refs[-6:]
+    rows = pair_ref.shape[0]
+    come = pltpu.make_async_copy(pair_hbm.at[pl.ds(start, rows)], pair_ref, in_sem)
+    come.start()
     h = wl.shape[0]
     for i, ref in enumerate((wl, wlg, wr, wrg)):
         back_ref[:, pl.ds(i * h, h)] = ref[...].T
-
-    copy.wait()
+    come.wait()
 
     def one_row(r, carry):
         standardized, inverse_scale = layer_norm(pair_ref[r])
-        d_normed = dot(back_ref[...], grads_ref[r])
+        d_normed = dot(back_ref[...], grads_ref[start + r])
         mean = jnp.mean(d_normed, axis=0, keepdims=True)
         input_mean = jnp.mean(d_normed * standardized, axis=0, keepdims=True)
         moved = (d_normed - mean - standardized * input_mean) * inverse_scale
         out_ref[r] = moved.astype(BF16).T
         return carry
 
-    lax.fori_loop(0, pair_ref.shape[0], one_row, 0, unroll=4)
-
-
-def finish_kernel(scale, bit_ref, mine_ref, other_ref, *out_refs):
+    parts = out_sems.shape[0]
+    count = rows // parts
+    gone = []
+    for part in range(parts):
+        lax.fori_loop(part * count, (part + 1) * count, one_row, 0, unroll=4)
+        at = pl.ds(part * count, count)
+        to = out_hbm.at[pl.ds(start + part * count, count)]
+        gone.append(pltpu.make_async_copy(out_ref.at[at], to, out_sems.at[part]))
+        gone[-1].start()
+    for copy in gone:
+        copy.wait()
+
+
+def finish_kernel(scale, mine_ref, other_ref, *out_refs):
     h = out_refs[0].shape[0]
+    bit = lax.rem(lax.axis_index("row"), 2)
     for i, out_ref in enumerate(out_refs):
         at = pl.ds(i % 2 * h, h)
-        mine = bit_ref[0] == i // 2
+        mine = bit == i // 2
         out_ref[...] = jnp.where(mine, mine_ref[at, :], other_ref[at, :]) * scale
 
 
@@ -248,7 +247,6 @@
     block = 16 if r % 16 == 0 else r
     pieces = 2 if r % 2 == 0 else 1
     weights = [w.T for w in weights]
-    late_weights = [pltpu.with_memory_space_constraint(w, pltpu.HBM) for w in weights]
     whole = pl.BlockSpec((hidden, dim), lambda i: (0, 0))
     tile = pl.BlockSpec((block, c, dim), lambda i: (i, 0, 0))
     exchange = functools.partial(
@@ -256,7 +254,7 @@
     )
     stacked = pltpu.VMEM((4 * hidden, dim), BF16)
     lanes = min(c, 128)
-    rows_scratch = pltpu.VMEM((c // lanes, 2 * hidden * (block + 1), lanes), F32)
+    rows_scratch = pltpu.VMEM((c // lanes, (2 * hidden + 1) * (block + 1), lanes), F32)
 
     def cost(flops, *arrays):
         moved = sum(a.size * a.dtype.itemsize for a in arrays)
@@ -267,7 +265,6 @@
 
     columns = r * c
     lr_shape = jax.ShapeDtypeStruct((devices, 2 * own, r, c), BF16)
-    by_hidden = pl.BlockSpec((block, 4 * hidden, c), lambda i: (i, 0, 0))
     g_all = exchange(cotangent.reshape(devices, own, r, c))
     normed_shape = jax.ShapeDtypeStruct((r, dim, c), BF16)
     sent, normed = pl.pallas_call(
@@ -300,56 +297,45 @@
         name="triangle",
     )(g_all, exchange(sent))
 
-    bit = (lax.axis_index("row") % 2).astype(jnp.int32).reshape(1)
-    smem = pl.BlockSpec(memory_space=pltpu.SMEM)
+    vmem = pl.BlockSpec(memory_space=pltpu.VMEM)
+    hbm = pl.BlockSpec(memory_space=pltpu.HBM)
     half_shape = jax.ShapeDtypeStruct((2 * hidden, dim), F32)
-    half = pl.BlockSpec(half_shape.shape, lambda i: (0, 0))
     grads, kept, given = pl.pallas_call(
         functools.partial(gates_kernel, own),
-        grid=(r // block,),
-        in_specs=[
-            smem,
-            pl.BlockSpec(memory_space=pltpu.HBM),
-            pl.BlockSpec((devices, 2 * own, block, c), lambda i: (0, 0, i, 0)),
-        ]
-        + [whole] * 4,
-        out_specs=[by_hidden, half, half],
+        in_specs=[hbm] + [vmem] * 5,
+        out_specs=[vmem] * 3,
         out_shape=[jax.ShapeDtypeStruct((r, 4 * hidden, c), BF16), half_shape, half_shape],
         scratch_shapes=[
             stacked,
             pltpu.VMEM((4 * hidden, dim), F32),
-            rows_scratch,
+            pltpu.VMEM((c // lanes, (2 * hidden + 1) * (r + 1), lanes), F32),
             pltpu.VMEM(normed_shape.shape, BF16),
-            pltpu.SemaphoreType.DMA((r // block,)),
+            pltpu.SemaphoreType.DMA,
         ],
         compiler_params=memory(28),
         name="gates",
-    )(bit, pltpu.with_memory_space_constraint(normed, pltpu.HBM), exchange(sent), *late_weights)
+    )(pltpu.with_memory_space_constraint(normed, pltpu.HBM), exchange(sent), *weights)
 
     def input_piece(piece, pair_gradient):
         held = [] if pair_gradient is None else [pair_gradient]
-        at = pl.BlockSpec((r // pieces, c, dim), lambda i: (piece, 0, 0))
+        count = r // pieces
         return pl.pallas_call(
-            functools.partial(input_kernel, piece * r // pieces),
-            grid=(1,),
-            in_specs=[
-                pl.BlockSpec(memory_space=pltpu.HBM),
-                pl.BlockSpec((r // pieces, 4 * hidden, c), lambda i: (piece, 0, 0)),
-            ]
-            + [whole] * 4
-            + [pl.BlockSpec(memory_space=pl.ANY)] * len(held),
-            out_specs=at,
+            functools.partial(input_kernel, piece * count),
+            in_specs=[hbm] + [vmem] * 5 + [hbm] * len(held),
+            out_specs=hbm,
             out_shape=jax.ShapeDtypeStruct(pair.shape, BF16),
             scratch_shapes=[
                 pltpu.VMEM((dim, 4 * hidden), BF16),
-                pltpu.VMEM((r // pieces, c, dim), BF16),
+                pltpu.VMEM((count, c, dim), BF16),
+                pltpu.VMEM((count, c, dim), BF16),
                 pltpu.SemaphoreType.DMA,
+                pltpu.SemaphoreType.DMA((2 if count % 8 == 0 else 1,)),
             ],
             input_output_aliases={6: 0} if held else {},
             compiler_params=memory(16),
             cost_estimate=cost(8 * hidden * dim * columns // pieces, pair),
             name="input",
-        )(pltpu.with_memory_space_constraint(pair, pltpu.HBM), grads, *late_weights, *held)
+        )(pltpu.with_memory_space_constraint(pair, pltpu.HBM), grads, *weights, *held)
 
     steps = [("row", rows, 1 << i) for i in range(1, rows.bit_length() - 1)][::-1]
     steps += [("col", cols, 1 << i) for i in range(cols.bit_length() - 1)]
@@ -365,11 +351,11 @@
         mine = mine + other
     weight_grads = pl.pallas_call(
         functools.partial(finish_kernel, 1.0 / n_i),
-        in_specs=[smem, pl.BlockSpec(memory_space=pltpu.VMEM), pl.BlockSpec(memory_space=pltpu.VMEM)],
+        in_specs=[vmem, vmem],
         out_shape=[jax.ShapeDtypeStruct((hidden, dim), F32)] * 4,
         compiler_params=memory(8),
         name="finish",
-    )(bit, mine, lax.ppermute(mine, "row", neighbours))
+    )(mine, lax.ppermute(mine, "row", neighbours))
     return (pair_gradient, *(g.T for g in weight_grads))
 
 

time: 172 us -> 169 us (0.983)
  blocking collectives: 52.3 us -> 105 us
  waiting for transfers between devices: 76.1 us -> 28.7 us
  starting transfers between devices: 16.2 us -> 12.2 us
  Pallas kernels: 25.1 us -> 22.6 us
    all_to_all x1 -> x2, blocking collectives: 52.3 us -> 105 us  [channel_shards(): exchange(sent)]
    all_to_all x1 -> x0, waiting for transfers between devices: 48.7 us -> none  [channel_shards(): exchange(sent)]
    all_to_all x1 -> x0, starting transfers between devices: 3.67 us -> none  [channel_shards(): exchange(sent)]
    pallas_call x4, Pallas kernels: 16.4 us -> 13.9 us  [the longest x2 7.89 us: input_piece(): pl.pallas_call(functools.partial(input_kernel, piece * count), in_specs=[...]
  transfers between devices with their start and end apart: 8 -> 7, of which waited for: 7 -> 6; matrix products, arithmetic and copies ran while one was open for 0% -> 0% of each run, Pallas kernels for 10% -> 9%
where the time goes in v8:
time: 169 us
  blocking collectives  105 us (62%)
  waiting for transfers between devices  28.7 us (17%)
  Pallas kernels  22.6 us (13%)
  starting transfers between devices  12.2 us (7%)
    all_to_all x2, blocking collectives, channel_shards(): exchange(sent)  105 us
    all_to_all x1, waiting for transfers between devices, channel_shards(): g_all = exchange(cotangent.reshape(devices, own, r, c))  19.3 us
    pallas_call x2, Pallas kernels, input_piece(): pl.pallas_call(functools.partial(input_kernel, piece * count), in_specs=[...  7.89 us
    all_to_all x1, starting transfers between devices, channel_shards(): g_all = exchange(cotangent.reshape(devices, own, r, c))  7.3 us
    ppermute x4, waiting for transfers between devices, channel_shards(): other = lax.ppermute(mine, axis, [(i, i ^ step) for i in range(size)])  6.96 us
    pallas_call x1, Pallas kernels, channel_shards(): pl.pallas_call(functools.partial(before_kernel, own), grid=(r // block,),...  6.94 us
    pallas_call x1, Pallas kernels, channel_shards(): pl.pallas_call(functools.partial(gates_kernel, own), in_specs=[hbm] + [vm...  5.34 us
    ppermute x4, starting transfers between devices, channel_shards(): other = lax.ppermute(mine, axis, [(i, i ^ step) for i in range(size)])  4.76 us
  transfers between devices with their start and end apart: 7, of which 6 were waited for; matrix products, arithmetic and copies ran while one was open for 0% of the time, Pallas kernels for 9%

profile of v8, /device:TPU:0, one launch (start us, length us, event | category | flops | bytes accessed | tf_op | source)
XLA Modules:
  0.0 168.9 jit_solution(10780338388190630955)
XLA Ops:
  0.6 7.3 %all-to-all-start = ((bf16[32,2,32,256]{3,2,1,0:T(8,128)(2,1)}), bf16[32,2,32,256]{3,2,1,0:T(8,128)(2,1)S(1)}, u32[]{:S(2)}, u32[]{:S(2)}) async-start(bf16[32,2,32,256]{3,2,1,0:T(8,128)(2,1)} %bitcast.25), calls=%async_computation | async-start | bytes 2097152 | tf_op jit(solution)/shard_map/all_to_all | solution.py:268
  7.9 6.9 %before.1 = (bf16[32,4,32,256]{3,2,1,0:T(8,128)(2,1)}, bf16[32,128,256]{2,1,0:T(8,128)(2,1)}) custom-call(bf16[32,256,128]{2,1,0:T(8,128)(2,1)} %pair_hbm.3, bf16[64,128]{1,0:T(8,128)(2,1)} %bitcast.9, bf16[64,128]{1,0:T(8,128)(2,1)} %bitcast.13, bf16[64,128]{1,0:T(8,128)(2,1)} %bitcast.17, bf16[64,128]{1,0:T(8,128)(2,1)} %bitcast.21), custom_call_target="tpu_custom_call" | custom-call | flops 536870912 | bytes 4194304 | tf_op jit(solution)/shard_map/before/pallas_call | solution.py:270
  14.9 19.3 %all-to-all-done.cot_ref = bf16[32,2,32,256]{3,2,1,0:T(8,128)(2,1)S(1)} async-done(((bf16[32,2,32,256]{3,2,1,0:T(8,128)(2,1)}), bf16[32,2,32,256]{3,2,1,0:T(8,128)(2,1)S(1)}, u32[]{:S(2)}, u32[]{:S(2)}) %all-to-all-start) | async-done | bytes 1048608 | tf_op jit(solution)/shard_map/all_to_all | solution.py:268
  34.2 52.3 %all_to_all.15.in_ref = bf16[32,4,32,256]{3,2,1,0:T(8,128)(2,1)S(1)} all-to-all(bf16[32,4,32,256]{3,2,1,0:T(8,128)(2,1)} %get-tuple-element.19), channel_id=1, replica_groups=mesh['row'=16,'col'=2] {'row','col'}, dimensions={0} | all-to-all | bytes 4194304 | tf_op jit(solution)/shard_map/all_to_all | solution.py:298
  86.5 1.8 %triangle.1 = bf16[32,4,32,256]{3,2,1,0:T(8,128)(2,1)S(1)} custom-call(bf16[32,2,32,256]{3,2,1,0:T(8,128)(2,1)S(1)} %all-to-all-done.cot_ref, bf16[32,4,32,256]{3,2,1,0:T(8,128)(2,1)S(1)} %all_to_all.15.in_ref), custom_call_target="tpu_custom_call" | custom-call | tf_op jit(solution)/shard_map/triangle/pallas_call | solution.py:286
  88.3 0.0 copy-start
  88.3 0.0 copy-start.1
  88.3 0.0 copy-start.2
  88.3 0.0 copy-start.3
  88.4 52.2 %all_to_all.16.d_ref = bf16[32,4,32,256]{3,2,1,0:T(8,128)(2,1)S(1)} all-to-all(bf16[32,4,32,256]{3,2,1,0:T(8,128)(2,1)S(1)} %triangle.1), channel_id=1, replica_groups=mesh['row'=16,'col'=2] {'row','col'}, dimensions={0} | all-to-all | bytes 4194304 | tf_op jit(solution)/shard_map/all_to_all | solution.py:317
  140.5 0.0 copy-done
  140.5 0.0 copy-done.1
  140.5 0.0 copy-done.2
  140.5 0.0 copy-done.3
  140.6 5.3 %gates.1 = (bf16[32,256,256]{2,1,0:T(8,128)(2,1)S(1)}, f32[128,128]{1,0:T(8,128)S(1)}, f32[128,128]{1,0:T(8,128)S(1)}) custom-call(bf16[32,128,256]{2,1,0:T(8,128)(2,1)} %get-tuple-element.18.normed_hbm, bf16[32,4,32,256]{3,2,1,0:T(8,128)(2,1)S(1)} %all_to_all.16.d_ref, bf16[64,128]{1,0:T(8,128)(2,1)S(1)} %bitcast.10, bf16[64,128]{1,0:T(8,128)(2,1)S(1)} %bitcast.14, ...), custom_call_target="tpu_custom_call" | custom-call | tf_op jit(solution)/shard_map/gates/pallas_call | solution.py:303
  145.9 0.1 collective-permute-start
  146.0 1.2 collective-permute-done
  147.2 1.8 %collective-permute-start.1 = (f32[128,128]{1,0:T(8,128)S(1)}, f32[128,128]{1,0:T(8,128)S(1)}, u32[]{:S(2)}, u32[]{:S(2)}) collective-permute-start(f32[128,128]{1,0:T(8,128)S(1)} %add.15), channel_id=1, source_target_pairs={{0,16},{2,18},{4,20},{6,22},{8,24},{10,26},{12,28},{14,30},{16,0},... | collective-permute-start | bytes 196616 | tf_op jit(solution)/shard_map/ppermute | solution.py:347
  149.1 3.9 %input.2.refs_0_ = bf16[32,256,128]{2,1,0:T(8,128)(2,1)} custom-call(bf16[32,256,128]{2,1,0:T(8,128)(2,1)} %pair_hbm.3, bf16[32,256,256]{2,1,0:T(8,128)(2,1)S(1)} %get-tuple-element.22.grads_ref, bf16[64,128]{1,0:T(8,128)(2,1)S(1)} %bitcast.11, bf16[64,128]{1,0:T(8,128)(2,1)S(1)} %bitcast.15, bf16[64,128]{1,0:T(8,128)(2,1)S(1)} %bitcast.19, ...), custom_call_target="tpu_custom_call" | custom-call | flops 268435456 | bytes 2097152 | tf_op jit(solution)/shard_map/input/pallas_call | solution.py:322
  153.0 0.9 collective-permute-done.1
  153.9 0.4 collective-permute-start.2
  154.2 3.9 %input.3 = bf16[32,256,128]{2,1,0:T(8,128)(2,1)} custom-call(bf16[32,256,128]{2,1,0:T(8,128)(2,1)} %pair_hbm.3, bf16[32,256,256]{2,1,0:T(8,128)(2,1)S(1)} %get-tuple-element.22.grads_ref, bf16[64,128]{1,0:T(8,128)(2,1)S(1)} %bitcast.12, bf16[64,128]{1,0:T(8,128)(2,1)S(1)} %bitcast.16, bf16[64,128]{1,0:T(8,128)(2,1)S(1)} %bitcast.20, ...), custom_call_target="tpu_custom_call", output_to_operand_aliasing={{}: (6, {})} | custom-call | flops 268435456 | bytes 2097152 | tf_op jit(solution)/shard_map/input/pallas_call | solution.py:322
  158.2 0.0 collective-permute-done.2
  158.2 1.2 collective-permute-start.3
  159.4 3.2 %collective-permute-done.3 = f32[128,128]{1,0:T(8,128)S(1)} collective-permute-done((f32[128,128]{1,0:T(8,128)S(1)}, f32[128,128]{1,0:T(8,128)S(1)}, u32[]{:S(2)}, u32[]{:S(2)}) %collective-permute-start.3) | collective-permute-done | bytes 65568 | tf_op jit(solution)/shard_map/ppermute | solution.py:347
  162.6 1.4 collective-permute-start.4
  164.0 2.9 %collective-permute-done.4 = f32[128,128]{1,0:T(8,128)S(1)} collective-permute-done((f32[128,128]{1,0:T(8,128)S(1)}, f32[128,128]{1,0:T(8,128)S(1)}, u32[]{:S(2)}, u32[]{:S(2)}) %collective-permute-start.4) | collective-permute-done | bytes 65568 | tf_op jit(solution)/shard_map/ppermute | solution.py:347
  166.9 0.1 collective-permute-start.5
  167.0 1.2 collective-permute-done.5.other_ref
  168.2 0.7 finish.1
  (5 shorter events, 0.0 us)
Async XLA Ops:
  0.6 33.5 %all-to-all-start = ((bf16[32,2,32,256]{3,2,1,0:T(8,128)(2,1)}), bf16[32,2,32,256]{3,2,1,0:T(8,128)(2,1)S(1)}, u32[]{:S(2)}, u32[]{:S(2)}) async-start(bf16[32,2,32,256]{3,2,1,0:T(8,128)(2,1)} %bitcast.25), calls=%async_computation | async-start | bytes 2097152 | tf_op jit(solution)/shard_map/all_to_all | solution.py:268
  88.3 52.2 %copy-start = (bf16[128,64]{0,1:T(8,128)(2,1)S(1)}, bf16[128,64]{0,1:T(8,128)(2,1)}, u32[]{:S(2)}) copy-start(bf16[128,64]{0,1:T(8,128)(2,1)} %param.8) | copy-start | bytes 49156
  88.3 52.2 %copy-start.1 = (bf16[128,64]{0,1:T(8,128)(2,1)S(1)}, bf16[128,64]{0,1:T(8,128)(2,1)}, u32[]{:S(2)}) copy-start(bf16[128,64]{0,1:T(8,128)(2,1)} %param.9) | copy-start | bytes 49156
  88.3 52.2 %copy-start.2 = (bf16[128,64]{0,1:T(8,128)(2,1)S(1)}, bf16[128,64]{0,1:T(8,128)(2,1)}, u32[]{:S(2)}) copy-start(bf16[128,64]{0,1:T(8,128)(2,1)} %param.10) | copy-start | bytes 49156
  88.3 52.2 %copy-start.3 = (bf16[128,64]{0,1:T(8,128)(2,1)S(1)}, bf16[128,64]{0,1:T(8,128)(2,1)}, u32[]{:S(2)}) copy-start(bf16[128,64]{0,1:T(8,128)(2,1)} %param.11) | copy-start | bytes 49156
  145.9 1.3 collective-permute-start
  147.2 6.6 %collective-permute-start.1 = (f32[128,128]{1,0:T(8,128)S(1)}, f32[128,128]{1,0:T(8,128)S(1)}, u32[]{:S(2)}, u32[]{:S(2)}) collective-permute-start(f32[128,128]{1,0:T(8,128)S(1)} %add.15), channel_id=1, source_target_pairs={{0,16},{2,18},{4,20},{6,22},{8,24},{10,26},{12,28},{14,30},{16,0},... | collective-permute-start | bytes 196616 | tf_op jit(solution)/shard_map/ppermute | solution.py:347
  153.9 4.3 %collective-permute-start.2 = (f32[128,128]{1,0:T(8,128)S(1)}, f32[128,128]{1,0:T(8,128)S(1)}, u32[]{:S(2)}, u32[]{:S(2)}) collective-permute-start(f32[128,128]{1,0:T(8,128)S(1)} %add.16), channel_id=1, source_target_pairs={{0,8},{2,10},{4,12},{6,14},{8,0},{10,2},{12,4},{14,6},{16,24},{18,... | collective-permute-start | bytes 196616 | tf_op jit(solution)/shard_map/ppermute | solution.py:347
  158.2 4.3 %collective-permute-start.3 = (f32[128,128]{1,0:T(8,128)S(1)}, f32[128,128]{1,0:T(8,128)S(1)}, u32[]{:S(2)}, u32[]{:S(2)}) collective-permute-start(f32[128,128]{1,0:T(8,128)S(1)} %add.17), channel_id=1, source_target_pairs={{0,4},{2,6},{4,0},{6,2},{8,12},{10,14},{12,8},{14,10},{16,20},{18,... | collective-permute-start | bytes 196616 | tf_op jit(solution)/shard_map/ppermute | solution.py:347
  162.6 4.3 %collective-permute-start.4 = (f32[128,128]{1,0:T(8,128)S(1)}, f32[128,128]{1,0:T(8,128)S(1)}, u32[]{:S(2)}, u32[]{:S(2)}) collective-permute-start(f32[128,128]{1,0:T(8,128)S(1)} %add.18), channel_id=1, source_target_pairs={{0,1},{1,0},{2,3},{3,2},{4,5},{5,4},{6,7},{7,6},{8,9},{9,8},{10,11... | collective-permute-start | bytes 196616 | tf_op jit(solution)/shard_map/ppermute | solution.py:347
  166.9 1.3 collective-permute-start.5

commit v9 on v8

--- a/solution.py
+++ b/solution.py
@@ -116,11 +116,33 @@
     return jnp.concatenate([ref[i, at, :] for i in range(ref.shape[0])], axis=1)
 
 
-def before_kernel(own, pair_ref, wl, wlg, wr, wrg, out_ref, normed_ref, w_ref, rows_ref):
-    stack_weights((wl, wlg, wr, wrg), w_ref)
+def before_kernel(own, pair_hbm, cot_hbm, wl, wlg, wr, wrg, out_ref, normed_hbm, *scratch):
+    w_ref, rows_ref, pair_ref, normed_ref, in_sems, out_sems, w_sems, cot_sem = scratch
     h = wl.shape[0]
     rows = pair_ref.shape[0]
     pitch = rows + 1
+    parts = in_sems.shape[0]
+    count = rows // parts
+
+    def come(part):
+        at = pl.ds(part * count, count)
+        return pltpu.make_async_copy(pair_hbm.at[at], pair_ref.at[at], in_sems.at[part])
+
+    def leave(part):
+        at = pl.ds(part * count, count)
+        return pltpu.make_async_copy(normed_ref.at[at], normed_hbm.at[at], out_sems.at[part])
+
+    def weight(i, w):
+        return pltpu.make_async_copy(w, w_ref.at[pl.ds(i * h, h)], w_sems.at[i])
+
+    for part in range(parts):
+        come(part).start()
+    for i, w in enumerate((wl, wlg, wr, wrg)):
+        weight(i, w).start()
+    cot = pltpu.make_async_copy(cot_hbm, out_ref.at[:, pl.ds(0, own)], cot_sem)
+    cot.start()
+    for i, w in enumerate((wl, wlg, wr, wrg)):
+        weight(i, w).wait()
 
     def one_row(r, carry):
         normed = layer_norm(pair_ref[r])[0].astype(BF16)
@@ -130,27 +152,34 @@
         put_lanes(rows_ref, pl.ds(r + h * pitch, h, stride=pitch), s_right * q_right)
         return carry
 
-    lax.fori_loop(0, rows, one_row, 0, unroll=4)
+    for part in range(parts):
+        come(part).wait()
+        lax.fori_loop(part * count, (part + 1) * count, one_row, 0, unroll=4)
+        leave(part).start()
     for channel in range(h):
-        to, slot = channel // own, (channel % own) * 2
         for side in range(2):
             line = get_lanes(rows_ref, pl.ds((side * h + channel) * pitch, rows))
-            out_ref[to, slot + side] = line.astype(BF16)
-
-
-def triangle_kernel(rows, cols, cot_ref, in_ref, out_ref, g_ref, l_ref, r_ref):
+            out_ref[channel // own, (1 + side) * own + channel % own] = line.astype(BF16)
+    for part in range(parts):
+        leave(part).wait()
+    cot.wait()
+
+
+def triangle_kernel(rows, cols, in_ref, out_ref, g_ref, l_ref, r_ref):
     r, c = in_ref.shape[2:]
-    for a in range(rows):
-        for b in range(cols):
-            at = (pl.ds(a * r, r), pl.ds(b * c, c))
-            g_ref[at] = cot_ref[a * cols + b, 0]
-            l_ref[at] = in_ref[a * cols + b, 0]
-            r_ref[at] = in_ref[a * cols + b, 1]
-    for i, (dims, ref) in enumerate(((NN, r_ref), (TN, l_ref))):
-        d = dot(g_ref[...], ref[...], dims).astype(BF16)
-        for a in range(rows):
-            for b in range(cols):
-                out_ref[a * cols + b, i] = d[a * r : (a + 1) * r, b * c : (b + 1) * c]
+    own = g_ref.shape[0]
+    for n in range(own):
+        for i, ref in enumerate((g_ref, l_ref, r_ref)):
+            for a in range(rows):
+                for b in range(cols):
+                    block = in_ref[a * cols + b, i * own + n]
+                    ref[n, pl.ds(a * r, r), pl.ds(b * c, c)] = block
+        for i, (dims, ref) in enumerate(((NN, r_ref), (TN, l_ref))):
+            d = dot(g_ref[n], ref[n], dims).astype(BF16)
+            for a in range(rows):
+                for b in range(cols):
+                    block = d[a * r : (a + 1) * r, b * c : (b + 1) * c]
+                    out_ref[a * cols + b, n * 2 + i] = block
 
 
 def gates_kernel(own, normed_hbm, d_ref, wl, wlg, wr, wrg, grads_ref, kept_ref, sent_ref, *scratch):
@@ -244,17 +273,20 @@
     hidden, r, c = cotangent.shape
     dim = pair.shape[2]
     own = hidden // devices
-    block = 16 if r % 16 == 0 else r
     pieces = 2 if r % 2 == 0 else 1
+    parts = 4 if r % 16 == 0 else 1
     weights = [w.T for w in weights]
-    whole = pl.BlockSpec((hidden, dim), lambda i: (0, 0))
-    tile = pl.BlockSpec((block, c, dim), lambda i: (i, 0, 0))
+    vmem = pl.BlockSpec(memory_space=pltpu.VMEM)
+    hbm = pl.BlockSpec(memory_space=pltpu.HBM)
     exchange = functools.partial(
         lax.all_to_all, axis_name=("row", "col"), split_axis=0, concat_axis=0, tiled=True
     )
     stacked = pltpu.VMEM((4 * hidden, dim), BF16)
     lanes = min(c, 128)
-    rows_scratch = pltpu.VMEM((c // lanes, (2 * hidden + 1) * (block + 1), lanes), F32)
+    rows_scratch = pltpu.VMEM((c // lanes, (2 * hidden + 1) * (r + 1), lanes), F32)
+    columns = r * c
+    n_i, n_k = rows * r, cols * c
+    pair = pltpu.with_memory_space_constraint(pair, pltpu.HBM)
 
     def cost(flops, *arrays):
         moved = sum(a.size * a.dtype.itemsize for a in arrays)
@@ -263,42 +295,43 @@
     def memory(mib):
         return pltpu.CompilerParams(vmem_limit_bytes=mib * 2**20)
 
-    columns = r * c
-    lr_shape = jax.ShapeDtypeStruct((devices, 2 * own, r, c), BF16)
-    g_all = exchange(cotangent.reshape(devices, own, r, c))
     normed_shape = jax.ShapeDtypeStruct((r, dim, c), BF16)
     sent, normed = pl.pallas_call(
         functools.partial(before_kernel, own),
-        grid=(r // block,),
-        in_specs=[tile] + [whole] * 4,
-        out_specs=[
-            pl.BlockSpec((devices, 2 * own, block, c), lambda i: (0, 0, i, 0)),
-            pl.BlockSpec((block, dim, c), lambda i: (i, 0, 0)),
+        in_specs=[hbm] * 6,
+        out_specs=[vmem, hbm],
+        out_shape=[
+            jax.ShapeDtypeStruct((devices, 3 * own, r, c), BF16),
+            pltpu.HBM(normed_shape.shape, BF16),
         ],
-        out_shape=[lr_shape, normed_shape],
-        scratch_shapes=[stacked, rows_scratch],
-        compiler_params=memory(60),
-        cost_estimate=cost(8 * hidden * dim * columns, pair, lr_shape),
+        scratch_shapes=[
+            stacked,
+            rows_scratch,
+            pltpu.VMEM(pair.shape, BF16),
+            pltpu.VMEM(normed_shape.shape, BF16),
+            pltpu.SemaphoreType.DMA((parts,)),
+            pltpu.SemaphoreType.DMA((parts,)),
+            pltpu.SemaphoreType.DMA((4,)),
+            pltpu.SemaphoreType.DMA,
+        ],
+        compiler_params=memory(24),
         name="before",
-    )(pair, *weights)
-
-    n_i, n_k = rows * r, cols * c
+    )(
+        pair,
+        pltpu.with_memory_space_constraint(cotangent.reshape(devices, own, r, c), pltpu.HBM),
+        *(pltpu.with_memory_space_constraint(w, pltpu.HBM) for w in weights),
+    )
+
     sent = pl.pallas_call(
         functools.partial(triangle_kernel, rows, cols),
-        grid=(own,),
-        in_specs=[
-            pl.BlockSpec((devices, 1, r, c), lambda i: (0, i, 0, 0)),
-            pl.BlockSpec((devices, 2, r, c), lambda i: (0, i, 0, 0)),
-        ],
-        out_specs=pl.BlockSpec((devices, 2, r, c), lambda i: (0, i, 0, 0)),
-        out_shape=lr_shape,
-        scratch_shapes=[pltpu.VMEM((n_i, n_k), BF16)] * 3,
+        in_specs=[vmem],
+        out_specs=vmem,
+        out_shape=jax.ShapeDtypeStruct((devices, 2 * own, r, c), BF16),
+        scratch_shapes=[pltpu.VMEM((own, n_i, n_k), BF16)] * 3,
         compiler_params=memory(32),
         name="triangle",
-    )(g_all, exchange(sent))
-
-    vmem = pl.BlockSpec(memory_space=pltpu.VMEM)
-    hbm = pl.BlockSpec(memory_space=pltpu.HBM)
+    )(exchange(sent))
+
     half_shape = jax.ShapeDtypeStruct((2 * hidden, dim), F32)
     grads, kept, given = pl.pallas_call(
         functools.partial(gates_kernel, own),
@@ -308,7 +341,7 @@
         scratch_shapes=[
             stacked,
             pltpu.VMEM((4 * hidden, dim), F32),
-            pltpu.VMEM((c // lanes, (2 * hidden + 1) * (r + 1), lanes), F32),
+            rows_scratch,
             pltpu.VMEM(normed_shape.shape, BF16),
             pltpu.SemaphoreType.DMA,
         ],
@@ -335,7 +368,7 @@
             compiler_params=memory(16),
             cost_estimate=cost(8 * hidden * dim * columns // pieces, pair),
             name="input",
-        )(pltpu.with_memory_space_constraint(pair, pltpu.HBM), grads, *weights, *held)
+        )(pair, grads, *weights, *held)
 
     steps = [("row", rows, 1 << i) for i in range(1, rows.bit_length() - 1)][::-1]
     steps += [("col", cols, 1 << i) for i in range(cols.bit_length() - 1)]

time: 169 us -> 167 us (0.988)
  blocking collectives: 105 us -> 130 us
  waiting for transfers between devices: 28.7 us -> 9.41 us
  starting transfers between devices: 12.2 us -> 4.96 us
    all_to_all x2, blocking collectives: 105 us -> 130 us  [channel_shards(): exchange(sent)]
    all_to_all x1 -> x0, waiting for transfers between devices: 19.3 us -> none  [channel_shards(): g_all = exchange(cotangent.reshape(devices, own, r, c))]
    all_to_all x1 -> x0, starting transfers between devices: 7.3 us -> none  [channel_shards(): g_all = exchange(cotangent.reshape(devices, own, r, c))]
  transfers between devices with their start and end apart: 7 -> 6, of which waited for: 6 -> 5; matrix products, arithmetic and copies ran while one was open for 0% -> 0% of each run, Pallas kernels for 9% -> 5%
where the time goes in v9:
time: 167 us
  blocking collectives  130 us (78%)
  Pallas kernels  21.3 us (13%)
  waiting for transfers between devices  9.41 us (6%)
  starting transfers between devices  4.96 us (3%)
    all_to_all x2, blocking collectives, channel_shards(): exchange(sent)  130 us
    pallas_call x2, Pallas kernels, input_piece(): pl.pallas_call(functools.partial(input_kernel, piece * count), in_specs=[...  7.87 us
    ppermute x4, waiting for transfers between devices, channel_shards(): other = lax.ppermute(mine, axis, [(i, i ^ step) for i in range(size)])  6.94 us
    pallas_call x1, Pallas kernels, channel_shards(): pl.pallas_call(functools.partial(before_kernel, own), in_specs=[hbm] * 6,...  6.15 us
    pallas_call x1, Pallas kernels, channel_shards(): pl.pallas_call(functools.partial(gates_kernel, own), in_specs=[hbm] + [vm...  5.34 us
    ppermute x4, starting transfers between devices, channel_shards(): other = lax.ppermute(mine, axis, [(i, i ^ step) for i in range(size)])  4.8 us
  transfers between devices with their start and end apart: 6, of which 5 were waited for; matrix products, arithmetic and copies ran while one was open for 0% of the time, Pallas kernels for 5%

profile of v9, /device:TPU:0, one launch (start us, length us, event | category | flops | bytes accessed | tf_op | source)
XLA Modules:
  0.0 166.9 jit_solution(11304797367460233549)
XLA Ops:
  0.6 6.1 %before.1 = (bf16[32,6,32,256]{3,2,1,0:T(8,128)(2,1)S(1)}, bf16[32,128,256]{2,1,0:T(8,128)(2,1)}) custom-call(bf16[32,256,128]{2,1,0:T(8,128)(2,1)} %pair_hbm.5, bf16[32,2,32,256]{3,2,1,0:T(8,128)(2,1)} %bitcast.25, bf16[64,128]{1,0:T(8,128)(2,1)} %bitcast.9, bf16[64,128]{1,0:T(8,128)(2,1)} %bitcast.13, bf16[64,128]{1,0:T(8,128)(2,1)} %bitcast.17, ...), custom_call_target="tpu_custom_call" | custom-call | tf_op jit(solution)/shard_map/before/pallas_call | solution.py:299
  6.8 78.3 %all_to_all.10.in_ref = bf16[32,6,32,256]{3,2,1,0:T(8,128)(2,1)S(1)} all-to-all(bf16[32,6,32,256]{3,2,1,0:T(8,128)(2,1)S(1)} %get-tuple-element.19), channel_id=1, replica_groups=mesh['row'=16,'col'=2] {'row','col'}, dimensions={0} | all-to-all | bytes 6291456 | tf_op jit(solution)/shard_map/all_to_all | solution.py:333
  85.1 1.3 triangle.1
  86.4 0.0 copy-start
  86.4 0.0 copy-start.1
  86.4 0.0 copy-start.2
  86.4 0.0 copy-start.3
  86.4 52.2 %all_to_all.11.d_ref = bf16[32,4,32,256]{3,2,1,0:T(8,128)(2,1)S(1)} all-to-all(bf16[32,4,32,256]{3,2,1,0:T(8,128)(2,1)S(1)} %triangle.1), channel_id=1, replica_groups=mesh['row'=16,'col'=2] {'row','col'}, dimensions={0} | all-to-all | bytes 4194304 | tf_op jit(solution)/shard_map/all_to_all | solution.py:350
  138.6 0.0 copy-done
  138.6 0.0 copy-done.1
  138.6 0.0 copy-done.2
  138.6 0.0 copy-done.3
  138.6 5.3 %gates.1 = (bf16[32,256,256]{2,1,0:T(8,128)(2,1)S(1)}, f32[128,128]{1,0:T(8,128)S(1)}, f32[128,128]{1,0:T(8,128)S(1)}) custom-call(bf16[32,128,256]{2,1,0:T(8,128)(2,1)} %get-tuple-element.18.normed_hbm, bf16[32,4,32,256]{3,2,1,0:T(8,128)(2,1)S(1)} %all_to_all.11.d_ref, bf16[64,128]{1,0:T(8,128)(2,1)S(1)} %bitcast.10, bf16[64,128]{1,0:T(8,128)(2,1)S(1)} %bitcast.14, ...), custom_call_target="tpu_custom_call" | custom-call | tf_op jit(solution)/shard_map/gates/pallas_call | solution.py:336
  143.9 0.1 collective-permute-start
  144.0 1.2 collective-permute-done
  145.3 1.8 %collective-permute-start.1 = (f32[128,128]{1,0:T(8,128)S(1)}, f32[128,128]{1,0:T(8,128)S(1)}, u32[]{:S(2)}, u32[]{:S(2)}) collective-permute-start(f32[128,128]{1,0:T(8,128)S(1)} %add.15), channel_id=1, source_target_pairs={{0,16},{2,18},{4,20},{6,22},{8,24},{10,26},{12,28},{14,30},{16,0},... | collective-permute-start | bytes 196616 | tf_op jit(solution)/shard_map/ppermute | solution.py:380
  147.1 3.9 %input.2.refs_0_ = bf16[32,256,128]{2,1,0:T(8,128)(2,1)} custom-call(bf16[32,256,128]{2,1,0:T(8,128)(2,1)} %pair_hbm.5, bf16[32,256,256]{2,1,0:T(8,128)(2,1)S(1)} %get-tuple-element.22.grads_ref, bf16[64,128]{1,0:T(8,128)(2,1)S(1)} %bitcast.11, bf16[64,128]{1,0:T(8,128)(2,1)S(1)} %bitcast.15, bf16[64,128]{1,0:T(8,128)(2,1)S(1)} %bitcast.19, ...), custom_call_target="tpu_custom_call" | custom-call | flops 268435456 | bytes 2097152 | tf_op jit(solution)/shard_map/input/pallas_call | solution.py:355
  151.0 0.9 collective-permute-done.1
  151.9 0.4 collective-permute-start.2
  152.3 3.9 %input.3 = bf16[32,256,128]{2,1,0:T(8,128)(2,1)} custom-call(bf16[32,256,128]{2,1,0:T(8,128)(2,1)} %pair_hbm.5, bf16[32,256,256]{2,1,0:T(8,128)(2,1)S(1)} %get-tuple-element.22.grads_ref, bf16[64,128]{1,0:T(8,128)(2,1)S(1)} %bitcast.12, bf16[64,128]{1,0:T(8,128)(2,1)S(1)} %bitcast.16, bf16[64,128]{1,0:T(8,128)(2,1)S(1)} %bitcast.20, ...), custom_call_target="tpu_custom_call", output_to_operand_aliasing={{}: (6, {})} | custom-call | flops 268435456 | bytes 2097152 | tf_op jit(solution)/shard_map/input/pallas_call | solution.py:355
  156.2 0.0 collective-permute-done.2
  156.3 1.2 collective-permute-start.3
  157.4 3.2 %collective-permute-done.3 = f32[128,128]{1,0:T(8,128)S(1)} collective-permute-done((f32[128,128]{1,0:T(8,128)S(1)}, f32[128,128]{1,0:T(8,128)S(1)}, u32[]{:S(2)}, u32[]{:S(2)}) %collective-permute-start.3) | collective-permute-done | bytes 65568 | tf_op jit(solution)/shard_map/ppermute | solution.py:380
  160.6 1.4 collective-permute-start.4
  162.0 2.9 %collective-permute-done.4 = f32[128,128]{1,0:T(8,128)S(1)} collective-permute-done((f32[128,128]{1,0:T(8,128)S(1)}, f32[128,128]{1,0:T(8,128)S(1)}, u32[]{:S(2)}, u32[]{:S(2)}) %collective-permute-start.4) | collective-permute-done | bytes 65568 | tf_op jit(solution)/shard_map/ppermute | solution.py:380
  165.0 0.1 collective-permute-start.5
  165.0 1.2 collective-permute-done.5.other_ref
  166.3 0.7 finish.1
  (5 shorter events, 0.0 us)
Async XLA Ops:
  86.4 52.2 %copy-start = (bf16[128,64]{0,1:T(8,128)(2,1)S(1)}, bf16[128,64]{0,1:T(8,128)(2,1)}, u32[]{:S(2)}) copy-start(bf16[128,64]{0,1:T(8,128)(2,1)} %param.8) | copy-start | bytes 49156
  86.4 52.2 %copy-start.1 = (bf16[128,64]{0,1:T(8,128)(2,1)S(1)}, bf16[128,64]{0,1:T(8,128)(2,1)}, u32[]{:S(2)}) copy-start(bf16[128,64]{0,1:T(8,128)(2,1)} %param.9) | copy-start | bytes 49156
  86.4 52.2 %copy-start.2 = (bf16[128,64]{0,1:T(8,128)(2,1)S(1)}, bf16[128,64]{0,1:T(8,128)(2,1)}, u32[]{:S(2)}) copy-start(bf16[128,64]{0,1:T(8,128)(2,1)} %param.10) | copy-start | bytes 49156
  86.4 52.2 %copy-start.3 = (bf16[128,64]{0,1:T(8,128)(2,1)S(1)}, bf16[128,64]{0,1:T(8,128)(2,1)}, u32[]{:S(2)}) copy-start(bf16[128,64]{0,1:T(8,128)(2,1)} %param.11) | copy-start | bytes 49156
  143.9 1.3 collective-permute-start
  145.3 6.6 %collective-permute-start.1 = (f32[128,128]{1,0:T(8,128)S(1)}, f32[128,128]{1,0:T(8,128)S(1)}, u32[]{:S(2)}, u32[]{:S(2)}) collective-permute-start(f32[128,128]{1,0:T(8,128)S(1)} %add.15), channel_id=1, source_target_pairs={{0,16},{2,18},{4,20},{6,22},{8,24},{10,26},{12,28},{14,30},{16,0},... | collective-permute-start | bytes 196616 | tf_op jit(solution)/shard_map/ppermute | solution.py:380
  151.9 4.3 %collective-permute-start.2 = (f32[128,128]{1,0:T(8,128)S(1)}, f32[128,128]{1,0:T(8,128)S(1)}, u32[]{:S(2)}, u32[]{:S(2)}) collective-permute-start(f32[128,128]{1,0:T(8,128)S(1)} %add.16), channel_id=1, source_target_pairs={{0,8},{2,10},{4,12},{6,14},{8,0},{10,2},{12,4},{14,6},{16,24},{18,... | collective-permute-start | bytes 196616 | tf_op jit(solution)/shard_map/ppermute | solution.py:380
  156.3 4.3 %collective-permute-start.3 = (f32[128,128]{1,0:T(8,128)S(1)}, f32[128,128]{1,0:T(8,128)S(1)}, u32[]{:S(2)}, u32[]{:S(2)}) collective-permute-start(f32[128,128]{1,0:T(8,128)S(1)} %add.17), channel_id=1, source_target_pairs={{0,4},{2,6},{4,0},{6,2},{8,12},{10,14},{12,8},{14,10},{16,20},{18,... | collective-permute-start | bytes 196616 | tf_op jit(solution)/shard_map/ppermute | solution.py:380
  160.6 4.3 %collective-permute-start.4 = (f32[128,128]{1,0:T(8,128)S(1)}, f32[128,128]{1,0:T(8,128)S(1)}, u32[]{:S(2)}, u32[]{:S(2)}) collective-permute-start(f32[128,128]{1,0:T(8,128)S(1)} %add.18), channel_id=1, source_target_pairs={{0,1},{1,0},{2,3},{3,2},{4,5},{5,4},{6,7},{7,6},{8,9},{9,8},{10,11... | collective-permute-start | bytes 196616 | tf_op jit(solution)/shard_map/ppermute | solution.py:380
  165.0 1.3 collective-permute-start.5

commit v10 on v9

--- a/solution.py
+++ b/solution.py
@@ -91,8 +91,13 @@
         w_ref[pl.ds(i * h, h), :] = ref[...]
 
 
+def identity(n):
+    row = lax.broadcasted_iota(jnp.int32, (n, n), 0)
+    return (row == lax.broadcasted_iota(jnp.int32, (n, n), 1)).astype(BF16)
+
+
 def layer_norm(x):
-    x = x.T.astype(F32)
+    x = dot(identity(x.shape[1]), x, NT)
     centered = x - jnp.mean(x, axis=0, keepdims=True)
     variance = jnp.mean(centered * centered, axis=0, keepdims=True)
     inverse_scale = lax.rsqrt(variance + 1e-05)

time: 167 us -> 170 us (1.018)
  Pallas kernels: 21.3 us -> 24.2 us
    pallas_call x1, Pallas kernels: 6.15 us -> 8.41 us  [channel_shards(): pl.pallas_call(functools.partial(before_kernel, own), in_specs=[hbm] * 6,...]
where the time goes in v10:
time: 170 us
  blocking collectives  130 us (76%)
  Pallas kernels  24.2 us (14%)
  waiting for transfers between devices  9.43 us (6%)
  starting transfers between devices  4.56 us (3%)
    all_to_all x2, blocking collectives, channel_shards(): exchange(sent)  130 us
    pallas_call x2, Pallas kernels, input_piece(): pl.pallas_call(functools.partial(input_kernel, piece * count), in_specs=[...  8.55 us
    pallas_call x1, Pallas kernels, channel_shards(): pl.pallas_call(functools.partial(before_kernel, own), in_specs=[hbm] * 6,...  8.41 us
    ppermute x4, waiting for transfers between devices, channel_shards(): other = lax.ppermute(mine, axis, [(i, i ^ step) for i in range(size)])  6.95 us
    pallas_call x1, Pallas kernels, channel_shards(): pl.pallas_call(functools.partial(gates_kernel, own), in_specs=[hbm] + [vm...  5.34 us
    ppermute x4, starting transfers between devices, channel_shards(): other = lax.ppermute(mine, axis, [(i, i ^ step) for i in range(size)])  4.42 us
  transfers between devices with their start and end apart: 6, of which 5 were waited for; matrix products, arithmetic and copies ran while one was open for 0% of the time, Pallas kernels for 5%

profile of v10, /device:TPU:0, one launch (start us, length us, event | category | flops | bytes accessed | tf_op | source)
XLA Modules:
  0.0 169.5 jit_solution(3741581133040515566)
XLA Ops:
  0.6 8.4 %before.1 = (bf16[32,6,32,256]{3,2,1,0:T(8,128)(2,1)S(1)}, bf16[32,128,256]{2,1,0:T(8,128)(2,1)}) custom-call(bf16[32,256,128]{2,1,0:T(8,128)(2,1)} %pair_hbm.5, bf16[32,2,32,256]{3,2,1,0:T(8,128)(2,1)} %bitcast.25, bf16[64,128]{1,0:T(8,128)(2,1)} %bitcast.9, bf16[64,128]{1,0:T(8,128)(2,1)} %bitcast.13, bf16[64,128]{1,0:T(8,128)(2,1)} %bitcast.17, ...), custom_call_target="tpu_custom_call" | custom-call | tf_op jit(solution)/shard_map/before/pallas_call | solution.py:304
  9.1 78.3 %all_to_all.10.in_ref = bf16[32,6,32,256]{3,2,1,0:T(8,128)(2,1)S(1)} all-to-all(bf16[32,6,32,256]{3,2,1,0:T(8,128)(2,1)S(1)} %get-tuple-element.19), channel_id=1, replica_groups=mesh['row'=16,'col'=2] {'row','col'}, dimensions={0} | all-to-all | bytes 6291456 | tf_op jit(solution)/shard_map/all_to_all | solution.py:338
  87.4 1.3 triangle.1
  88.6 0.0 copy-start
  88.6 0.0 copy-start.1
  88.6 0.0 copy-start.2
  88.7 0.0 copy-start.3
  88.7 52.2 %all_to_all.11.d_ref = bf16[32,4,32,256]{3,2,1,0:T(8,128)(2,1)S(1)} all-to-all(bf16[32,4,32,256]{3,2,1,0:T(8,128)(2,1)S(1)} %triangle.1), channel_id=1, replica_groups=mesh['row'=16,'col'=2] {'row','col'}, dimensions={0} | all-to-all | bytes 4194304 | tf_op jit(solution)/shard_map/all_to_all | solution.py:355
  140.8 0.0 copy-done
  140.8 0.0 copy-done.1
  140.8 0.0 copy-done.2
  140.8 0.0 copy-done.3
  140.9 5.3 %gates.1 = (bf16[32,256,256]{2,1,0:T(8,128)(2,1)S(1)}, f32[128,128]{1,0:T(8,128)S(1)}, f32[128,128]{1,0:T(8,128)S(1)}) custom-call(bf16[32,128,256]{2,1,0:T(8,128)(2,1)} %get-tuple-element.18.normed_hbm, bf16[32,4,32,256]{3,2,1,0:T(8,128)(2,1)S(1)} %all_to_all.11.d_ref, bf16[64,128]{1,0:T(8,128)(2,1)S(1)} %bitcast.10, bf16[64,128]{1,0:T(8,128)(2,1)S(1)} %bitcast.14, ...), custom_call_target="tpu_custom_call" | custom-call | tf_op jit(solution)/shard_map/gates/pallas_call | solution.py:341
  146.2 0.1 collective-permute-start
  146.3 1.2 collective-permute-done
  147.5 1.8 %collective-permute-start.1 = (f32[128,128]{1,0:T(8,128)S(1)}, f32[128,128]{1,0:T(8,128)S(1)}, u32[]{:S(2)}, u32[]{:S(2)}) collective-permute-start(f32[128,128]{1,0:T(8,128)S(1)} %add.15), channel_id=1, source_target_pairs={{0,16},{2,18},{4,20},{6,22},{8,24},{10,26},{12,28},{14,30},{16,0},... | collective-permute-start | bytes 196616 | tf_op jit(solution)/shard_map/ppermute | solution.py:385
  149.4 4.3 %input.2.refs_0_ = bf16[32,256,128]{2,1,0:T(8,128)(2,1)} custom-call(bf16[32,256,128]{2,1,0:T(8,128)(2,1)} %pair_hbm.5, bf16[32,256,256]{2,1,0:T(8,128)(2,1)S(1)} %get-tuple-element.22.grads_ref, bf16[64,128]{1,0:T(8,128)(2,1)S(1)} %bitcast.11, bf16[64,128]{1,0:T(8,128)(2,1)S(1)} %bitcast.15, bf16[64,128]{1,0:T(8,128)(2,1)S(1)} %bitcast.19, ...), custom_call_target="tpu_custom_call" | custom-call | flops 268435456 | bytes 2097152 | tf_op jit(solution)/shard_map/input/pallas_call | solution.py:360
  153.6 0.5 collective-permute-done.1
  154.2 0.4 collective-permute-start.2
  154.5 4.3 %input.3 = bf16[32,256,128]{2,1,0:T(8,128)(2,1)} custom-call(bf16[32,256,128]{2,1,0:T(8,128)(2,1)} %pair_hbm.5, bf16[32,256,256]{2,1,0:T(8,128)(2,1)S(1)} %get-tuple-element.22.grads_ref, bf16[64,128]{1,0:T(8,128)(2,1)S(1)} %bitcast.12, bf16[64,128]{1,0:T(8,128)(2,1)S(1)} %bitcast.16, bf16[64,128]{1,0:T(8,128)(2,1)S(1)} %bitcast.20, ...), custom_call_target="tpu_custom_call", output_to_operand_aliasing={{}: (6, {})} | custom-call | flops 268435456 | bytes 2097152 | tf_op jit(solution)/shard_map/input/pallas_call | solution.py:360
  158.8 0.0 collective-permute-done.2
  158.9 1.1 collective-permute-start.3
  160.0 3.2 %collective-permute-done.3 = f32[128,128]{1,0:T(8,128)S(1)} collective-permute-done((f32[128,128]{1,0:T(8,128)S(1)}, f32[128,128]{1,0:T(8,128)S(1)}, u32[]{:S(2)}, u32[]{:S(2)}) %collective-permute-start.3) | collective-permute-done | bytes 65568 | tf_op jit(solution)/shard_map/ppermute | solution.py:385
  163.2 1.2 collective-permute-start.4
  164.4 3.2 %collective-permute-done.4 = f32[128,128]{1,0:T(8,128)S(1)} collective-permute-done((f32[128,128]{1,0:T(8,128)S(1)}, f32[128,128]{1,0:T(8,128)S(1)}, u32[]{:S(2)}, u32[]{:S(2)}) %collective-permute-start.4) | collective-permute-done | bytes 65568 | tf_op jit(solution)/shard_map/ppermute | solution.py:385
  167.5 0.1 collective-permute-start.5
  167.6 1.2 collective-permute-done.5.other_ref
  168.9 0.7 finish.1
  (5 shorter events, 0.0 us)
Async XLA Ops:
  88.6 52.2 %copy-start = (bf16[128,64]{0,1:T(8,128)(2,1)S(1)}, bf16[128,64]{0,1:T(8,128)(2,1)}, u32[]{:S(2)}) copy-start(bf16[128,64]{0,1:T(8,128)(2,1)} %param.8) | copy-start | bytes 49156
  88.6 52.2 %copy-start.1 = (bf16[128,64]{0,1:T(8,128)(2,1)S(1)}, bf16[128,64]{0,1:T(8,128)(2,1)}, u32[]{:S(2)}) copy-start(bf16[128,64]{0,1:T(8,128)(2,1)} %param.9) | copy-start | bytes 49156
  88.6 52.2 %copy-start.2 = (bf16[128,64]{0,1:T(8,128)(2,1)S(1)}, bf16[128,64]{0,1:T(8,128)(2,1)}, u32[]{:S(2)}) copy-start(bf16[128,64]{0,1:T(8,128)(2,1)} %param.10) | copy-start | bytes 49156
  88.7 52.2 %copy-start.3 = (bf16[128,64]{0,1:T(8,128)(2,1)S(1)}, bf16[128,64]{0,1:T(8,128)(2,1)}, u32[]{:S(2)}) copy-start(bf16[128,64]{0,1:T(8,128)(2,1)} %param.11) | copy-start | bytes 49156
  146.2 1.3 collective-permute-start
  147.5 6.6 %collective-permute-start.1 = (f32[128,128]{1,0:T(8,128)S(1)}, f32[128,128]{1,0:T(8,128)S(1)}, u32[]{:S(2)}, u32[]{:S(2)}) collective-permute-start(f32[128,128]{1,0:T(8,128)S(1)} %add.15), channel_id=1, source_target_pairs={{0,16},{2,18},{4,20},{6,22},{8,24},{10,26},{12,28},{14,30},{16,0},... | collective-permute-start | bytes 196616 | tf_op jit(solution)/shard_map/ppermute | solution.py:385
  154.2 4.6 %collective-permute-start.2 = (f32[128,128]{1,0:T(8,128)S(1)}, f32[128,128]{1,0:T(8,128)S(1)}, u32[]{:S(2)}, u32[]{:S(2)}) collective-permute-start(f32[128,128]{1,0:T(8,128)S(1)} %add.16), channel_id=1, source_target_pairs={{0,8},{2,10},{4,12},{6,14},{8,0},{10,2},{12,4},{14,6},{16,24},{18,... | collective-permute-start | bytes 196616 | tf_op jit(solution)/shard_map/ppermute | solution.py:385
  158.9 4.3 %collective-permute-start.3 = (f32[128,128]{1,0:T(8,128)S(1)}, f32[128,128]{1,0:T(8,128)S(1)}, u32[]{:S(2)}, u32[]{:S(2)}) collective-permute-start(f32[128,128]{1,0:T(8,128)S(1)} %add.17), channel_id=1, source_target_pairs={{0,4},{2,6},{4,0},{6,2},{8,12},{10,14},{12,8},{14,10},{16,20},{18,... | collective-permute-start | bytes 196616 | tf_op jit(solution)/shard_map/ppermute | solution.py:385
  163.2 4.3 %collective-permute-start.4 = (f32[128,128]{1,0:T(8,128)S(1)}, f32[128,128]{1,0:T(8,128)S(1)}, u32[]{:S(2)}, u32[]{:S(2)}) collective-permute-start(f32[128,128]{1,0:T(8,128)S(1)} %add.18), channel_id=1, source_target_pairs={{0,1},{1,0},{2,3},{3,2},{4,5},{5,4},{6,7},{7,6},{8,9},{9,8},{10,11... | collective-permute-start | bytes 196616 | tf_op jit(solution)/shard_map/ppermute | solution.py:385
  167.5 1.3 collective-permute-start.5

commit v11 on v9

--- a/solution.py
+++ b/solution.py
@@ -154,7 +154,7 @@
 
     for part in range(parts):
         come(part).wait()
-        lax.fori_loop(part * count, (part + 1) * count, one_row, 0, unroll=4)
+        lax.fori_loop(part * count, (part + 1) * count, one_row, 0, unroll=8)
         leave(part).start()
     for channel in range(h):
         for side in range(2):
@@ -189,7 +189,7 @@
     h = wl.shape[0]
     rows = grads_ref.shape[0]
     pitch = rows + 1
-    together = 4 if rows % 4 == 0 else 1
+    together = 8 if rows % 8 == 0 else 1
     stack_weights((wl, wlg, wr, wrg), w_ref)
     sums_ref[...] = jnp.zeros_like(sums_ref)
 

time: 167 us -> 166 us (level)
  Pallas kernels: 21.3 us -> 19.6 us
where the time goes in v11:
time: 166 us; the launch traced here: 165 us
  blocking collectives  130 us (78%)
  Pallas kernels  19.6 us (12%)
  waiting for transfers between devices  9.46 us (6%)
  starting transfers between devices  4.91 us (3%)
    all_to_all x2, blocking collectives, channel_shards(): exchange(sent)  130 us
    pallas_call x2, Pallas kernels, input_piece(): pl.pallas_call(functools.partial(input_kernel, piece * count), in_specs=[...  7.87 us
    ppermute x4, waiting for transfers between devices, channel_shards(): other = lax.ppermute(mine, axis, [(i, i ^ step) for i in range(size)])  6.97 us
    pallas_call x1, Pallas kernels, channel_shards(): pl.pallas_call(functools.partial(before_kernel, own), in_specs=[hbm] * 6,...  4.99 us
    pallas_call x1, Pallas kernels, channel_shards(): pl.pallas_call(functools.partial(gates_kernel, own), in_specs=[hbm] + [vm...  4.85 us
    ppermute x4, starting transfers between devices, channel_shards(): other = lax.ppermute(mine, axis, [(i, i ^ step) for i in range(size)])  4.76 us
  transfers between devices with their start and end apart: 6, of which 5 were waited for; matrix products, arithmetic and copies ran while one was open for 0% of the time, Pallas kernels for 5%

profile of v11, /device:TPU:0, one launch (start us, length us, event | category | flops | bytes accessed | tf_op | source)
XLA Modules:
  0.0 165.3 jit_solution(1971856109571514023)
XLA Ops:
  0.6 5.0 %before.1 = (bf16[32,6,32,256]{3,2,1,0:T(8,128)(2,1)S(1)}, bf16[32,128,256]{2,1,0:T(8,128)(2,1)}) custom-call(bf16[32,256,128]{2,1,0:T(8,128)(2,1)} %pair_hbm.5, bf16[32,2,32,256]{3,2,1,0:T(8,128)(2,1)} %bitcast.25, bf16[64,128]{1,0:T(8,128)(2,1)} %bitcast.9, bf16[64,128]{1,0:T(8,128)(2,1)} %bitcast.13, bf16[64,128]{1,0:T(8,128)(2,1)} %bitcast.17, ...), custom_call_target="tpu_custom_call" | custom-call | tf_op jit(solution)/shard_map/before/pallas_call | solution.py:299
  5.6 78.3 %all_to_all.10.in_ref = bf16[32,6,32,256]{3,2,1,0:T(8,128)(2,1)S(1)} all-to-all(bf16[32,6,32,256]{3,2,1,0:T(8,128)(2,1)S(1)} %get-tuple-element.19), channel_id=1, replica_groups=mesh['row'=16,'col'=2] {'row','col'}, dimensions={0} | all-to-all | bytes 6291456 | tf_op jit(solution)/shard_map/all_to_all | solution.py:333
  83.9 1.3 triangle.1
  85.2 0.0 copy-start
  85.2 0.0 copy-start.1
  85.2 0.0 copy-start.2
  85.2 0.0 copy-start.3
  85.2 52.2 %all_to_all.11.d_ref = bf16[32,4,32,256]{3,2,1,0:T(8,128)(2,1)S(1)} all-to-all(bf16[32,4,32,256]{3,2,1,0:T(8,128)(2,1)S(1)} %triangle.1), channel_id=1, replica_groups=mesh['row'=16,'col'=2] {'row','col'}, dimensions={0} | all-to-all | bytes 4194304 | tf_op jit(solution)/shard_map/all_to_all | solution.py:350
  137.4 0.0 copy-done
  137.4 0.0 copy-done.1
  137.4 0.0 copy-done.2
  137.4 0.0 copy-done.3
  137.4 4.8 %gates.1 = (bf16[32,256,256]{2,1,0:T(8,128)(2,1)S(1)}, f32[128,128]{1,0:T(8,128)S(1)}, f32[128,128]{1,0:T(8,128)S(1)}) custom-call(bf16[32,128,256]{2,1,0:T(8,128)(2,1)} %get-tuple-element.18.normed_hbm, bf16[32,4,32,256]{3,2,1,0:T(8,128)(2,1)S(1)} %all_to_all.11.d_ref, bf16[64,128]{1,0:T(8,128)(2,1)S(1)} %bitcast.10, bf16[64,128]{1,0:T(8,128)(2,1)S(1)} %bitcast.14, ...), custom_call_target="tpu_custom_call" | custom-call | tf_op jit(solution)/shard_map/gates/pallas_call | solution.py:336
  142.3 0.1 collective-permute-start
  142.4 1.2 collective-permute-done
  143.6 1.8 %collective-permute-start.1 = (f32[128,128]{1,0:T(8,128)S(1)}, f32[128,128]{1,0:T(8,128)S(1)}, u32[]{:S(2)}, u32[]{:S(2)}) collective-permute-start(f32[128,128]{1,0:T(8,128)S(1)} %add.15), channel_id=1, source_target_pairs={{0,16},{2,18},{4,20},{6,22},{8,24},{10,26},{12,28},{14,30},{16,0},... | collective-permute-start | bytes 196616 | tf_op jit(solution)/shard_map/ppermute | solution.py:380
  145.4 3.9 %input.2.refs_0_ = bf16[32,256,128]{2,1,0:T(8,128)(2,1)} custom-call(bf16[32,256,128]{2,1,0:T(8,128)(2,1)} %pair_hbm.5, bf16[32,256,256]{2,1,0:T(8,128)(2,1)S(1)} %get-tuple-element.22.grads_ref, bf16[64,128]{1,0:T(8,128)(2,1)S(1)} %bitcast.11, bf16[64,128]{1,0:T(8,128)(2,1)S(1)} %bitcast.15, bf16[64,128]{1,0:T(8,128)(2,1)S(1)} %bitcast.19, ...), custom_call_target="tpu_custom_call" | custom-call | flops 268435456 | bytes 2097152 | tf_op jit(solution)/shard_map/input/pallas_call | solution.py:355
  149.4 0.9 collective-permute-done.1
  150.3 0.4 collective-permute-start.2
  150.6 3.9 %input.3 = bf16[32,256,128]{2,1,0:T(8,128)(2,1)} custom-call(bf16[32,256,128]{2,1,0:T(8,128)(2,1)} %pair_hbm.5, bf16[32,256,256]{2,1,0:T(8,128)(2,1)S(1)} %get-tuple-element.22.grads_ref, bf16[64,128]{1,0:T(8,128)(2,1)S(1)} %bitcast.12, bf16[64,128]{1,0:T(8,128)(2,1)S(1)} %bitcast.16, bf16[64,128]{1,0:T(8,128)(2,1)S(1)} %bitcast.20, ...), custom_call_target="tpu_custom_call", output_to_operand_aliasing={{}: (6, {})} | custom-call | flops 268435456 | bytes 2097152 | tf_op jit(solution)/shard_map/input/pallas_call | solution.py:355
  154.6 0.0 collective-permute-done.2
  154.6 1.2 collective-permute-start.3
  155.8 3.2 %collective-permute-done.3 = f32[128,128]{1,0:T(8,128)S(1)} collective-permute-done((f32[128,128]{1,0:T(8,128)S(1)}, f32[128,128]{1,0:T(8,128)S(1)}, u32[]{:S(2)}, u32[]{:S(2)}) %collective-permute-start.3) | collective-permute-done | bytes 65568 | tf_op jit(solution)/shard_map/ppermute | solution.py:380
  158.9 1.4 collective-permute-start.4
  160.4 2.9 %collective-permute-done.4 = f32[128,128]{1,0:T(8,128)S(1)} collective-permute-done((f32[128,128]{1,0:T(8,128)S(1)}, f32[128,128]{1,0:T(8,128)S(1)}, u32[]{:S(2)}, u32[]{:S(2)}) %collective-permute-start.4) | collective-permute-done | bytes 65568 | tf_op jit(solution)/shard_map/ppermute | solution.py:380
  163.3 0.1 collective-permute-start.5
  163.4 1.2 collective-permute-done.5.other_ref
  164.6 0.7 finish.1
  (5 shorter events, 0.0 us)
Async XLA Ops:
  85.2 52.2 %copy-start = (bf16[128,64]{0,1:T(8,128)(2,1)S(1)}, bf16[128,64]{0,1:T(8,128)(2,1)}, u32[]{:S(2)}) copy-start(bf16[128,64]{0,1:T(8,128)(2,1)} %param.8) | copy-start | bytes 49156
  85.2 52.2 %copy-start.1 = (bf16[128,64]{0,1:T(8,128)(2,1)S(1)}, bf16[128,64]{0,1:T(8,128)(2,1)}, u32[]{:S(2)}) copy-start(bf16[128,64]{0,1:T(8,128)(2,1)} %param.9) | copy-start | bytes 49156
  85.2 52.2 %copy-start.2 = (bf16[128,64]{0,1:T(8,128)(2,1)S(1)}, bf16[128,64]{0,1:T(8,128)(2,1)}, u32[]{:S(2)}) copy-start(bf16[128,64]{0,1:T(8,128)(2,1)} %param.10) | copy-start | bytes 49156
  85.2 52.2 %copy-start.3 = (bf16[128,64]{0,1:T(8,128)(2,1)S(1)}, bf16[128,64]{0,1:T(8,128)(2,1)}, u32[]{:S(2)}) copy-start(bf16[128,64]{0,1:T(8,128)(2,1)} %param.11) | copy-start | bytes 49156
  142.3 1.3 collective-permute-start
  143.6 6.6 %collective-permute-start.1 = (f32[128,128]{1,0:T(8,128)S(1)}, f32[128,128]{1,0:T(8,128)S(1)}, u32[]{:S(2)}, u32[]{:S(2)}) collective-permute-start(f32[128,128]{1,0:T(8,128)S(1)} %add.15), channel_id=1, source_target_pairs={{0,16},{2,18},{4,20},{6,22},{8,24},{10,26},{12,28},{14,30},{16,0},... | collective-permute-start | bytes 196616 | tf_op jit(solution)/shard_map/ppermute | solution.py:380
  150.3 4.3 %collective-permute-start.2 = (f32[128,128]{1,0:T(8,128)S(1)}, f32[128,128]{1,0:T(8,128)S(1)}, u32[]{:S(2)}, u32[]{:S(2)}) collective-permute-start(f32[128,128]{1,0:T(8,128)S(1)} %add.16), channel_id=1, source_target_pairs={{0,8},{2,10},{4,12},{6,14},{8,0},{10,2},{12,4},{14,6},{16,24},{18,... | collective-permute-start | bytes 196616 | tf_op jit(solution)/shard_map/ppermute | solution.py:380
  154.6 4.3 %collective-permute-start.3 = (f32[128,128]{1,0:T(8,128)S(1)}, f32[128,128]{1,0:T(8,128)S(1)}, u32[]{:S(2)}, u32[]{:S(2)}) collective-permute-start(f32[128,128]{1,0:T(8,128)S(1)} %add.17), channel_id=1, source_target_pairs={{0,4},{2,6},{4,0},{6,2},{8,12},{10,14},{12,8},{14,10},{16,20},{18,... | collective-permute-start | bytes 196616 | tf_op jit(solution)/shard_map/ppermute | solution.py:380
  158.9 4.3 %collective-permute-start.4 = (f32[128,128]{1,0:T(8,128)S(1)}, f32[128,128]{1,0:T(8,128)S(1)}, u32[]{:S(2)}, u32[]{:S(2)}) collective-permute-start(f32[128,128]{1,0:T(8,128)S(1)} %add.18), channel_id=1, source_target_pairs={{0,1},{1,0},{2,3},{3,2},{4,5},{5,4},{6,7},{7,6},{8,9},{9,8},{10,11... | collective-permute-start | bytes 196616 | tf_op jit(solution)/shard_map/ppermute | solution.py:380
  163.3 1.3 collective-permute-start.5

commit v12 on v11

--- a/solution.py
+++ b/solution.py
@@ -154,7 +154,7 @@
 
     for part in range(parts):
         come(part).wait()
-        lax.fori_loop(part * count, (part + 1) * count, one_row, 0, unroll=8)
+        lax.fori_loop(part * count, (part + 1) * count, one_row, 0, unroll=16)
         leave(part).start()
     for channel in range(h):
         for side in range(2):
@@ -189,7 +189,7 @@
     h = wl.shape[0]
     rows = grads_ref.shape[0]
     pitch = rows + 1
-    together = 8 if rows % 8 == 0 else 1
+    together = 16 if rows % 16 == 0 else 1
     stack_weights((wl, wlg, wr, wrg), w_ref)
     sums_ref[...] = jnp.zeros_like(sums_ref)
 
@@ -249,7 +249,7 @@
     count = rows // parts
     gone = []
     for part in range(parts):
-        lax.fori_loop(part * count, (part + 1) * count, one_row, 0, unroll=4)
+        lax.fori_loop(part * count, (part + 1) * count, one_row, 0, unroll=8)
         at = pl.ds(part * count, count)
         to = out_hbm.at[pl.ds(start + part * count, count)]
         gone.append(pltpu.make_async_copy(out_ref.at[at], to, out_sems.at[part]))
@@ -274,7 +274,7 @@
     dim = pair.shape[2]
     own = hidden // devices
     pieces = 2 if r % 2 == 0 else 1
-    parts = 4 if r % 16 == 0 else 1
+    parts = 2 if r % 16 == 0 else 1
     weights = [w.T for w in weights]
     vmem = pl.BlockSpec(memory_space=pltpu.VMEM)
     hbm = pl.BlockSpec(memory_space=pltpu.HBM)

time: 166 us -> 165 us (level)
  transfers between devices with their start and end apart: 6 -> 6, of which waited for: 5 -> 6; matrix products, arithmetic and copies ran while one was open for 0% -> 0% of each run, Pallas kernels for 5% -> 5%
where the time goes in v12:
time: 165 us
  blocking collectives  130 us (79%)
  Pallas kernels  18.8 us (11%)
  waiting for transfers between devices  9.77 us (6%)
  starting transfers between devices  4.92 us (3%)
    all_to_all x2, blocking collectives, channel_shards(): exchange(sent)  130 us
    pallas_call x2, Pallas kernels, input_piece(): pl.pallas_call(functools.partial(input_kernel, piece * count), in_specs=[...  7.55 us
    ppermute x4, waiting for transfers between devices, channel_shards(): other = lax.ppermute(mine, axis, [(i, i ^ step) for i in range(size)])  7.29 us
    pallas_call x1, Pallas kernels, channel_shards(): pl.pallas_call(functools.partial(before_kernel, own), in_specs=[hbm] * 6,...  4.81 us
    ppermute x4, starting transfers between devices, channel_shards(): other = lax.ppermute(mine, axis, [(i, i ^ step) for i in range(size)])  4.77 us
    pallas_call x1, Pallas kernels, channel_shards(): pl.pallas_call(functools.partial(gates_kernel, own), in_specs=[hbm] + [vm...  4.55 us
  transfers between devices with their start and end apart: 6, of which 6 were waited for; matrix products, arithmetic and copies ran while one was open for 0% of the time, Pallas kernels for 5%

profile of v12, /device:TPU:0, one launch (start us, length us, event | category | flops | bytes accessed | tf_op | source)
XLA Modules:
  0.0 164.8 jit_solution(11731062481898413370)
XLA Ops:
  0.6 4.8 %before.1 = (bf16[32,6,32,256]{3,2,1,0:T(8,128)(2,1)S(1)}, bf16[32,128,256]{2,1,0:T(8,128)(2,1)}) custom-call(bf16[32,256,128]{2,1,0:T(8,128)(2,1)} %pair_hbm.5, bf16[32,2,32,256]{3,2,1,0:T(8,128)(2,1)} %bitcast.25, bf16[64,128]{1,0:T(8,128)(2,1)} %bitcast.9, bf16[64,128]{1,0:T(8,128)(2,1)} %bitcast.13, bf16[64,128]{1,0:T(8,128)(2,1)} %bitcast.17, ...), custom_call_target="tpu_custom_call" | custom-call | tf_op jit(solution)/shard_map/before/pallas_call | solution.py:299
  5.5 78.3 %all_to_all.10.in_ref = bf16[32,6,32,256]{3,2,1,0:T(8,128)(2,1)S(1)} all-to-all(bf16[32,6,32,256]{3,2,1,0:T(8,128)(2,1)S(1)} %get-tuple-element.19), channel_id=1, replica_groups=mesh['row'=16,'col'=2] {'row','col'}, dimensions={0} | all-to-all | bytes 6291456 | tf_op jit(solution)/shard_map/all_to_all | solution.py:333
  83.8 1.3 triangle.1
  85.0 0.0 copy-start
  85.0 0.0 copy-start.1
  85.1 0.0 copy-start.2
  85.1 0.0 copy-start.3
  85.1 52.2 %all_to_all.11.d_ref = bf16[32,4,32,256]{3,2,1,0:T(8,128)(2,1)S(1)} all-to-all(bf16[32,4,32,256]{3,2,1,0:T(8,128)(2,1)S(1)} %triangle.1), channel_id=1, replica_groups=mesh['row'=16,'col'=2] {'row','col'}, dimensions={0} | all-to-all | bytes 4194304 | tf_op jit(solution)/shard_map/all_to_all | solution.py:350
  137.2 0.0 copy-done
  137.2 0.0 copy-done.1
  137.2 0.0 copy-done.2
  137.3 0.0 copy-done.3
  137.3 4.6 %gates.1 = (bf16[32,256,256]{2,1,0:T(8,128)(2,1)S(1)}, f32[128,128]{1,0:T(8,128)S(1)}, f32[128,128]{1,0:T(8,128)S(1)}) custom-call(bf16[32,128,256]{2,1,0:T(8,128)(2,1)} %get-tuple-element.18.normed_hbm, bf16[32,4,32,256]{3,2,1,0:T(8,128)(2,1)S(1)} %all_to_all.11.d_ref, bf16[64,128]{1,0:T(8,128)(2,1)S(1)} %bitcast.10, bf16[64,128]{1,0:T(8,128)(2,1)S(1)} %bitcast.14, ...), custom_call_target="tpu_custom_call" | custom-call | tf_op jit(solution)/shard_map/gates/pallas_call | solution.py:336
  141.8 0.1 collective-permute-start
  141.9 1.2 collective-permute-done
  143.2 1.8 %collective-permute-start.1 = (f32[128,128]{1,0:T(8,128)S(1)}, f32[128,128]{1,0:T(8,128)S(1)}, u32[]{:S(2)}, u32[]{:S(2)}) collective-permute-start(f32[128,128]{1,0:T(8,128)S(1)} %add.15), channel_id=1, source_target_pairs={{0,16},{2,18},{4,20},{6,22},{8,24},{10,26},{12,28},{14,30},{16,0},... | collective-permute-start | bytes 196616 | tf_op jit(solution)/shard_map/ppermute | solution.py:380
  145.0 3.8 %input.2.refs_0_ = bf16[32,256,128]{2,1,0:T(8,128)(2,1)} custom-call(bf16[32,256,128]{2,1,0:T(8,128)(2,1)} %pair_hbm.5, bf16[32,256,256]{2,1,0:T(8,128)(2,1)S(1)} %get-tuple-element.22.grads_ref, bf16[64,128]{1,0:T(8,128)(2,1)S(1)} %bitcast.11, bf16[64,128]{1,0:T(8,128)(2,1)S(1)} %bitcast.15, bf16[64,128]{1,0:T(8,128)(2,1)S(1)} %bitcast.19, ...), custom_call_target="tpu_custom_call" | custom-call | flops 268435456 | bytes 2097152 | tf_op jit(solution)/shard_map/input/pallas_call | solution.py:355
  148.8 1.0 collective-permute-done.1
  149.8 0.4 collective-permute-start.2
  150.2 3.8 %input.3 = bf16[32,256,128]{2,1,0:T(8,128)(2,1)} custom-call(bf16[32,256,128]{2,1,0:T(8,128)(2,1)} %pair_hbm.5, bf16[32,256,256]{2,1,0:T(8,128)(2,1)S(1)} %get-tuple-element.22.grads_ref, bf16[64,128]{1,0:T(8,128)(2,1)S(1)} %bitcast.12, bf16[64,128]{1,0:T(8,128)(2,1)S(1)} %bitcast.16, bf16[64,128]{1,0:T(8,128)(2,1)S(1)} %bitcast.20, ...), custom_call_target="tpu_custom_call", output_to_operand_aliasing={{}: (6, {})} | custom-call | flops 268435456 | bytes 2097152 | tf_op jit(solution)/shard_map/input/pallas_call | solution.py:355
  153.9 0.2 collective-permute-done.2
  154.1 1.2 collective-permute-start.3
  155.3 3.2 %collective-permute-done.3 = f32[128,128]{1,0:T(8,128)S(1)} collective-permute-done((f32[128,128]{1,0:T(8,128)S(1)}, f32[128,128]{1,0:T(8,128)S(1)}, u32[]{:S(2)}, u32[]{:S(2)}) %collective-permute-start.3) | collective-permute-done | bytes 65568 | tf_op jit(solution)/shard_map/ppermute | solution.py:380
  158.5 1.4 collective-permute-start.4
  159.9 2.9 %collective-permute-done.4 = f32[128,128]{1,0:T(8,128)S(1)} collective-permute-done((f32[128,128]{1,0:T(8,128)S(1)}, f32[128,128]{1,0:T(8,128)S(1)}, u32[]{:S(2)}, u32[]{:S(2)}) %collective-permute-start.4) | collective-permute-done | bytes 65568 | tf_op jit(solution)/shard_map/ppermute | solution.py:380
  162.8 0.1 collective-permute-start.5
  162.9 1.2 collective-permute-done.5.other_ref
  164.2 0.7 finish.1
  (5 shorter events, 0.0 us)
Async XLA Ops:
  85.0 52.2 %copy-start = (bf16[128,64]{0,1:T(8,128)(2,1)S(1)}, bf16[128,64]{0,1:T(8,128)(2,1)}, u32[]{:S(2)}) copy-start(bf16[128,64]{0,1:T(8,128)(2,1)} %param.8) | copy-start | bytes 49156
  85.0 52.2 %copy-start.1 = (bf16[128,64]{0,1:T(8,128)(2,1)S(1)}, bf16[128,64]{0,1:T(8,128)(2,1)}, u32[]{:S(2)}) copy-start(bf16[128,64]{0,1:T(8,128)(2,1)} %param.9) | copy-start | bytes 49156
  85.1 52.2 %copy-start.2 = (bf16[128,64]{0,1:T(8,128)(2,1)S(1)}, bf16[128,64]{0,1:T(8,128)(2,1)}, u32[]{:S(2)}) copy-start(bf16[128,64]{0,1:T(8,128)(2,1)} %param.10) | copy-start | bytes 49156
  85.1 52.2 %copy-start.3 = (bf16[128,64]{0,1:T(8,128)(2,1)S(1)}, bf16[128,64]{0,1:T(8,128)(2,1)}, u32[]{:S(2)}) copy-start(bf16[128,64]{0,1:T(8,128)(2,1)} %param.11) | copy-start | bytes 49156
  141.8 1.3 collective-permute-start
  143.2 6.6 %collective-permute-start.1 = (f32[128,128]{1,0:T(8,128)S(1)}, f32[128,128]{1,0:T(8,128)S(1)}, u32[]{:S(2)}, u32[]{:S(2)}) collective-permute-start(f32[128,128]{1,0:T(8,128)S(1)} %add.15), channel_id=1, source_target_pairs={{0,16},{2,18},{4,20},{6,22},{8,24},{10,26},{12,28},{14,30},{16,0},... | collective-permute-start | bytes 196616 | tf_op jit(solution)/shard_map/ppermute | solution.py:380
  149.8 4.3 %collective-permute-start.2 = (f32[128,128]{1,0:T(8,128)S(1)}, f32[128,128]{1,0:T(8,128)S(1)}, u32[]{:S(2)}, u32[]{:S(2)}) collective-permute-start(f32[128,128]{1,0:T(8,128)S(1)} %add.16), channel_id=1, source_target_pairs={{0,8},{2,10},{4,12},{6,14},{8,0},{10,2},{12,4},{14,6},{16,24},{18,... | collective-permute-start | bytes 196616 | tf_op jit(solution)/shard_map/ppermute | solution.py:380
  154.1 4.3 %collective-permute-start.3 = (f32[128,128]{1,0:T(8,128)S(1)}, f32[128,128]{1,0:T(8,128)S(1)}, u32[]{:S(2)}, u32[]{:S(2)}) collective-permute-start(f32[128,128]{1,0:T(8,128)S(1)} %add.17), channel_id=1, source_target_pairs={{0,4},{2,6},{4,0},{6,2},{8,12},{10,14},{12,8},{14,10},{16,20},{18,... | collective-permute-start | bytes 196616 | tf_op jit(solution)/shard_map/ppermute | solution.py:380
  158.5 4.3 %collective-permute-start.4 = (f32[128,128]{1,0:T(8,128)S(1)}, f32[128,128]{1,0:T(8,128)S(1)}, u32[]{:S(2)}, u32[]{:S(2)}) collective-permute-start(f32[128,128]{1,0:T(8,128)S(1)} %add.18), channel_id=1, source_target_pairs={{0,1},{1,0},{2,3},{3,2},{4,5},{5,4},{6,7},{7,6},{8,9},{9,8},{10,11... | collective-permute-start | bytes 196616 | tf_op jit(solution)/shard_map/ppermute | solution.py:380
  162.8 1.3 collective-permute-start.5

commit v13 on v12

--- a/solution.py
+++ b/solution.py
@@ -117,12 +117,12 @@
 
 
 def before_kernel(own, pair_hbm, cot_hbm, wl, wlg, wr, wrg, out_ref, normed_hbm, *scratch):
-    w_ref, rows_ref, pair_ref, normed_ref, in_sems, out_sems, w_sems, cot_sem = scratch
+    w_ref, *rows_refs, pair_ref, normed_ref, in_sems, out_sems, w_sems, cot_sem = scratch
     h = wl.shape[0]
     rows = pair_ref.shape[0]
-    pitch = rows + 1
     parts = in_sems.shape[0]
     count = rows // parts
+    pitch = count + 1
 
     def come(part):
         at = pl.ds(part * count, count)
@@ -144,22 +144,32 @@
     for i, w in enumerate((wl, wlg, wr, wrg)):
         weight(i, w).wait()
 
-    def one_row(r, carry):
+    def one_row(part, i):
+        r = part * count + i
         normed = layer_norm(pair_ref[r])[0].astype(BF16)
         normed_ref[r] = normed
         q_left, s_left, q_right, s_right = project(w_ref, normed)
-        put_lanes(rows_ref, pl.ds(r, h, stride=pitch), s_left * q_left)
-        put_lanes(rows_ref, pl.ds(r + h * pitch, h, stride=pitch), s_right * q_right)
-        return carry
-
-    for part in range(parts):
-        come(part).wait()
-        lax.fori_loop(part * count, (part + 1) * count, one_row, 0, unroll=16)
-        leave(part).start()
-    for channel in range(h):
-        for side in range(2):
-            line = get_lanes(rows_ref, pl.ds((side * h + channel) * pitch, rows))
-            out_ref[channel // own, (1 + side) * own + channel % own] = line.astype(BF16)
+        put_lanes(rows_refs[part], pl.ds(i, h, stride=pitch), s_left * q_left)
+        put_lanes(rows_refs[part], pl.ds(i + h * pitch, h, stride=pitch), s_right * q_right)
+
+    def some_channels(part, i):
+        for channel in range(i * h // count, (i + 1) * h // count):
+            for side in range(2):
+                at = pl.ds((side * h + channel) * pitch, count)
+                line = get_lanes(rows_refs[part], at).astype(BF16)
+                slot = (1 + side) * own + channel % own
+                out_ref[channel // own, slot, pl.ds(part * count, count), :] = line
+
+    for part in range(parts + 1):
+        if part < parts:
+            come(part).wait()
+        for i in range(count):
+            if part < parts:
+                one_row(part, i)
+            if part > 0:
+                some_channels(part - 1, i)
+        if part < parts:
+            leave(part).start()
     for part in range(parts):
         leave(part).wait()
     cot.wait()
@@ -183,44 +193,47 @@
 
 
 def gates_kernel(own, normed_hbm, d_ref, wl, wlg, wr, wrg, grads_ref, kept_ref, sent_ref, *scratch):
-    w_ref, sums_ref, rows_ref, normed_ref, sem = scratch
+    w_ref, sums_ref, *rows_refs, normed_ref, sem = scratch
     copy = pltpu.make_async_copy(normed_hbm, normed_ref, sem)
     copy.start()
     h = wl.shape[0]
     rows = grads_ref.shape[0]
-    pitch = rows + 1
-    together = 16 if rows % 16 == 0 else 1
+    parts = len(rows_refs)
+    count = rows // parts
+    pitch = count + 1
     stack_weights((wl, wlg, wr, wrg), w_ref)
-    sums_ref[...] = jnp.zeros_like(sums_ref)
-
-    for channel in range(h):
-        to, slot = channel // own, (channel % own) * 2
-        for side in range(2):
-            line = d_ref[to, slot + side].astype(F32)
-            put_lanes(rows_ref, pl.ds((side * h + channel) * pitch, rows), line)
-
-    copy.wait()
-
-    def some_rows(n, carry):
-        all_grads, all_normed = [], []
-        for i in range(together):
-            r = n * together + i
-            normed = normed_ref[r]
-            q_left, s_left, q_right, s_right = project(w_ref, normed)
-            e_left = get_lanes(rows_ref, pl.ds(r, h, stride=pitch)) * s_left
-            e_right = get_lanes(rows_ref, pl.ds(r + h * pitch, h, stride=pitch)) * s_right
-            f_left = e_left * q_left * (1.0 - s_left)
-            f_right = e_right * q_right * (1.0 - s_right)
-            grads = jnp.concatenate([e_left, f_left, e_right, f_right], axis=0).astype(BF16)
-            grads_ref[r] = grads
-            all_grads.append(grads)
-            all_normed.append(normed)
-        sums_ref[...] += dot(
-            jnp.concatenate(all_grads, axis=1), jnp.concatenate(all_normed, axis=1), NT
-        )
-        return carry
-
-    lax.fori_loop(0, rows // together, some_rows, 0)
+
+    def some_channels(part, i):
+        for channel in range(i * h // count, (i + 1) * h // count):
+            to, slot = channel // own, (channel % own) * 2
+            for side in range(2):
+                line = d_ref[to, slot + side, pl.ds(part * count, count), :].astype(F32)
+                put_lanes(rows_refs[part], pl.ds((side * h + channel) * pitch, count), line)
+
+    def one_row(part, i):
+        normed = normed_ref[part * count + i]
+        q_left, s_left, q_right, s_right = project(w_ref, normed)
+        e_left = get_lanes(rows_refs[part], pl.ds(i, h, stride=pitch)) * s_left
+        e_right = get_lanes(rows_refs[part], pl.ds(i + h * pitch, h, stride=pitch)) * s_right
+        f_left = e_left * q_left * (1.0 - s_left)
+        f_right = e_right * q_right * (1.0 - s_right)
+        grads = jnp.concatenate([e_left, f_left, e_right, f_right], axis=0).astype(BF16)
+        grads_ref[part * count + i] = grads
+        return grads, normed
+
+    for part in range(parts + 1):
+        if part == 1:
+            copy.wait()
+        done = []
+        for i in range(count):
+            if part > 0:
+                done.append(one_row(part - 1, i))
+            if part < parts:
+                some_channels(part, i)
+        if part > 0:
+            all_grads, all_normed = (jnp.concatenate(x, axis=1) for x in zip(*done))
+            total = dot(all_grads, all_normed, NT)
+            sums_ref[...] = total if part == 1 else sums_ref[...] + total
     bit = lax.rem(lax.axis_index("row"), 2)
     kept_ref[...] = sums_ref[pl.ds(pl.multiple_of(bit * 2 * h, 2 * h), 2 * h), :]
     sent_ref[...] = sums_ref[pl.ds(pl.multiple_of((1 - bit) * 2 * h, 2 * h), 2 * h), :]
@@ -274,7 +287,7 @@
     dim = pair.shape[2]
     own = hidden // devices
     pieces = 2 if r % 2 == 0 else 1
-    parts = 2 if r % 16 == 0 else 1
+    parts = 2 if r % 32 == 0 else 1
     weights = [w.T for w in weights]
     vmem = pl.BlockSpec(memory_space=pltpu.VMEM)
     hbm = pl.BlockSpec(memory_space=pltpu.HBM)
@@ -283,7 +296,7 @@
     )
     stacked = pltpu.VMEM((4 * hidden, dim), BF16)
     lanes = min(c, 128)
-    rows_scratch = pltpu.VMEM((c // lanes, (2 * hidden + 1) * (r + 1), lanes), F32)
+    rows_scratch = pltpu.VMEM((c // lanes, (2 * hidden + 1) * (r // parts + 1), lanes), F32)
     columns = r * c
     n_i, n_k = rows * r, cols * c
     pair = pltpu.with_memory_space_constraint(pair, pltpu.HBM)
@@ -306,7 +319,7 @@
         ],
         scratch_shapes=[
             stacked,
-            rows_scratch,
+            *[rows_scratch] * parts,
             pltpu.VMEM(pair.shape, BF16),
             pltpu.VMEM(normed_shape.shape, BF16),
             pltpu.SemaphoreType.DMA((parts,)),
@@ -341,7 +354,7 @@
         scratch_shapes=[
             stacked,
             pltpu.VMEM((4 * hidden, dim), F32),
-            rows_scratch,
+            *[rows_scratch] * parts,
             pltpu.VMEM(normed_shape.shape, BF16),
             pltpu.SemaphoreType.DMA,
         ],

time: 165 us -> 165 us (level)
  no operation moved by 1% of the time
where the time goes in v13:
time: 165 us; the launch traced here: 164 us
  blocking collectives  130 us (79%)
  Pallas kernels  18.4 us (11%)
  waiting for transfers between devices  9.77 us (6%)
  starting transfers between devices  4.92 us (3%)
    all_to_all x2, blocking collectives, channel_shards(): exchange(sent)  130 us
    pallas_call x2, Pallas kernels, input_piece(): pl.pallas_call(functools.partial(input_kernel, piece * count), in_specs=[...  7.55 us
    ppermute x4, waiting for transfers between devices, channel_shards(): other = lax.ppermute(mine, axis, [(i, i ^ step) for i in range(size)])  7.29 us
    ppermute x4, starting transfers between devices, channel_shards(): other = lax.ppermute(mine, axis, [(i, i ^ step) for i in range(size)])  4.77 us
    pallas_call x1, Pallas kernels, channel_shards(): pl.pallas_call(functools.partial(before_kernel, own), in_specs=[hbm] * 6,...  4.77 us
    pallas_call x1, Pallas kernels, channel_shards(): pl.pallas_call(functools.partial(gates_kernel, own), in_specs=[hbm] + [vm...  4.17 us
  transfers between devices with their start and end apart: 6, of which 6 were waited for; matrix products, arithmetic and copies ran while one was open for 0% of the time, Pallas kernels for 5%

profile of v13, /device:TPU:0, one launch (start us, length us, event | category | flops | bytes accessed | tf_op | source)
XLA Modules:
  0.0 164.4 jit_solution(6838883948624807863)
XLA Ops:
  0.6 4.8 %before.1 = (bf16[32,6,32,256]{3,2,1,0:T(8,128)(2,1)S(1)}, bf16[32,128,256]{2,1,0:T(8,128)(2,1)}) custom-call(bf16[32,256,128]{2,1,0:T(8,128)(2,1)} %pair_hbm.5, bf16[32,2,32,256]{3,2,1,0:T(8,128)(2,1)} %bitcast.25, bf16[64,128]{1,0:T(8,128)(2,1)} %bitcast.9, bf16[64,128]{1,0:T(8,128)(2,1)} %bitcast.13, bf16[64,128]{1,0:T(8,128)(2,1)} %bitcast.17, ...), custom_call_target="tpu_custom_call" | custom-call | tf_op jit(solution)/shard_map/before/pallas_call | solution.py:312
  5.4 78.3 %all_to_all.10.in_ref = bf16[32,6,32,256]{3,2,1,0:T(8,128)(2,1)S(1)} all-to-all(bf16[32,6,32,256]{3,2,1,0:T(8,128)(2,1)S(1)} %get-tuple-element.19), channel_id=1, replica_groups=mesh['row'=16,'col'=2] {'row','col'}, dimensions={0} | all-to-all | bytes 6291456 | tf_op jit(solution)/shard_map/all_to_all | solution.py:346
  83.7 1.3 triangle.1
  85.0 0.0 copy-start
  85.0 0.0 copy-start.1
  85.0 0.0 copy-start.2
  85.0 0.0 copy-start.3
  85.0 52.2 %all_to_all.11.d_ref = bf16[32,4,32,256]{3,2,1,0:T(8,128)(2,1)S(1)} all-to-all(bf16[32,4,32,256]{3,2,1,0:T(8,128)(2,1)S(1)} %triangle.1), channel_id=1, replica_groups=mesh['row'=16,'col'=2] {'row','col'}, dimensions={0} | all-to-all | bytes 4194304 | tf_op jit(solution)/shard_map/all_to_all | solution.py:363
  137.2 0.0 copy-done
  137.2 0.0 copy-done.1
  137.2 0.0 copy-done.2
  137.2 0.0 copy-done.3
  137.2 4.2 %gates.1 = (bf16[32,256,256]{2,1,0:T(8,128)(2,1)S(1)}, f32[128,128]{1,0:T(8,128)S(1)}, f32[128,128]{1,0:T(8,128)S(1)}) custom-call(bf16[32,128,256]{2,1,0:T(8,128)(2,1)} %get-tuple-element.18.normed_hbm, bf16[32,4,32,256]{3,2,1,0:T(8,128)(2,1)S(1)} %all_to_all.11.d_ref, bf16[64,128]{1,0:T(8,128)(2,1)S(1)} %bitcast.10, bf16[64,128]{1,0:T(8,128)(2,1)S(1)} %bitcast.14, ...), custom_call_target="tpu_custom_call" | custom-call | tf_op jit(solution)/shard_map/gates/pallas_call | solution.py:349
  141.4 0.1 collective-permute-start
  141.5 1.2 collective-permute-done
  142.7 1.8 %collective-permute-start.1 = (f32[128,128]{1,0:T(8,128)S(1)}, f32[128,128]{1,0:T(8,128)S(1)}, u32[]{:S(2)}, u32[]{:S(2)}) collective-permute-start(f32[128,128]{1,0:T(8,128)S(1)} %add.15), channel_id=1, source_target_pairs={{0,16},{2,18},{4,20},{6,22},{8,24},{10,26},{12,28},{14,30},{16,0},... | collective-permute-start | bytes 196616 | tf_op jit(solution)/shard_map/ppermute | solution.py:393
  144.5 3.8 %input.2.refs_0_ = bf16[32,256,128]{2,1,0:T(8,128)(2,1)} custom-call(bf16[32,256,128]{2,1,0:T(8,128)(2,1)} %pair_hbm.5, bf16[32,256,256]{2,1,0:T(8,128)(2,1)S(1)} %get-tuple-element.22.grads_ref, bf16[64,128]{1,0:T(8,128)(2,1)S(1)} %bitcast.11, bf16[64,128]{1,0:T(8,128)(2,1)S(1)} %bitcast.15, bf16[64,128]{1,0:T(8,128)(2,1)S(1)} %bitcast.19, ...), custom_call_target="tpu_custom_call" | custom-call | flops 268435456 | bytes 2097152 | tf_op jit(solution)/shard_map/input/pallas_call | solution.py:368
  148.3 1.0 collective-permute-done.1
  149.4 0.4 collective-permute-start.2
  149.7 3.8 %input.3 = bf16[32,256,128]{2,1,0:T(8,128)(2,1)} custom-call(bf16[32,256,128]{2,1,0:T(8,128)(2,1)} %pair_hbm.5, bf16[32,256,256]{2,1,0:T(8,128)(2,1)S(1)} %get-tuple-element.22.grads_ref, bf16[64,128]{1,0:T(8,128)(2,1)S(1)} %bitcast.12, bf16[64,128]{1,0:T(8,128)(2,1)S(1)} %bitcast.16, bf16[64,128]{1,0:T(8,128)(2,1)S(1)} %bitcast.20, ...), custom_call_target="tpu_custom_call", output_to_operand_aliasing={{}: (6, {})} | custom-call | flops 268435456 | bytes 2097152 | tf_op jit(solution)/shard_map/input/pallas_call | solution.py:368
  153.5 0.2 collective-permute-done.2
  153.7 1.2 collective-permute-start.3
  154.9 3.2 %collective-permute-done.3 = f32[128,128]{1,0:T(8,128)S(1)} collective-permute-done((f32[128,128]{1,0:T(8,128)S(1)}, f32[128,128]{1,0:T(8,128)S(1)}, u32[]{:S(2)}, u32[]{:S(2)}) %collective-permute-start.3) | collective-permute-done | bytes 65568 | tf_op jit(solution)/shard_map/ppermute | solution.py:393
  158.1 1.4 collective-permute-start.4
  159.5 2.9 %collective-permute-done.4 = f32[128,128]{1,0:T(8,128)S(1)} collective-permute-done((f32[128,128]{1,0:T(8,128)S(1)}, f32[128,128]{1,0:T(8,128)S(1)}, u32[]{:S(2)}, u32[]{:S(2)}) %collective-permute-start.4) | collective-permute-done | bytes 65568 | tf_op jit(solution)/shard_map/ppermute | solution.py:393
  162.4 0.1 collective-permute-start.5
  162.5 1.2 collective-permute-done.5.other_ref
  163.7 0.7 finish.1
  (5 shorter events, 0.0 us)
Async XLA Ops:
  85.0 52.2 %copy-start = (bf16[128,64]{0,1:T(8,128)(2,1)S(1)}, bf16[128,64]{0,1:T(8,128)(2,1)}, u32[]{:S(2)}) copy-start(bf16[128,64]{0,1:T(8,128)(2,1)} %param.8) | copy-start | bytes 49156
  85.0 52.2 %copy-start.1 = (bf16[128,64]{0,1:T(8,128)(2,1)S(1)}, bf16[128,64]{0,1:T(8,128)(2,1)}, u32[]{:S(2)}) copy-start(bf16[128,64]{0,1:T(8,128)(2,1)} %param.9) | copy-start | bytes 49156
  85.0 52.2 %copy-start.2 = (bf16[128,64]{0,1:T(8,128)(2,1)S(1)}, bf16[128,64]{0,1:T(8,128)(2,1)}, u32[]{:S(2)}) copy-start(bf16[128,64]{0,1:T(8,128)(2,1)} %param.10) | copy-start | bytes 49156
  85.0 52.2 %copy-start.3 = (bf16[128,64]{0,1:T(8,128)(2,1)S(1)}, bf16[128,64]{0,1:T(8,128)(2,1)}, u32[]{:S(2)}) copy-start(bf16[128,64]{0,1:T(8,128)(2,1)} %param.11) | copy-start | bytes 49156
  141.4 1.3 collective-permute-start
  142.7 6.6 %collective-permute-start.1 = (f32[128,128]{1,0:T(8,128)S(1)}, f32[128,128]{1,0:T(8,128)S(1)}, u32[]{:S(2)}, u32[]{:S(2)}) collective-permute-start(f32[128,128]{1,0:T(8,128)S(1)} %add.15), channel_id=1, source_target_pairs={{0,16},{2,18},{4,20},{6,22},{8,24},{10,26},{12,28},{14,30},{16,0},... | collective-permute-start | bytes 196616 | tf_op jit(solution)/shard_map/ppermute | solution.py:393
  149.4 4.3 %collective-permute-start.2 = (f32[128,128]{1,0:T(8,128)S(1)}, f32[128,128]{1,0:T(8,128)S(1)}, u32[]{:S(2)}, u32[]{:S(2)}) collective-permute-start(f32[128,128]{1,0:T(8,128)S(1)} %add.16), channel_id=1, source_target_pairs={{0,8},{2,10},{4,12},{6,14},{8,0},{10,2},{12,4},{14,6},{16,24},{18,... | collective-permute-start | bytes 196616 | tf_op jit(solution)/shard_map/ppermute | solution.py:393
  153.7 4.3 %collective-permute-start.3 = (f32[128,128]{1,0:T(8,128)S(1)}, f32[128,128]{1,0:T(8,128)S(1)}, u32[]{:S(2)}, u32[]{:S(2)}) collective-permute-start(f32[128,128]{1,0:T(8,128)S(1)} %add.17), channel_id=1, source_target_pairs={{0,4},{2,6},{4,0},{6,2},{8,12},{10,14},{12,8},{14,10},{16,20},{18,... | collective-permute-start | bytes 196616 | tf_op jit(solution)/shard_map/ppermute | solution.py:393
  158.1 4.3 %collective-permute-start.4 = (f32[128,128]{1,0:T(8,128)S(1)}, f32[128,128]{1,0:T(8,128)S(1)}, u32[]{:S(2)}, u32[]{:S(2)}) collective-permute-start(f32[128,128]{1,0:T(8,128)S(1)} %add.18), channel_id=1, source_target_pairs={{0,1},{1,0},{2,3},{3,2},{4,5},{5,4},{6,7},{7,6},{8,9},{9,8},{10,11... | collective-permute-start | bytes 196616 | tf_op jit(solution)/shard_map/ppermute | solution.py:393
  162.4 1.3 collective-permute-start.5

commit v14 on v13

--- a/solution.py
+++ b/solution.py
@@ -383,18 +383,21 @@
             name="input",
         )(pair, grads, *weights, *held)
 
-    steps = [("row", rows, 1 << i) for i in range(1, rows.bit_length() - 1)][::-1]
-    steps += [("col", cols, 1 << i) for i in range(cols.bit_length() - 1)]
-    pieces = min(pieces, len(steps))
     neighbours = [(i, i ^ 1) for i in range(rows)]
+    alike = [
+        [i * cols + j for i in range(bit, rows, 2) for j in range(cols)] for bit in range(2)
+    ]
+    share = functools.partial(exchange, axis_index_groups=alike)
+    mine = kept + lax.ppermute(given, "row", neighbours)
+    blocks = mine.reshape(devices // 2, -1, dim)
     pair_gradient = None
-    mine = kept + lax.ppermute(given, "row", neighbours)
-    for n, (axis, size, step) in enumerate(steps):
-        other = lax.ppermute(mine, axis, [(i, i ^ step) for i in range(size)])
-        if n < pieces:
-            pair_gradient = input_piece(n, pair_gradient)
-            other, pair_gradient = lax.optimization_barrier((other, pair_gradient))
-        mine = mine + other
+    for piece in range(pieces):
+        if piece == 1:
+            blocks = jnp.broadcast_to(jnp.sum(blocks, axis=0, keepdims=True), blocks.shape)
+        blocks = share(blocks)
+        pair_gradient = input_piece(piece, pair_gradient)
+        blocks, pair_gradient = lax.optimization_barrier((blocks, pair_gradient))
+    mine = blocks.reshape(mine.shape)
     weight_grads = pl.pallas_call(
         functools.partial(finish_kernel, 1.0 / n_i),
         in_specs=[vmem, vmem],

time: 165 us -> 173 us (1.048)
  local copies, waits for them, and re-layouts: 0.03 us -> 6.95 us
  starting transfers between devices: 4.92 us -> 10.1 us
  waiting for transfers between devices: 9.77 us -> 5.6 us
    all_to_all x0 -> x2, starting transfers between devices: none -> 10 us  [channel_shards(): blocks = share(blocks)]
    ppermute x4 -> x0, waiting for transfers between devices: 7.29 us -> none  [channel_shards(): other = lax.ppermute(mine, axis, [(i, i ^ step) for i in range(size)])]
    unnamed x8 -> x14, local copies, waits for them, and re-layouts: 0.03 us -> 6.33 us
    ppermute x4 -> x0, starting transfers between devices: 4.77 us -> none  [channel_shards(): other = lax.ppermute(mine, axis, [(i, i ^ step) for i in range(size)])]
    all_to_all x0 -> x2, waiting for transfers between devices: none -> 3.11 us  [channel_shards(): blocks = share(blocks)]
  transfers between devices with their start and end apart: 6 -> 4, of which waited for: 6 -> 4; matrix products, arithmetic and copies ran while one was open for 0% -> 0% of each run, Pallas kernels for 5% -> 4%
where the time goes in v14:
time: 173 us
  blocking collectives  130 us (75%)
  Pallas kernels  18.4 us (11%)
  starting transfers between devices  10.1 us (6%)
  local copies, waits for them, and re-layouts  6.95 us (4%)
  waiting for transfers between devices  5.6 us (3%)
    all_to_all x2, blocking collectives, channel_shards(): exchange(sent)  130 us
    all_to_all x2, starting transfers between devices, channel_shards(): blocks = share(blocks)  10 us
    pallas_call x2, Pallas kernels, input_piece(): pl.pallas_call(functools.partial(input_kernel, piece * count), in_specs=[...  7.56 us
    unnamed x14, local copies, waits for them, and re-layouts  6.33 us
    pallas_call x1, Pallas kernels, channel_shards(): pl.pallas_call(functools.partial(before_kernel, own), in_specs=[hbm] * 6,...  4.74 us
    pallas_call x1, Pallas kernels, channel_shards(): pl.pallas_call(functools.partial(gates_kernel, own), in_specs=[hbm] + [vm...  4.17 us
  transfers between devices with their start and end apart: 4, of which 4 were waited for; matrix products, arithmetic and copies ran while one was open for 0% of the time, Pallas kernels for 4%

profile of v14, /device:TPU:0, one launch (start us, length us, event | category | flops | bytes accessed | tf_op | source)
XLA Modules:
  0.0 172.9 jit_solution(5980508112812851213)
XLA Ops:
  0.6 4.7 %before.1 = (bf16[32,6,32,256]{3,2,1,0:T(8,128)(2,1)S(1)}, bf16[32,128,256]{2,1,0:T(8,128)(2,1)}) custom-call(bf16[32,256,128]{2,1,0:T(8,128)(2,1)} %pair_hbm.5, bf16[32,2,32,256]{3,2,1,0:T(8,128)(2,1)} %bitcast.30, bf16[64,128]{1,0:T(8,128)(2,1)} %bitcast.12, bf16[64,128]{1,0:T(8,128)(2,1)} %bitcast.16, bf16[64,128]{1,0:T(8,128)(2,1)} %bitcast.20, ...), custom_call_target="tpu_custom_call" | custom-call | tf_op jit(solution)/shard_map/before/pallas_call | solution.py:312
  5.4 78.3 %all_to_all.20.in_ref = bf16[32,6,32,256]{3,2,1,0:T(8,128)(2,1)S(1)} all-to-all(bf16[32,6,32,256]{3,2,1,0:T(8,128)(2,1)S(1)} %get-tuple-element.19), channel_id=1, replica_groups=mesh['row'=16,'col'=2] {'row','col'}, dimensions={0} | all-to-all | bytes 6291456 | tf_op jit(solution)/shard_map/all_to_all | solution.py:346
  83.7 1.3 triangle.1
  84.9 0.0 copy-start.3
  84.9 0.0 copy-start.4
  85.0 0.0 copy-start.5
  85.0 0.0 copy-start.6
  85.0 52.2 %all_to_all.21.d_ref = bf16[32,4,32,256]{3,2,1,0:T(8,128)(2,1)S(1)} all-to-all(bf16[32,4,32,256]{3,2,1,0:T(8,128)(2,1)S(1)} %triangle.1), channel_id=1, replica_groups=mesh['row'=16,'col'=2] {'row','col'}, dimensions={0} | all-to-all | bytes 4194304 | tf_op jit(solution)/shard_map/all_to_all | solution.py:363
  137.2 0.0 copy-done.3
  137.2 0.0 copy-done.4
  137.2 0.0 copy-done.5
  137.2 0.0 copy-done.6
  137.2 4.2 %gates.1 = (bf16[32,256,256]{2,1,0:T(8,128)(2,1)S(1)}, f32[128,128]{1,0:T(8,128)S(1)}, f32[128,128]{1,0:T(8,128)S(1)}) custom-call(bf16[32,128,256]{2,1,0:T(8,128)(2,1)} %get-tuple-element.18.normed_hbm, bf16[32,4,32,256]{3,2,1,0:T(8,128)(2,1)S(1)} %all_to_all.21.d_ref, bf16[64,128]{1,0:T(8,128)(2,1)S(1)} %bitcast.13, bf16[64,128]{1,0:T(8,128)(2,1)S(1)} %bitcast.17, ...), custom_call_target="tpu_custom_call" | custom-call | tf_op jit(solution)/shard_map/gates/pallas_call | solution.py:349
  141.4 0.0 copy-start
  141.4 1.9 %copy-done = bf16[32,256,256]{2,1,0:T(8,128)(2,1)} copy-done((bf16[32,256,256]{2,1,0:T(8,128)(2,1)}, bf16[32,256,256]{2,1,0:T(8,128)(2,1)S(1)}, u32[]{:S(2)}) %copy-start) | copy-done | bytes 4194328
  143.3 0.0 collective-permute-start
  143.3 1.2 collective-permute-done
  144.6 0.6 add_bitcast_fusion
  145.2 4.7 %all-to-all-start.2 = ((f32[16,8,128]{2,1,0:T(8,128)}), f32[16,8,128]{2,1,0:T(8,128)S(1)}, u32[]{:S(2)}, u32[]{:S(2)}) async-start(f32[16,8,128]{2,1,0:T(8,128)} %add_bitcast_fusion), calls=%async_computation.2 | async-start | bytes 131072 | tf_op jit(solution)/shard_map/all_to_all | solution.py:397
  149.9 0.0 copy-start.1
  149.9 2.2 %copy-done.1 = bf16[32,256,256]{2,1,0:T(8,128)(2,1)S(1)} copy-done((bf16[32,256,256]{2,1,0:T(8,128)(2,1)S(1)}, bf16[32,256,256]{2,1,0:T(8,128)(2,1)}, u32[]{:S(2)}) %copy-start.1) | copy-done | bytes 4194328
  152.1 3.8 %input.2.refs_0_ = bf16[32,256,128]{2,1,0:T(8,128)(2,1)} custom-call(bf16[32,256,128]{2,1,0:T(8,128)(2,1)} %pair_hbm.5, bf16[32,256,256]{2,1,0:T(8,128)(2,1)S(1)} %copy-done.1, bf16[64,128]{1,0:T(8,128)(2,1)S(1)} %bitcast.14, bf16[64,128]{1,0:T(8,128)(2,1)S(1)} %bitcast.18, bf16[64,128]{1,0:T(8,128)(2,1)S(1)} %bitcast.22, bf16[64,128]{1,0:T(8,128)(2,1)S(1)} %bitcast.26), custom_call_target="tpu_custom_call" | custom-call | flops 268435456 | bytes 2097152 | tf_op jit(solution)/shard_map/input/pallas_call | solution.py:368
  155.8 1.6 all-to-all-done.2
  157.4 0.6 broadcast_in_dim.2
  158.0 5.4 %all-to-all-start.3 = ((f32[16,8,128]{2,1,0:T(8,128)}), f32[16,8,128]{2,1,0:T(8,128)S(1)}, u32[]{:S(2)}, u32[]{:S(2)}) async-start(f32[16,8,128]{2,1,0:T(8,128)} %broadcast_in_dim.2), calls=%async_computation.3 | async-start | bytes 131072 | tf_op jit(solution)/shard_map/all_to_all | solution.py:397
  163.4 0.0 copy-start.2
  163.4 2.2 %copy-done.2 = bf16[32,256,256]{2,1,0:T(8,128)(2,1)S(1)} copy-done((bf16[32,256,256]{2,1,0:T(8,128)(2,1)S(1)}, bf16[32,256,256]{2,1,0:T(8,128)(2,1)}, u32[]{:S(2)}) %copy-start.2) | copy-done | bytes 4194328
  165.6 3.8 %input.3 = bf16[32,256,128]{2,1,0:T(8,128)(2,1)} custom-call(bf16[32,256,128]{2,1,0:T(8,128)(2,1)} %pair_hbm.5, bf16[32,256,256]{2,1,0:T(8,128)(2,1)S(1)} %copy-done.2, bf16[64,128]{1,0:T(8,128)(2,1)S(1)} %bitcast.15, bf16[64,128]{1,0:T(8,128)(2,1)S(1)} %bitcast.19, bf16[64,128]{1,0:T(8,128)(2,1)S(1)} %bitcast.23, ...), custom_call_target="tpu_custom_call", output_to_operand_aliasing={{}: (6, {})} | custom-call | flops 268435456 | bytes 2097152 | tf_op jit(solution)/shard_map/input/pallas_call | solution.py:368
  169.4 1.6 all-to-all-done.3
  170.9 0.0 collective-permute-start.1
  170.9 1.3 collective-permute-done.1.other_ref
  172.2 0.7 finish.1
  (1 shorter events, 0.0 us)
Async XLA Ops:
  84.9 52.2 %copy-start.3 = (bf16[128,64]{0,1:T(8,128)(2,1)S(1)}, bf16[128,64]{0,1:T(8,128)(2,1)}, u32[]{:S(2)}) copy-start(bf16[128,64]{0,1:T(8,128)(2,1)} %param.8) | copy-start | bytes 49156
  84.9 52.2 %copy-start.4 = (bf16[128,64]{0,1:T(8,128)(2,1)S(1)}, bf16[128,64]{0,1:T(8,128)(2,1)}, u32[]{:S(2)}) copy-start(bf16[128,64]{0,1:T(8,128)(2,1)} %param.9) | copy-start | bytes 49156
  85.0 52.2 %copy-start.5 = (bf16[128,64]{0,1:T(8,128)(2,1)S(1)}, bf16[128,64]{0,1:T(8,128)(2,1)}, u32[]{:S(2)}) copy-start(bf16[128,64]{0,1:T(8,128)(2,1)} %param.10) | copy-start | bytes 49156
  85.0 52.2 %copy-start.6 = (bf16[128,64]{0,1:T(8,128)(2,1)S(1)}, bf16[128,64]{0,1:T(8,128)(2,1)}, u32[]{:S(2)}) copy-start(bf16[128,64]{0,1:T(8,128)(2,1)} %param.11) | copy-start | bytes 49156
  141.4 1.9 %copy-start = (bf16[32,256,256]{2,1,0:T(8,128)(2,1)}, bf16[32,256,256]{2,1,0:T(8,128)(2,1)S(1)}, u32[]{:S(2)}) copy-start(bf16[32,256,256]{2,1,0:T(8,128)(2,1)S(1)} %get-tuple-element.22.grads_ref) | copy-start | bytes 12582916
  143.3 1.3 collective-permute-start
  145.2 12.2 %all-to-all-start.2 = ((f32[16,8,128]{2,1,0:T(8,128)}), f32[16,8,128]{2,1,0:T(8,128)S(1)}, u32[]{:S(2)}, u32[]{:S(2)}) async-start(f32[16,8,128]{2,1,0:T(8,128)} %add_bitcast_fusion), calls=%async_computation.2 | async-start | bytes 131072 | tf_op jit(solution)/shard_map/all_to_all | solution.py:397
  149.9 2.2 %copy-start.1 = (bf16[32,256,256]{2,1,0:T(8,128)(2,1)S(1)}, bf16[32,256,256]{2,1,0:T(8,128)(2,1)}, u32[]{:S(2)}) copy-start(bf16[32,256,256]{2,1,0:T(8,128)(2,1)} %copy-done) | copy-start | bytes 12582916
  158.0 12.9 %all-to-all-start.3 = ((f32[16,8,128]{2,1,0:T(8,128)}), f32[16,8,128]{2,1,0:T(8,128)S(1)}, u32[]{:S(2)}, u32[]{:S(2)}) async-start(f32[16,8,128]{2,1,0:T(8,128)} %broadcast_in_dim.2), calls=%async_computation.3 | async-start | bytes 131072 | tf_op jit(solution)/shard_map/all_to_all | solution.py:397
  163.4 2.2 %copy-start.2 = (bf16[32,256,256]{2,1,0:T(8,128)(2,1)S(1)}, bf16[32,256,256]{2,1,0:T(8,128)(2,1)}, u32[]{:S(2)}) copy-start(bf16[32,256,256]{2,1,0:T(8,128)(2,1)} %copy-done) | copy-start | bytes 12582916
  170.9 1.3 collective-permute-start.1

commit v15 on v13

--- a/solution.py
+++ b/solution.py
@@ -135,10 +135,10 @@
     def weight(i, w):
         return pltpu.make_async_copy(w, w_ref.at[pl.ds(i * h, h)], w_sems.at[i])
 
+    for i, w in enumerate((wl, wlg, wr, wrg)):
+        weight(i, w).start()
     for part in range(parts):
         come(part).start()
-    for i, w in enumerate((wl, wlg, wr, wrg)):
-        weight(i, w).start()
     cot = pltpu.make_async_copy(cot_hbm, out_ref.at[:, pl.ds(0, own)], cot_sem)
     cot.start()
     for i, w in enumerate((wl, wlg, wr, wrg)):
@@ -221,6 +221,8 @@
         grads_ref[part * count + i] = grads
         return grads, normed
 
+    together = 8 if count % 8 == 0 else count
+    sums_ref[...] = jnp.zeros_like(sums_ref)
     for part in range(parts + 1):
         if part == 1:
             copy.wait()
@@ -230,10 +232,10 @@
                 done.append(one_row(part - 1, i))
             if part < parts:
                 some_channels(part, i)
-        if part > 0:
-            all_grads, all_normed = (jnp.concatenate(x, axis=1) for x in zip(*done))
-            total = dot(all_grads, all_normed, NT)
-            sums_ref[...] = total if part == 1 else sums_ref[...] + total
+            if len(done) == together:
+                all_grads, all_normed = (jnp.concatenate(x, axis=1) for x in zip(*done))
+                sums_ref[...] += dot(all_grads, all_normed, NT)
+                done = []
     bit = lax.rem(lax.axis_index("row"), 2)
     kept_ref[...] = sums_ref[pl.ds(pl.multiple_of(bit * 2 * h, 2 * h), 2 * h), :]
     sent_ref[...] = sums_ref[pl.ds(pl.multiple_of((1 - bit) * 2 * h, 2 * h), 2 * h), :]

time: 165 us -> 165 us (level)
  no operation moved by 1% of the time
where the time goes in v15:
time: 165 us; the launch traced here: 164 us
  blocking collectives  130 us (79%)
  Pallas kernels  18.3 us (11%)
  waiting for transfers between devices  9.77 us (6%)
  starting transfers between devices  4.91 us (3%)
    all_to_all x2, blocking collectives, channel_shards(): exchange(sent)  130 us
    pallas_call x2, Pallas kernels, input_piece(): pl.pallas_call(functools.partial(input_kernel, piece * count), in_specs=[...  7.56 us
    ppermute x4, waiting for transfers between devices, channel_shards(): other = lax.ppermute(mine, axis, [(i, i ^ step) for i in range(size)])  7.29 us
    ppermute x4, starting transfers between devices, channel_shards(): other = lax.ppermute(mine, axis, [(i, i ^ step) for i in range(size)])  4.76 us
    pallas_call x1, Pallas kernels, channel_shards(): pl.pallas_call(functools.partial(before_kernel, own), in_specs=[hbm] * 6,...  4.61 us
    pallas_call x1, Pallas kernels, channel_shards(): pl.pallas_call(functools.partial(gates_kernel, own), in_specs=[hbm] + [vm...  4.19 us
  transfers between devices with their start and end apart: 6, of which 6 were waited for; matrix products, arithmetic and copies ran while one was open for 0% of the time, Pallas kernels for 5%

profile of v15, /device:TPU:0, one launch (start us, length us, event | category | flops | bytes accessed | tf_op | source)
XLA Modules:
  0.0 164.2 jit_solution(14055069140852219242)
XLA Ops:
  0.6 4.6 %before.1 = (bf16[32,6,32,256]{3,2,1,0:T(8,128)(2,1)S(1)}, bf16[32,128,256]{2,1,0:T(8,128)(2,1)}) custom-call(bf16[32,256,128]{2,1,0:T(8,128)(2,1)} %pair_hbm.5, bf16[32,2,32,256]{3,2,1,0:T(8,128)(2,1)} %bitcast.25, bf16[64,128]{1,0:T(8,128)(2,1)} %bitcast.9, bf16[64,128]{1,0:T(8,128)(2,1)} %bitcast.13, bf16[64,128]{1,0:T(8,128)(2,1)} %bitcast.17, ...), custom_call_target="tpu_custom_call" | custom-call | tf_op jit(solution)/shard_map/before/pallas_call | solution.py:314
  5.2 78.3 %all_to_all.10.in_ref = bf16[32,6,32,256]{3,2,1,0:T(8,128)(2,1)S(1)} all-to-all(bf16[32,6,32,256]{3,2,1,0:T(8,128)(2,1)S(1)} %get-tuple-element.19), channel_id=1, replica_groups=mesh['row'=16,'col'=2] {'row','col'}, dimensions={0} | all-to-all | bytes 6291456 | tf_op jit(solution)/shard_map/all_to_all | solution.py:348
  83.5 1.3 triangle.1
  84.8 0.0 copy-start
  84.8 0.0 copy-start.1
  84.8 0.0 copy-start.2
  84.8 0.0 copy-start.3
  84.9 52.2 %all_to_all.11.d_ref = bf16[32,4,32,256]{3,2,1,0:T(8,128)(2,1)S(1)} all-to-all(bf16[32,4,32,256]{3,2,1,0:T(8,128)(2,1)S(1)} %triangle.1), channel_id=1, replica_groups=mesh['row'=16,'col'=2] {'row','col'}, dimensions={0} | all-to-all | bytes 4194304 | tf_op jit(solution)/shard_map/all_to_all | solution.py:365
  137.0 0.0 copy-done
  137.0 0.0 copy-done.1
  137.0 0.0 copy-done.2
  137.0 0.0 copy-done.3
  137.0 4.2 %gates.1 = (bf16[32,256,256]{2,1,0:T(8,128)(2,1)S(1)}, f32[128,128]{1,0:T(8,128)S(1)}, f32[128,128]{1,0:T(8,128)S(1)}) custom-call(bf16[32,128,256]{2,1,0:T(8,128)(2,1)} %get-tuple-element.18.normed_hbm, bf16[32,4,32,256]{3,2,1,0:T(8,128)(2,1)S(1)} %all_to_all.11.d_ref, bf16[64,128]{1,0:T(8,128)(2,1)S(1)} %bitcast.10, bf16[64,128]{1,0:T(8,128)(2,1)S(1)} %bitcast.14, ...), custom_call_target="tpu_custom_call" | custom-call | tf_op jit(solution)/shard_map/gates/pallas_call | solution.py:351
  141.2 0.1 collective-permute-start
  141.3 1.2 collective-permute-done
  142.6 1.8 %collective-permute-start.1 = (f32[128,128]{1,0:T(8,128)S(1)}, f32[128,128]{1,0:T(8,128)S(1)}, u32[]{:S(2)}, u32[]{:S(2)}) collective-permute-start(f32[128,128]{1,0:T(8,128)S(1)} %add.15), channel_id=1, source_target_pairs={{0,16},{2,18},{4,20},{6,22},{8,24},{10,26},{12,28},{14,30},{16,0},... | collective-permute-start | bytes 196616 | tf_op jit(solution)/shard_map/ppermute | solution.py:395
  144.4 3.8 %input.2.refs_0_ = bf16[32,256,128]{2,1,0:T(8,128)(2,1)} custom-call(bf16[32,256,128]{2,1,0:T(8,128)(2,1)} %pair_hbm.5, bf16[32,256,256]{2,1,0:T(8,128)(2,1)S(1)} %get-tuple-element.22.grads_ref, bf16[64,128]{1,0:T(8,128)(2,1)S(1)} %bitcast.11, bf16[64,128]{1,0:T(8,128)(2,1)S(1)} %bitcast.15, bf16[64,128]{1,0:T(8,128)(2,1)S(1)} %bitcast.19, ...), custom_call_target="tpu_custom_call" | custom-call | flops 268435456 | bytes 2097152 | tf_op jit(solution)/shard_map/input/pallas_call | solution.py:370
  148.2 1.0 collective-permute-done.1
  149.2 0.4 collective-permute-start.2
  149.6 3.8 %input.3 = bf16[32,256,128]{2,1,0:T(8,128)(2,1)} custom-call(bf16[32,256,128]{2,1,0:T(8,128)(2,1)} %pair_hbm.5, bf16[32,256,256]{2,1,0:T(8,128)(2,1)S(1)} %get-tuple-element.22.grads_ref, bf16[64,128]{1,0:T(8,128)(2,1)S(1)} %bitcast.12, bf16[64,128]{1,0:T(8,128)(2,1)S(1)} %bitcast.16, bf16[64,128]{1,0:T(8,128)(2,1)S(1)} %bitcast.20, ...), custom_call_target="tpu_custom_call", output_to_operand_aliasing={{}: (6, {})} | custom-call | flops 268435456 | bytes 2097152 | tf_op jit(solution)/shard_map/input/pallas_call | solution.py:370
  153.4 0.2 collective-permute-done.2
  153.6 1.2 collective-permute-start.3
  154.7 3.2 %collective-permute-done.3 = f32[128,128]{1,0:T(8,128)S(1)} collective-permute-done((f32[128,128]{1,0:T(8,128)S(1)}, f32[128,128]{1,0:T(8,128)S(1)}, u32[]{:S(2)}, u32[]{:S(2)}) %collective-permute-start.3) | collective-permute-done | bytes 65568 | tf_op jit(solution)/shard_map/ppermute | solution.py:395
  157.9 1.4 collective-permute-start.4
  159.3 2.9 %collective-permute-done.4 = f32[128,128]{1,0:T(8,128)S(1)} collective-permute-done((f32[128,128]{1,0:T(8,128)S(1)}, f32[128,128]{1,0:T(8,128)S(1)}, u32[]{:S(2)}, u32[]{:S(2)}) %collective-permute-start.4) | collective-permute-done | bytes 65568 | tf_op jit(solution)/shard_map/ppermute | solution.py:395
  162.3 0.1 collective-permute-start.5
  162.3 1.2 collective-permute-done.5.other_ref
  163.6 0.7 finish.1
  (5 shorter events, 0.0 us)
Async XLA Ops:
  84.8 52.2 %copy-start = (bf16[128,64]{0,1:T(8,128)(2,1)S(1)}, bf16[128,64]{0,1:T(8,128)(2,1)}, u32[]{:S(2)}) copy-start(bf16[128,64]{0,1:T(8,128)(2,1)} %param.8) | copy-start | bytes 49156
  84.8 52.2 %copy-start.1 = (bf16[128,64]{0,1:T(8,128)(2,1)S(1)}, bf16[128,64]{0,1:T(8,128)(2,1)}, u32[]{:S(2)}) copy-start(bf16[128,64]{0,1:T(8,128)(2,1)} %param.9) | copy-start | bytes 49156
  84.8 52.2 %copy-start.2 = (bf16[128,64]{0,1:T(8,128)(2,1)S(1)}, bf16[128,64]{0,1:T(8,128)(2,1)}, u32[]{:S(2)}) copy-start(bf16[128,64]{0,1:T(8,128)(2,1)} %param.10) | copy-start | bytes 49156
  84.8 52.2 %copy-start.3 = (bf16[128,64]{0,1:T(8,128)(2,1)S(1)}, bf16[128,64]{0,1:T(8,128)(2,1)}, u32[]{:S(2)}) copy-start(bf16[128,64]{0,1:T(8,128)(2,1)} %param.11) | copy-start | bytes 49156
  141.2 1.3 collective-permute-start
  142.6 6.6 %collective-permute-start.1 = (f32[128,128]{1,0:T(8,128)S(1)}, f32[128,128]{1,0:T(8,128)S(1)}, u32[]{:S(2)}, u32[]{:S(2)}) collective-permute-start(f32[128,128]{1,0:T(8,128)S(1)} %add.15), channel_id=1, source_target_pairs={{0,16},{2,18},{4,20},{6,22},{8,24},{10,26},{12,28},{14,30},{16,0},... | collective-permute-start | bytes 196616 | tf_op jit(solution)/shard_map/ppermute | solution.py:395
  149.2 4.3 %collective-permute-start.2 = (f32[128,128]{1,0:T(8,128)S(1)}, f32[128,128]{1,0:T(8,128)S(1)}, u32[]{:S(2)}, u32[]{:S(2)}) collective-permute-start(f32[128,128]{1,0:T(8,128)S(1)} %add.16), channel_id=1, source_target_pairs={{0,8},{2,10},{4,12},{6,14},{8,0},{10,2},{12,4},{14,6},{16,24},{18,... | collective-permute-start | bytes 196616 | tf_op jit(solution)/shard_map/ppermute | solution.py:395
  153.6 4.3 %collective-permute-start.3 = (f32[128,128]{1,0:T(8,128)S(1)}, f32[128,128]{1,0:T(8,128)S(1)}, u32[]{:S(2)}, u32[]{:S(2)}) collective-permute-start(f32[128,128]{1,0:T(8,128)S(1)} %add.17), channel_id=1, source_target_pairs={{0,4},{2,6},{4,0},{6,2},{8,12},{10,14},{12,8},{14,10},{16,20},{18,... | collective-permute-start | bytes 196616 | tf_op jit(solution)/shard_map/ppermute | solution.py:395
  157.9 4.3 %collective-permute-start.4 = (f32[128,128]{1,0:T(8,128)S(1)}, f32[128,128]{1,0:T(8,128)S(1)}, u32[]{:S(2)}, u32[]{:S(2)}) collective-permute-start(f32[128,128]{1,0:T(8,128)S(1)} %add.18), channel_id=1, source_target_pairs={{0,1},{1,0},{2,3},{3,2},{4,5},{5,4},{6,7},{7,6},{8,9},{9,8},{10,11... | collective-permute-start | bytes 196616 | tf_op jit(solution)/shard_map/ppermute | solution.py:395
  162.3 1.3 collective-permute-start.5

commit v16 on v15

--- a/solution.py
+++ b/solution.py
@@ -92,7 +92,7 @@
 
 
 def layer_norm(x):
-    x = x.T.astype(F32)
+    x = x.astype(F32).T
     centered = x - jnp.mean(x, axis=0, keepdims=True)
     variance = jnp.mean(centered * centered, axis=0, keepdims=True)
     inverse_scale = lax.rsqrt(variance + 1e-05)

time: 165 us -> 165 us (level)
  no operation moved by 1% of the time
where the time goes in v16:
time: 165 us
  blocking collectives  130 us (79%)
  Pallas kernels  18.6 us (11%)
  waiting for transfers between devices  9.81 us (6%)
  starting transfers between devices  4.91 us (3%)
    all_to_all x2, blocking collectives, channel_shards(): exchange(sent)  130 us
    pallas_call x2, Pallas kernels, input_piece(): pl.pallas_call(functools.partial(input_kernel, piece * count), in_specs=[...  7.52 us
    ppermute x4, waiting for transfers between devices, channel_shards(): other = lax.ppermute(mine, axis, [(i, i ^ step) for i in range(size)])  7.33 us
    pallas_call x1, Pallas kernels, channel_shards(): pl.pallas_call(functools.partial(before_kernel, own), in_specs=[hbm] * 6,...  4.98 us
    ppermute x4, starting transfers between devices, channel_shards(): other = lax.ppermute(mine, axis, [(i, i ^ step) for i in range(size)])  4.76 us
    pallas_call x1, Pallas kernels, channel_shards(): pl.pallas_call(functools.partial(gates_kernel, own), in_specs=[hbm] + [vm...  4.19 us
  transfers between devices with their start and end apart: 6, of which 6 were waited for; matrix products, arithmetic and copies ran while one was open for 0% of the time, Pallas kernels for 5%

profile of v16, /device:TPU:0, one launch (start us, length us, event | category | flops | bytes accessed | tf_op | source)
XLA Modules:
  0.0 164.6 jit_solution(17655816568257190105)
XLA Ops:
  0.6 5.0 %before.1 = (bf16[32,6,32,256]{3,2,1,0:T(8,128)(2,1)S(1)}, bf16[32,128,256]{2,1,0:T(8,128)(2,1)}) custom-call(bf16[32,256,128]{2,1,0:T(8,128)(2,1)} %pair_hbm.5, bf16[32,2,32,256]{3,2,1,0:T(8,128)(2,1)} %bitcast.25, bf16[64,128]{1,0:T(8,128)(2,1)} %bitcast.9, bf16[64,128]{1,0:T(8,128)(2,1)} %bitcast.13, bf16[64,128]{1,0:T(8,128)(2,1)} %bitcast.17, ...), custom_call_target="tpu_custom_call" | custom-call | tf_op jit(solution)/shard_map/before/pallas_call | solution.py:314
  5.6 78.3 %all_to_all.10.in_ref = bf16[32,6,32,256]{3,2,1,0:T(8,128)(2,1)S(1)} all-to-all(bf16[32,6,32,256]{3,2,1,0:T(8,128)(2,1)S(1)} %get-tuple-element.19), channel_id=1, replica_groups=mesh['row'=16,'col'=2] {'row','col'}, dimensions={0} | all-to-all | bytes 6291456 | tf_op jit(solution)/shard_map/all_to_all | solution.py:348
  83.9 1.3 triangle.1
  85.2 0.0 copy-start
  85.2 0.0 copy-start.1
  85.2 0.0 copy-start.2
  85.2 0.0 copy-start.3
  85.2 52.2 %all_to_all.11.d_ref = bf16[32,4,32,256]{3,2,1,0:T(8,128)(2,1)S(1)} all-to-all(bf16[32,4,32,256]{3,2,1,0:T(8,128)(2,1)S(1)} %triangle.1), channel_id=1, replica_groups=mesh['row'=16,'col'=2] {'row','col'}, dimensions={0} | all-to-all | bytes 4194304 | tf_op jit(solution)/shard_map/all_to_all | solution.py:365
  137.4 0.0 copy-done
  137.4 0.0 copy-done.1
  137.4 0.0 copy-done.2
  137.4 0.0 copy-done.3
  137.4 4.2 %gates.1 = (bf16[32,256,256]{2,1,0:T(8,128)(2,1)S(1)}, f32[128,128]{1,0:T(8,128)S(1)}, f32[128,128]{1,0:T(8,128)S(1)}) custom-call(bf16[32,128,256]{2,1,0:T(8,128)(2,1)} %get-tuple-element.18.normed_hbm, bf16[32,4,32,256]{3,2,1,0:T(8,128)(2,1)S(1)} %all_to_all.11.d_ref, bf16[64,128]{1,0:T(8,128)(2,1)S(1)} %bitcast.10, bf16[64,128]{1,0:T(8,128)(2,1)S(1)} %bitcast.14, ...), custom_call_target="tpu_custom_call" | custom-call | tf_op jit(solution)/shard_map/gates/pallas_call | solution.py:351
  141.6 0.1 collective-permute-start
  141.7 1.2 collective-permute-done
  142.9 1.8 %collective-permute-start.1 = (f32[128,128]{1,0:T(8,128)S(1)}, f32[128,128]{1,0:T(8,128)S(1)}, u32[]{:S(2)}, u32[]{:S(2)}) collective-permute-start(f32[128,128]{1,0:T(8,128)S(1)} %add.15), channel_id=1, source_target_pairs={{0,16},{2,18},{4,20},{6,22},{8,24},{10,26},{12,28},{14,30},{16,0},... | collective-permute-start | bytes 196616 | tf_op jit(solution)/shard_map/ppermute | solution.py:395
  144.7 3.8 %input.2.refs_0_ = bf16[32,256,128]{2,1,0:T(8,128)(2,1)} custom-call(bf16[32,256,128]{2,1,0:T(8,128)(2,1)} %pair_hbm.5, bf16[32,256,256]{2,1,0:T(8,128)(2,1)S(1)} %get-tuple-element.22.grads_ref, bf16[64,128]{1,0:T(8,128)(2,1)S(1)} %bitcast.11, bf16[64,128]{1,0:T(8,128)(2,1)S(1)} %bitcast.15, bf16[64,128]{1,0:T(8,128)(2,1)S(1)} %bitcast.19, ...), custom_call_target="tpu_custom_call" | custom-call | flops 268435456 | bytes 2097152 | tf_op jit(solution)/shard_map/input/pallas_call | solution.py:370
  148.5 1.1 collective-permute-done.1
  149.6 0.4 collective-permute-start.2
  149.9 3.8 %input.3 = bf16[32,256,128]{2,1,0:T(8,128)(2,1)} custom-call(bf16[32,256,128]{2,1,0:T(8,128)(2,1)} %pair_hbm.5, bf16[32,256,256]{2,1,0:T(8,128)(2,1)S(1)} %get-tuple-element.22.grads_ref, bf16[64,128]{1,0:T(8,128)(2,1)S(1)} %bitcast.12, bf16[64,128]{1,0:T(8,128)(2,1)S(1)} %bitcast.16, bf16[64,128]{1,0:T(8,128)(2,1)S(1)} %bitcast.20, ...), custom_call_target="tpu_custom_call", output_to_operand_aliasing={{}: (6, {})} | custom-call | flops 268435456 | bytes 2097152 | tf_op jit(solution)/shard_map/input/pallas_call | solution.py:370
  153.7 0.2 collective-permute-done.2
  153.9 1.2 collective-permute-start.3
  155.1 3.2 %collective-permute-done.3 = f32[128,128]{1,0:T(8,128)S(1)} collective-permute-done((f32[128,128]{1,0:T(8,128)S(1)}, f32[128,128]{1,0:T(8,128)S(1)}, u32[]{:S(2)}, u32[]{:S(2)}) %collective-permute-start.3) | collective-permute-done | bytes 65568 | tf_op jit(solution)/shard_map/ppermute | solution.py:395
  158.3 1.4 collective-permute-start.4
  159.7 2.9 %collective-permute-done.4 = f32[128,128]{1,0:T(8,128)S(1)} collective-permute-done((f32[128,128]{1,0:T(8,128)S(1)}, f32[128,128]{1,0:T(8,128)S(1)}, u32[]{:S(2)}, u32[]{:S(2)}) %collective-permute-start.4) | collective-permute-done | bytes 65568 | tf_op jit(solution)/shard_map/ppermute | solution.py:395
  162.6 0.1 collective-permute-start.5
  162.7 1.2 collective-permute-done.5.other_ref
  163.9 0.7 finish.1
  (5 shorter events, 0.0 us)
Async XLA Ops:
  85.2 52.2 %copy-start = (bf16[128,64]{0,1:T(8,128)(2,1)S(1)}, bf16[128,64]{0,1:T(8,128)(2,1)}, u32[]{:S(2)}) copy-start(bf16[128,64]{0,1:T(8,128)(2,1)} %param.8) | copy-start | bytes 49156
  85.2 52.2 %copy-start.1 = (bf16[128,64]{0,1:T(8,128)(2,1)S(1)}, bf16[128,64]{0,1:T(8,128)(2,1)}, u32[]{:S(2)}) copy-start(bf16[128,64]{0,1:T(8,128)(2,1)} %param.9) | copy-start | bytes 49156
  85.2 52.2 %copy-start.2 = (bf16[128,64]{0,1:T(8,128)(2,1)S(1)}, bf16[128,64]{0,1:T(8,128)(2,1)}, u32[]{:S(2)}) copy-start(bf16[128,64]{0,1:T(8,128)(2,1)} %param.10) | copy-start | bytes 49156
  85.2 52.2 %copy-start.3 = (bf16[128,64]{0,1:T(8,128)(2,1)S(1)}, bf16[128,64]{0,1:T(8,128)(2,1)}, u32[]{:S(2)}) copy-start(bf16[128,64]{0,1:T(8,128)(2,1)} %param.11) | copy-start | bytes 49156
  141.6 1.3 collective-permute-start
  142.9 6.6 %collective-permute-start.1 = (f32[128,128]{1,0:T(8,128)S(1)}, f32[128,128]{1,0:T(8,128)S(1)}, u32[]{:S(2)}, u32[]{:S(2)}) collective-permute-start(f32[128,128]{1,0:T(8,128)S(1)} %add.15), channel_id=1, source_target_pairs={{0,16},{2,18},{4,20},{6,22},{8,24},{10,26},{12,28},{14,30},{16,0},... | collective-permute-start | bytes 196616 | tf_op jit(solution)/shard_map/ppermute | solution.py:395
  149.6 4.3 %collective-permute-start.2 = (f32[128,128]{1,0:T(8,128)S(1)}, f32[128,128]{1,0:T(8,128)S(1)}, u32[]{:S(2)}, u32[]{:S(2)}) collective-permute-start(f32[128,128]{1,0:T(8,128)S(1)} %add.16), channel_id=1, source_target_pairs={{0,8},{2,10},{4,12},{6,14},{8,0},{10,2},{12,4},{14,6},{16,24},{18,... | collective-permute-start | bytes 196616 | tf_op jit(solution)/shard_map/ppermute | solution.py:395
  153.9 4.3 %collective-permute-start.3 = (f32[128,128]{1,0:T(8,128)S(1)}, f32[128,128]{1,0:T(8,128)S(1)}, u32[]{:S(2)}, u32[]{:S(2)}) collective-permute-start(f32[128,128]{1,0:T(8,128)S(1)} %add.17), channel_id=1, source_target_pairs={{0,4},{2,6},{4,0},{6,2},{8,12},{10,14},{12,8},{14,10},{16,20},{18,... | collective-permute-start | bytes 196616 | tf_op jit(solution)/shard_map/ppermute | solution.py:395
  158.3 4.3 %collective-permute-start.4 = (f32[128,128]{1,0:T(8,128)S(1)}, f32[128,128]{1,0:T(8,128)S(1)}, u32[]{:S(2)}, u32[]{:S(2)}) collective-permute-start(f32[128,128]{1,0:T(8,128)S(1)} %add.18), channel_id=1, source_target_pairs={{0,1},{1,0},{2,3},{3,2},{4,5},{5,4},{6,7},{7,6},{8,9},{9,8},{10,11... | collective-permute-start | bytes 196616 | tf_op jit(solution)/shard_map/ppermute | solution.py:395
  162.6 1.3 collective-permute-start.5

commit v17 on v15

--- a/solution.py
+++ b/solution.py
@@ -99,11 +99,17 @@
     return centered * inverse_scale, inverse_scale
 
 
+def sigmoid(p):
+    y = 1.0 + jnp.exp(-p)
+    r = pl.reciprocal(y, approx=True)
+    return r * (2.0 - y * r)
+
+
 def project(w_ref, normed):
     projected = dot(w_ref[...], normed)
     h = projected.shape[0] // 4
     q_left, p_left, q_right, p_right = (projected[i * h : (i + 1) * h] for i in range(4))
-    return q_left, jax.nn.sigmoid(p_left), q_right, jax.nn.sigmoid(p_right)
+    return q_left, sigmoid(p_left), q_right, sigmoid(p_right)
 
 
 def put_lanes(ref, at, value):

time: 165 us -> 165 us (level)
  no operation moved by 1% of the time
where the time goes in v17:
time: 165 us
  blocking collectives  130 us (79%)
  Pallas kernels  19 us (12%)
  waiting for transfers between devices  9.76 us (6%)
  starting transfers between devices  4.93 us (3%)
    all_to_all x2, blocking collectives, channel_shards(): exchange(sent)  130 us
    pallas_call x2, Pallas kernels, input_piece(): pl.pallas_call(functools.partial(input_kernel, piece * count), in_specs=[...  7.55 us
    ppermute x4, waiting for transfers between devices, channel_shards(): other = lax.ppermute(mine, axis, [(i, i ^ step) for i in range(size)])  7.28 us
    pallas_call x1, Pallas kernels, channel_shards(): pl.pallas_call(functools.partial(before_kernel, own), in_specs=[hbm] * 6,...  5.27 us
    ppermute x4, starting transfers between devices, channel_shards(): other = lax.ppermute(mine, axis, [(i, i ^ step) for i in range(size)])  4.77 us
    pallas_call x1, Pallas kernels, channel_shards(): pl.pallas_call(functools.partial(gates_kernel, own), in_specs=[hbm] + [vm...  4.31 us
  transfers between devices with their start and end apart: 6, of which 6 were waited for; matrix products, arithmetic and copies ran while one was open for 0% of the time, Pallas kernels for 5%

profile of v17, /device:TPU:0, one launch (start us, length us, event | category | flops | bytes accessed | tf_op | source)
XLA Modules:
  0.0 165.0 jit_solution(15500319064384661863)
XLA Ops:
  0.6 5.3 %before.1 = (bf16[32,6,32,256]{3,2,1,0:T(8,128)(2,1)S(1)}, bf16[32,128,256]{2,1,0:T(8,128)(2,1)}) custom-call(bf16[32,256,128]{2,1,0:T(8,128)(2,1)} %pair_hbm.5, bf16[32,2,32,256]{3,2,1,0:T(8,128)(2,1)} %bitcast.25, bf16[64,128]{1,0:T(8,128)(2,1)} %bitcast.9, bf16[64,128]{1,0:T(8,128)(2,1)} %bitcast.13, bf16[64,128]{1,0:T(8,128)(2,1)} %bitcast.17, ...), custom_call_target="tpu_custom_call" | custom-call | tf_op jit(solution)/shard_map/before/pallas_call | solution.py:320
  5.9 78.3 %all_to_all.10.in_ref = bf16[32,6,32,256]{3,2,1,0:T(8,128)(2,1)S(1)} all-to-all(bf16[32,6,32,256]{3,2,1,0:T(8,128)(2,1)S(1)} %get-tuple-element.19), channel_id=1, replica_groups=mesh['row'=16,'col'=2] {'row','col'}, dimensions={0} | all-to-all | bytes 6291456 | tf_op jit(solution)/shard_map/all_to_all | solution.py:354
  84.2 1.3 triangle.1
  85.5 0.0 copy-start
  85.5 0.0 copy-start.1
  85.5 0.0 copy-start.2
  85.5 0.0 copy-start.3
  85.5 52.2 %all_to_all.11.d_ref = bf16[32,4,32,256]{3,2,1,0:T(8,128)(2,1)S(1)} all-to-all(bf16[32,4,32,256]{3,2,1,0:T(8,128)(2,1)S(1)} %triangle.1), channel_id=1, replica_groups=mesh['row'=16,'col'=2] {'row','col'}, dimensions={0} | all-to-all | bytes 4194304 | tf_op jit(solution)/shard_map/all_to_all | solution.py:371
  137.7 0.0 copy-done
  137.7 0.0 copy-done.1
  137.7 0.0 copy-done.2
  137.7 0.0 copy-done.3
  137.7 4.3 %gates.1 = (bf16[32,256,256]{2,1,0:T(8,128)(2,1)S(1)}, f32[128,128]{1,0:T(8,128)S(1)}, f32[128,128]{1,0:T(8,128)S(1)}) custom-call(bf16[32,128,256]{2,1,0:T(8,128)(2,1)} %get-tuple-element.18.normed_hbm, bf16[32,4,32,256]{3,2,1,0:T(8,128)(2,1)S(1)} %all_to_all.11.d_ref, bf16[64,128]{1,0:T(8,128)(2,1)S(1)} %bitcast.10, bf16[64,128]{1,0:T(8,128)(2,1)S(1)} %bitcast.14, ...), custom_call_target="tpu_custom_call" | custom-call | tf_op jit(solution)/shard_map/gates/pallas_call | solution.py:357
  142.0 0.1 collective-permute-start
  142.1 1.2 collective-permute-done
  143.4 1.8 %collective-permute-start.1 = (f32[128,128]{1,0:T(8,128)S(1)}, f32[128,128]{1,0:T(8,128)S(1)}, u32[]{:S(2)}, u32[]{:S(2)}) collective-permute-start(f32[128,128]{1,0:T(8,128)S(1)} %add.15), channel_id=1, source_target_pairs={{0,16},{2,18},{4,20},{6,22},{8,24},{10,26},{12,28},{14,30},{16,0},... | collective-permute-start | bytes 196616 | tf_op jit(solution)/shard_map/ppermute | solution.py:401
  145.2 3.8 %input.2.refs_0_ = bf16[32,256,128]{2,1,0:T(8,128)(2,1)} custom-call(bf16[32,256,128]{2,1,0:T(8,128)(2,1)} %pair_hbm.5, bf16[32,256,256]{2,1,0:T(8,128)(2,1)S(1)} %get-tuple-element.22.grads_ref, bf16[64,128]{1,0:T(8,128)(2,1)S(1)} %bitcast.11, bf16[64,128]{1,0:T(8,128)(2,1)S(1)} %bitcast.15, bf16[64,128]{1,0:T(8,128)(2,1)S(1)} %bitcast.19, ...), custom_call_target="tpu_custom_call" | custom-call | flops 268435456 | bytes 2097152 | tf_op jit(solution)/shard_map/input/pallas_call | solution.py:376
  149.0 1.0 collective-permute-done.1
  150.0 0.4 collective-permute-start.2
  150.4 3.8 %input.3 = bf16[32,256,128]{2,1,0:T(8,128)(2,1)} custom-call(bf16[32,256,128]{2,1,0:T(8,128)(2,1)} %pair_hbm.5, bf16[32,256,256]{2,1,0:T(8,128)(2,1)S(1)} %get-tuple-element.22.grads_ref, bf16[64,128]{1,0:T(8,128)(2,1)S(1)} %bitcast.12, bf16[64,128]{1,0:T(8,128)(2,1)S(1)} %bitcast.16, bf16[64,128]{1,0:T(8,128)(2,1)S(1)} %bitcast.20, ...), custom_call_target="tpu_custom_call", output_to_operand_aliasing={{}: (6, {})} | custom-call | flops 268435456 | bytes 2097152 | tf_op jit(solution)/shard_map/input/pallas_call | solution.py:376
  154.1 0.2 collective-permute-done.2
  154.3 1.2 collective-permute-start.3
  155.5 3.2 %collective-permute-done.3 = f32[128,128]{1,0:T(8,128)S(1)} collective-permute-done((f32[128,128]{1,0:T(8,128)S(1)}, f32[128,128]{1,0:T(8,128)S(1)}, u32[]{:S(2)}, u32[]{:S(2)}) %collective-permute-start.3) | collective-permute-done | bytes 65568 | tf_op jit(solution)/shard_map/ppermute | solution.py:401
  158.7 1.4 collective-permute-start.4
  160.1 2.9 %collective-permute-done.4 = f32[128,128]{1,0:T(8,128)S(1)} collective-permute-done((f32[128,128]{1,0:T(8,128)S(1)}, f32[128,128]{1,0:T(8,128)S(1)}, u32[]{:S(2)}, u32[]{:S(2)}) %collective-permute-start.4) | collective-permute-done | bytes 65568 | tf_op jit(solution)/shard_map/ppermute | solution.py:401
  163.0 0.1 collective-permute-start.5
  163.1 1.2 collective-permute-done.5.other_ref
  164.4 0.7 finish.1
  (5 shorter events, 0.0 us)
Async XLA Ops:
  85.5 52.2 %copy-start = (bf16[128,64]{0,1:T(8,128)(2,1)S(1)}, bf16[128,64]{0,1:T(8,128)(2,1)}, u32[]{:S(2)}) copy-start(bf16[128,64]{0,1:T(8,128)(2,1)} %param.8) | copy-start | bytes 49156
  85.5 52.2 %copy-start.1 = (bf16[128,64]{0,1:T(8,128)(2,1)S(1)}, bf16[128,64]{0,1:T(8,128)(2,1)}, u32[]{:S(2)}) copy-start(bf16[128,64]{0,1:T(8,128)(2,1)} %param.9) | copy-start | bytes 49156
  85.5 52.2 %copy-start.2 = (bf16[128,64]{0,1:T(8,128)(2,1)S(1)}, bf16[128,64]{0,1:T(8,128)(2,1)}, u32[]{:S(2)}) copy-start(bf16[128,64]{0,1:T(8,128)(2,1)} %param.10) | copy-start | bytes 49156
  85.5 52.2 %copy-start.3 = (bf16[128,64]{0,1:T(8,128)(2,1)S(1)}, bf16[128,64]{0,1:T(8,128)(2,1)}, u32[]{:S(2)}) copy-start(bf16[128,64]{0,1:T(8,128)(2,1)} %param.11) | copy-start | bytes 49156
  142.0 1.3 collective-permute-start
  143.4 6.6 %collective-permute-start.1 = (f32[128,128]{1,0:T(8,128)S(1)}, f32[128,128]{1,0:T(8,128)S(1)}, u32[]{:S(2)}, u32[]{:S(2)}) collective-permute-start(f32[128,128]{1,0:T(8,128)S(1)} %add.15), channel_id=1, source_target_pairs={{0,16},{2,18},{4,20},{6,22},{8,24},{10,26},{12,28},{14,30},{16,0},... | collective-permute-start | bytes 196616 | tf_op jit(solution)/shard_map/ppermute | solution.py:401
  150.0 4.3 %collective-permute-start.2 = (f32[128,128]{1,0:T(8,128)S(1)}, f32[128,128]{1,0:T(8,128)S(1)}, u32[]{:S(2)}, u32[]{:S(2)}) collective-permute-start(f32[128,128]{1,0:T(8,128)S(1)} %add.16), channel_id=1, source_target_pairs={{0,8},{2,10},{4,12},{6,14},{8,0},{10,2},{12,4},{14,6},{16,24},{18,... | collective-permute-start | bytes 196616 | tf_op jit(solution)/shard_map/ppermute | solution.py:401
  154.3 4.3 %collective-permute-start.3 = (f32[128,128]{1,0:T(8,128)S(1)}, f32[128,128]{1,0:T(8,128)S(1)}, u32[]{:S(2)}, u32[]{:S(2)}) collective-permute-start(f32[128,128]{1,0:T(8,128)S(1)} %add.17), channel_id=1, source_target_pairs={{0,4},{2,6},{4,0},{6,2},{8,12},{10,14},{12,8},{14,10},{16,20},{18,... | collective-permute-start | bytes 196616 | tf_op jit(solution)/shard_map/ppermute | solution.py:401
  158.7 4.3 %collective-permute-start.4 = (f32[128,128]{1,0:T(8,128)S(1)}, f32[128,128]{1,0:T(8,128)S(1)}, u32[]{:S(2)}, u32[]{:S(2)}) collective-permute-start(f32[128,128]{1,0:T(8,128)S(1)} %add.18), channel_id=1, source_target_pairs={{0,1},{1,0},{2,3},{3,2},{4,5},{5,4},{6,7},{7,6},{8,9},{9,8},{10,11... | collective-permute-start | bytes 196616 | tf_op jit(solution)/shard_map/ppermute | solution.py:401
  163.0 1.3 collective-permute-start.5

commit v18 on v15

--- a/solution.py
+++ b/solution.py
@@ -137,10 +137,8 @@
 
     for i, w in enumerate((wl, wlg, wr, wrg)):
         weight(i, w).start()
-    for part in range(parts):
-        come(part).start()
+    come(0).start()
     cot = pltpu.make_async_copy(cot_hbm, out_ref.at[:, pl.ds(0, own)], cot_sem)
-    cot.start()
     for i, w in enumerate((wl, wlg, wr, wrg)):
         weight(i, w).wait()
 
@@ -163,6 +161,10 @@
     for part in range(parts + 1):
         if part < parts:
             come(part).wait()
+        if part == 0:
+            for later in range(1, parts):
+                come(later).start()
+            cot.start()
         for i in range(count):
             if part < parts:
                 one_row(part, i)

time: 165 us -> 165 us (level)
  no operation moved by 1% of the time
where the time goes in v18:
time: 165 us; the launch traced here: 164 us
  blocking collectives  130 us (79%)
  Pallas kernels  18.4 us (11%)
  waiting for transfers between devices  9.75 us (6%)
  starting transfers between devices  4.92 us (3%)
    all_to_all x2, blocking collectives, channel_shards(): exchange(sent)  130 us
    pallas_call x2, Pallas kernels, input_piece(): pl.pallas_call(functools.partial(input_kernel, piece * count), in_specs=[...  7.56 us
    ppermute x4, waiting for transfers between devices, channel_shards(): other = lax.ppermute(mine, axis, [(i, i ^ step) for i in range(size)])  7.28 us
    ppermute x4, starting transfers between devices, channel_shards(): other = lax.ppermute(mine, axis, [(i, i ^ step) for i in range(size)])  4.77 us
    pallas_call x1, Pallas kernels, channel_shards(): pl.pallas_call(functools.partial(before_kernel, own), in_specs=[hbm] * 6,...  4.69 us
    pallas_call x1, Pallas kernels, channel_shards(): pl.pallas_call(functools.partial(gates_kernel, own), in_specs=[hbm] + [vm...  4.18 us
  transfers between devices with their start and end apart: 6, of which 6 were waited for; matrix products, arithmetic and copies ran while one was open for 0% of the time, Pallas kernels for 5%

profile of v18, /device:TPU:0, one launch (start us, length us, event | category | flops | bytes accessed | tf_op | source)
XLA Modules:
  0.0 164.3 jit_solution(10522601634230375943)
XLA Ops:
  0.6 4.7 %before.1 = (bf16[32,6,32,256]{3,2,1,0:T(8,128)(2,1)S(1)}, bf16[32,128,256]{2,1,0:T(8,128)(2,1)}) custom-call(bf16[32,256,128]{2,1,0:T(8,128)(2,1)} %pair_hbm.5, bf16[32,2,32,256]{3,2,1,0:T(8,128)(2,1)} %bitcast.25, bf16[64,128]{1,0:T(8,128)(2,1)} %bitcast.9, bf16[64,128]{1,0:T(8,128)(2,1)} %bitcast.13, bf16[64,128]{1,0:T(8,128)(2,1)} %bitcast.17, ...), custom_call_target="tpu_custom_call" | custom-call | tf_op jit(solution)/shard_map/before/pallas_call | solution.py:316
  5.3 78.3 %all_to_all.10.in_ref = bf16[32,6,32,256]{3,2,1,0:T(8,128)(2,1)S(1)} all-to-all(bf16[32,6,32,256]{3,2,1,0:T(8,128)(2,1)S(1)} %get-tuple-element.19), channel_id=1, replica_groups=mesh['row'=16,'col'=2] {'row','col'}, dimensions={0} | all-to-all | bytes 6291456 | tf_op jit(solution)/shard_map/all_to_all | solution.py:350
  83.6 1.3 triangle.1
  84.9 0.0 copy-start
  84.9 0.0 copy-start.1
  84.9 0.0 copy-start.2
  84.9 0.0 copy-start.3
  84.9 52.2 %all_to_all.11.d_ref = bf16[32,4,32,256]{3,2,1,0:T(8,128)(2,1)S(1)} all-to-all(bf16[32,4,32,256]{3,2,1,0:T(8,128)(2,1)S(1)} %triangle.1), channel_id=1, replica_groups=mesh['row'=16,'col'=2] {'row','col'}, dimensions={0} | all-to-all | bytes 4194304 | tf_op jit(solution)/shard_map/all_to_all | solution.py:367
  137.1 0.0 copy-done
  137.1 0.0 copy-done.1
  137.1 0.0 copy-done.2
  137.1 0.0 copy-done.3
  137.1 4.2 %gates.1 = (bf16[32,256,256]{2,1,0:T(8,128)(2,1)S(1)}, f32[128,128]{1,0:T(8,128)S(1)}, f32[128,128]{1,0:T(8,128)S(1)}) custom-call(bf16[32,128,256]{2,1,0:T(8,128)(2,1)} %get-tuple-element.18.normed_hbm, bf16[32,4,32,256]{3,2,1,0:T(8,128)(2,1)S(1)} %all_to_all.11.d_ref, bf16[64,128]{1,0:T(8,128)(2,1)S(1)} %bitcast.10, bf16[64,128]{1,0:T(8,128)(2,1)S(1)} %bitcast.14, ...), custom_call_target="tpu_custom_call" | custom-call | tf_op jit(solution)/shard_map/gates/pallas_call | solution.py:353
  141.3 0.1 collective-permute-start
  141.4 1.2 collective-permute-done
  142.6 1.8 %collective-permute-start.1 = (f32[128,128]{1,0:T(8,128)S(1)}, f32[128,128]{1,0:T(8,128)S(1)}, u32[]{:S(2)}, u32[]{:S(2)}) collective-permute-start(f32[128,128]{1,0:T(8,128)S(1)} %add.15), channel_id=1, source_target_pairs={{0,16},{2,18},{4,20},{6,22},{8,24},{10,26},{12,28},{14,30},{16,0},... | collective-permute-start | bytes 196616 | tf_op jit(solution)/shard_map/ppermute | solution.py:397
  144.5 3.8 %input.2.refs_0_ = bf16[32,256,128]{2,1,0:T(8,128)(2,1)} custom-call(bf16[32,256,128]{2,1,0:T(8,128)(2,1)} %pair_hbm.5, bf16[32,256,256]{2,1,0:T(8,128)(2,1)S(1)} %get-tuple-element.22.grads_ref, bf16[64,128]{1,0:T(8,128)(2,1)S(1)} %bitcast.11, bf16[64,128]{1,0:T(8,128)(2,1)S(1)} %bitcast.15, bf16[64,128]{1,0:T(8,128)(2,1)S(1)} %bitcast.19, ...), custom_call_target="tpu_custom_call" | custom-call | flops 268435456 | bytes 2097152 | tf_op jit(solution)/shard_map/input/pallas_call | solution.py:372
  148.3 1.0 collective-permute-done.1
  149.3 0.4 collective-permute-start.2
  149.7 3.8 %input.3 = bf16[32,256,128]{2,1,0:T(8,128)(2,1)} custom-call(bf16[32,256,128]{2,1,0:T(8,128)(2,1)} %pair_hbm.5, bf16[32,256,256]{2,1,0:T(8,128)(2,1)S(1)} %get-tuple-element.22.grads_ref, bf16[64,128]{1,0:T(8,128)(2,1)S(1)} %bitcast.12, bf16[64,128]{1,0:T(8,128)(2,1)S(1)} %bitcast.16, bf16[64,128]{1,0:T(8,128)(2,1)S(1)} %bitcast.20, ...), custom_call_target="tpu_custom_call", output_to_operand_aliasing={{}: (6, {})} | custom-call | flops 268435456 | bytes 2097152 | tf_op jit(solution)/shard_map/input/pallas_call | solution.py:372
  153.4 0.2 collective-permute-done.2
  153.6 1.2 collective-permute-start.3
  154.8 3.2 %collective-permute-done.3 = f32[128,128]{1,0:T(8,128)S(1)} collective-permute-done((f32[128,128]{1,0:T(8,128)S(1)}, f32[128,128]{1,0:T(8,128)S(1)}, u32[]{:S(2)}, u32[]{:S(2)}) %collective-permute-start.3) | collective-permute-done | bytes 65568 | tf_op jit(solution)/shard_map/ppermute | solution.py:397
  158.0 1.4 collective-permute-start.4
  159.4 2.9 %collective-permute-done.4 = f32[128,128]{1,0:T(8,128)S(1)} collective-permute-done((f32[128,128]{1,0:T(8,128)S(1)}, f32[128,128]{1,0:T(8,128)S(1)}, u32[]{:S(2)}, u32[]{:S(2)}) %collective-permute-start.4) | collective-permute-done | bytes 65568 | tf_op jit(solution)/shard_map/ppermute | solution.py:397
  162.3 0.1 collective-permute-start.5
  162.4 1.2 collective-permute-done.5.other_ref
  163.6 0.7 finish.1
  (5 shorter events, 0.0 us)
Async XLA Ops:
  84.9 52.2 %copy-start = (bf16[128,64]{0,1:T(8,128)(2,1)S(1)}, bf16[128,64]{0,1:T(8,128)(2,1)}, u32[]{:S(2)}) copy-start(bf16[128,64]{0,1:T(8,128)(2,1)} %param.8) | copy-start | bytes 49156
  84.9 52.2 %copy-start.1 = (bf16[128,64]{0,1:T(8,128)(2,1)S(1)}, bf16[128,64]{0,1:T(8,128)(2,1)}, u32[]{:S(2)}) copy-start(bf16[128,64]{0,1:T(8,128)(2,1)} %param.9) | copy-start | bytes 49156
  84.9 52.2 %copy-start.2 = (bf16[128,64]{0,1:T(8,128)(2,1)S(1)}, bf16[128,64]{0,1:T(8,128)(2,1)}, u32[]{:S(2)}) copy-start(bf16[128,64]{0,1:T(8,128)(2,1)} %param.10) | copy-start | bytes 49156
  84.9 52.2 %copy-start.3 = (bf16[128,64]{0,1:T(8,128)(2,1)S(1)}, bf16[128,64]{0,1:T(8,128)(2,1)}, u32[]{:S(2)}) copy-start(bf16[128,64]{0,1:T(8,128)(2,1)} %param.11) | copy-start | bytes 49156
  141.3 1.3 collective-permute-start
  142.6 6.6 %collective-permute-start.1 = (f32[128,128]{1,0:T(8,128)S(1)}, f32[128,128]{1,0:T(8,128)S(1)}, u32[]{:S(2)}, u32[]{:S(2)}) collective-permute-start(f32[128,128]{1,0:T(8,128)S(1)} %add.15), channel_id=1, source_target_pairs={{0,16},{2,18},{4,20},{6,22},{8,24},{10,26},{12,28},{14,30},{16,0},... | collective-permute-start | bytes 196616 | tf_op jit(solution)/shard_map/ppermute | solution.py:397
  149.3 4.3 %collective-permute-start.2 = (f32[128,128]{1,0:T(8,128)S(1)}, f32[128,128]{1,0:T(8,128)S(1)}, u32[]{:S(2)}, u32[]{:S(2)}) collective-permute-start(f32[128,128]{1,0:T(8,128)S(1)} %add.16), channel_id=1, source_target_pairs={{0,8},{2,10},{4,12},{6,14},{8,0},{10,2},{12,4},{14,6},{16,24},{18,... | collective-permute-start | bytes 196616 | tf_op jit(solution)/shard_map/ppermute | solution.py:397
  153.6 4.3 %collective-permute-start.3 = (f32[128,128]{1,0:T(8,128)S(1)}, f32[128,128]{1,0:T(8,128)S(1)}, u32[]{:S(2)}, u32[]{:S(2)}) collective-permute-start(f32[128,128]{1,0:T(8,128)S(1)} %add.17), channel_id=1, source_target_pairs={{0,4},{2,6},{4,0},{6,2},{8,12},{10,14},{12,8},{14,10},{16,20},{18,... | collective-permute-start | bytes 196616 | tf_op jit(solution)/shard_map/ppermute | solution.py:397
  158.0 4.3 %collective-permute-start.4 = (f32[128,128]{1,0:T(8,128)S(1)}, f32[128,128]{1,0:T(8,128)S(1)}, u32[]{:S(2)}, u32[]{:S(2)}) collective-permute-start(f32[128,128]{1,0:T(8,128)S(1)} %add.18), channel_id=1, source_target_pairs={{0,1},{1,0},{2,3},{3,2},{4,5},{5,4},{6,7},{7,6},{8,9},{9,8},{10,11... | collective-permute-start | bytes 196616 | tf_op jit(solution)/shard_map/ppermute | solution.py:397
  162.3 1.3 collective-permute-start.5

commit v19 on v15

--- a/solution.py
+++ b/solution.py
@@ -385,7 +385,8 @@
             name="input",
         )(pair, grads, *weights, *held)
 
-    steps = [("row", rows, 1 << i) for i in range(1, rows.bit_length() - 1)][::-1]
+    steps = [("row", rows, 1 << i) for i in range(1, rows.bit_length() - 1)]
+    steps = steps[1:] + steps[:1]
     steps += [("col", cols, 1 << i) for i in range(cols.bit_length() - 1)]
     pieces = min(pieces, len(steps))
     neighbours = [(i, i ^ 1) for i in range(rows)]

time: 165 us -> 165 us (level)
  transfers between devices with their start and end apart: 6 -> 6, of which waited for: 6 -> 5; matrix products, arithmetic and copies ran while one was open for 0% -> 0% of each run, Pallas kernels for 5% -> 5%
where the time goes in v19:
time: 165 us
  blocking collectives  130 us (79%)
  Pallas kernels  18.3 us (11%)
  waiting for transfers between devices  10.6 us (6%)
  starting transfers between devices  4.71 us (3%)
    all_to_all x2, blocking collectives, channel_shards(): exchange(sent)  130 us
    ppermute x4, waiting for transfers between devices, channel_shards(): other = lax.ppermute(mine, axis, [(i, i ^ step) for i in range(size)])  8.09 us
    pallas_call x2, Pallas kernels, input_piece(): pl.pallas_call(functools.partial(input_kernel, piece * count), in_specs=[...  7.56 us
    pallas_call x1, Pallas kernels, channel_shards(): pl.pallas_call(functools.partial(before_kernel, own), in_specs=[hbm] * 6,...  4.61 us
    ppermute x4, starting transfers between devices, channel_shards(): other = lax.ppermute(mine, axis, [(i, i ^ step) for i in range(size)])  4.56 us
    pallas_call x1, Pallas kernels, channel_shards(): pl.pallas_call(functools.partial(gates_kernel, own), in_specs=[hbm] + [vm...  4.19 us
  transfers between devices with their start and end apart: 6, of which 5 were waited for; matrix products, arithmetic and copies ran while one was open for 0% of the time, Pallas kernels for 5%

profile of v19, /device:TPU:0, one launch (start us, length us, event | category | flops | bytes accessed | tf_op | source)
XLA Modules:
  0.0 164.8 jit_solution(7281221628030902777)
XLA Ops:
  0.6 4.6 %before.1 = (bf16[32,6,32,256]{3,2,1,0:T(8,128)(2,1)S(1)}, bf16[32,128,256]{2,1,0:T(8,128)(2,1)}) custom-call(bf16[32,256,128]{2,1,0:T(8,128)(2,1)} %pair_hbm.5, bf16[32,2,32,256]{3,2,1,0:T(8,128)(2,1)} %bitcast.25, bf16[64,128]{1,0:T(8,128)(2,1)} %bitcast.9, bf16[64,128]{1,0:T(8,128)(2,1)} %bitcast.13, bf16[64,128]{1,0:T(8,128)(2,1)} %bitcast.17, ...), custom_call_target="tpu_custom_call" | custom-call | tf_op jit(solution)/shard_map/before/pallas_call | solution.py:314
  5.2 78.3 %all_to_all.10.in_ref = bf16[32,6,32,256]{3,2,1,0:T(8,128)(2,1)S(1)} all-to-all(bf16[32,6,32,256]{3,2,1,0:T(8,128)(2,1)S(1)} %get-tuple-element.19), channel_id=1, replica_groups=mesh['row'=16,'col'=2] {'row','col'}, dimensions={0} | all-to-all | bytes 6291456 | tf_op jit(solution)/shard_map/all_to_all | solution.py:348
  83.5 1.3 triangle.1
  84.8 0.0 copy-start
  84.8 0.0 copy-start.1
  84.8 0.0 copy-start.2
  84.8 0.0 copy-start.3
  84.9 52.2 %all_to_all.11.d_ref = bf16[32,4,32,256]{3,2,1,0:T(8,128)(2,1)S(1)} all-to-all(bf16[32,4,32,256]{3,2,1,0:T(8,128)(2,1)S(1)} %triangle.1), channel_id=1, replica_groups=mesh['row'=16,'col'=2] {'row','col'}, dimensions={0} | all-to-all | bytes 4194304 | tf_op jit(solution)/shard_map/all_to_all | solution.py:365
  137.0 0.0 copy-done
  137.0 0.0 copy-done.1
  137.0 0.0 copy-done.2
  137.0 0.0 copy-done.3
  137.0 4.2 %gates.1 = (bf16[32,256,256]{2,1,0:T(8,128)(2,1)S(1)}, f32[128,128]{1,0:T(8,128)S(1)}, f32[128,128]{1,0:T(8,128)S(1)}) custom-call(bf16[32,128,256]{2,1,0:T(8,128)(2,1)} %get-tuple-element.18.normed_hbm, bf16[32,4,32,256]{3,2,1,0:T(8,128)(2,1)S(1)} %all_to_all.11.d_ref, bf16[64,128]{1,0:T(8,128)(2,1)S(1)} %bitcast.10, bf16[64,128]{1,0:T(8,128)(2,1)S(1)} %bitcast.14, ...), custom_call_target="tpu_custom_call" | custom-call | tf_op jit(solution)/shard_map/gates/pallas_call | solution.py:351
  141.2 0.1 collective-permute-start
  141.3 1.2 collective-permute-done
  142.6 1.6 collective-permute-start.1
  144.1 3.8 %input.2.refs_0_ = bf16[32,256,128]{2,1,0:T(8,128)(2,1)} custom-call(bf16[32,256,128]{2,1,0:T(8,128)(2,1)} %pair_hbm.5, bf16[32,256,256]{2,1,0:T(8,128)(2,1)S(1)} %get-tuple-element.22.grads_ref, bf16[64,128]{1,0:T(8,128)(2,1)S(1)} %bitcast.11, bf16[64,128]{1,0:T(8,128)(2,1)S(1)} %bitcast.15, bf16[64,128]{1,0:T(8,128)(2,1)S(1)} %bitcast.19, ...), custom_call_target="tpu_custom_call" | custom-call | flops 268435456 | bytes 2097152 | tf_op jit(solution)/shard_map/input/pallas_call | solution.py:370
  147.9 0.0 collective-permute-done.1
  148.0 0.8 collective-permute-start.2
  148.7 3.8 %input.3 = bf16[32,256,128]{2,1,0:T(8,128)(2,1)} custom-call(bf16[32,256,128]{2,1,0:T(8,128)(2,1)} %pair_hbm.5, bf16[32,256,256]{2,1,0:T(8,128)(2,1)S(1)} %get-tuple-element.22.grads_ref, bf16[64,128]{1,0:T(8,128)(2,1)S(1)} %bitcast.12, bf16[64,128]{1,0:T(8,128)(2,1)S(1)} %bitcast.16, bf16[64,128]{1,0:T(8,128)(2,1)S(1)} %bitcast.20, ...), custom_call_target="tpu_custom_call", output_to_operand_aliasing={{}: (6, {})} | custom-call | flops 268435456 | bytes 2097152 | tf_op jit(solution)/shard_map/input/pallas_call | solution.py:370
  152.5 1.6 collective-permute-done.2
  154.2 1.0 collective-permute-start.3
  155.2 3.3 %collective-permute-done.3 = f32[128,128]{1,0:T(8,128)S(1)} collective-permute-done((f32[128,128]{1,0:T(8,128)S(1)}, f32[128,128]{1,0:T(8,128)S(1)}, u32[]{:S(2)}, u32[]{:S(2)}) %collective-permute-start.3) | collective-permute-done | bytes 65568 | tf_op jit(solution)/shard_map/ppermute | solution.py:396
  158.5 1.2 collective-permute-start.4
  159.7 3.2 %collective-permute-done.4 = f32[128,128]{1,0:T(8,128)S(1)} collective-permute-done((f32[128,128]{1,0:T(8,128)S(1)}, f32[128,128]{1,0:T(8,128)S(1)}, u32[]{:S(2)}, u32[]{:S(2)}) %collective-permute-start.4) | collective-permute-done | bytes 65568 | tf_op jit(solution)/shard_map/ppermute | solution.py:396
  162.9 0.1 collective-permute-start.5
  162.9 1.2 collective-permute-done.5.other_ref
  164.2 0.7 finish.1
  (5 shorter events, 0.0 us)
Async XLA Ops:
  84.8 52.2 %copy-start = (bf16[128,64]{0,1:T(8,128)(2,1)S(1)}, bf16[128,64]{0,1:T(8,128)(2,1)}, u32[]{:S(2)}) copy-start(bf16[128,64]{0,1:T(8,128)(2,1)} %param.8) | copy-start | bytes 49156
  84.8 52.2 %copy-start.1 = (bf16[128,64]{0,1:T(8,128)(2,1)S(1)}, bf16[128,64]{0,1:T(8,128)(2,1)}, u32[]{:S(2)}) copy-start(bf16[128,64]{0,1:T(8,128)(2,1)} %param.9) | copy-start | bytes 49156
  84.8 52.2 %copy-start.2 = (bf16[128,64]{0,1:T(8,128)(2,1)S(1)}, bf16[128,64]{0,1:T(8,128)(2,1)}, u32[]{:S(2)}) copy-start(bf16[128,64]{0,1:T(8,128)(2,1)} %param.10) | copy-start | bytes 49156
  84.8 52.2 %copy-start.3 = (bf16[128,64]{0,1:T(8,128)(2,1)S(1)}, bf16[128,64]{0,1:T(8,128)(2,1)}, u32[]{:S(2)}) copy-start(bf16[128,64]{0,1:T(8,128)(2,1)} %param.11) | copy-start | bytes 49156
  141.2 1.3 collective-permute-start
  142.6 5.4 %collective-permute-start.1 = (f32[128,128]{1,0:T(8,128)S(1)}, f32[128,128]{1,0:T(8,128)S(1)}, u32[]{:S(2)}, u32[]{:S(2)}) collective-permute-start(f32[128,128]{1,0:T(8,128)S(1)} %add.15), channel_id=1, source_target_pairs={{0,8},{2,10},{4,12},{6,14},{8,0},{10,2},{12,4},{14,6},{16,24},{18,... | collective-permute-start | bytes 196616 | tf_op jit(solution)/shard_map/ppermute | solution.py:396
  148.0 6.2 %collective-permute-start.2 = (f32[128,128]{1,0:T(8,128)S(1)}, f32[128,128]{1,0:T(8,128)S(1)}, u32[]{:S(2)}, u32[]{:S(2)}) collective-permute-start(f32[128,128]{1,0:T(8,128)S(1)} %add.16), channel_id=1, source_target_pairs={{0,16},{2,18},{4,20},{6,22},{8,24},{10,26},{12,28},{14,30},{16,0},... | collective-permute-start | bytes 196616 | tf_op jit(solution)/shard_map/ppermute | solution.py:396
  154.2 4.3 %collective-permute-start.3 = (f32[128,128]{1,0:T(8,128)S(1)}, f32[128,128]{1,0:T(8,128)S(1)}, u32[]{:S(2)}, u32[]{:S(2)}) collective-permute-start(f32[128,128]{1,0:T(8,128)S(1)} %add.17), channel_id=1, source_target_pairs={{0,4},{2,6},{4,0},{6,2},{8,12},{10,14},{12,8},{14,10},{16,20},{18,... | collective-permute-start | bytes 196616 | tf_op jit(solution)/shard_map/ppermute | solution.py:396
  158.5 4.3 %collective-permute-start.4 = (f32[128,128]{1,0:T(8,128)S(1)}, f32[128,128]{1,0:T(8,128)S(1)}, u32[]{:S(2)}, u32[]{:S(2)}) collective-permute-start(f32[128,128]{1,0:T(8,128)S(1)} %add.18), channel_id=1, source_target_pairs={{0,1},{1,0},{2,3},{3,2},{4,5},{5,4},{6,7},{7,6},{8,9},{9,8},{10,11... | collective-permute-start | bytes 196616 | tf_op jit(solution)/shard_map/ppermute | solution.py:396
  162.9 1.3 collective-permute-start.5

commit v20 on v15

--- a/solution.py
+++ b/solution.py
@@ -123,6 +123,8 @@
     parts = in_sems.shape[0]
     count = rows // parts
     pitch = count + 1
+    rows_each = count
+    pair_of = 2 if count % 2 == 0 else 1
 
     def come(part):
         at = pl.ds(part * count, count)
@@ -144,13 +146,18 @@
     for i, w in enumerate((wl, wlg, wr, wrg)):
         weight(i, w).wait()
 
-    def one_row(part, i):
-        r = part * count + i
-        normed = layer_norm(pair_ref[r])[0].astype(BF16)
-        normed_ref[r] = normed
-        q_left, s_left, q_right, s_right = project(w_ref, normed)
-        put_lanes(rows_refs[part], pl.ds(i, h, stride=pitch), s_left * q_left)
-        put_lanes(rows_refs[part], pl.ds(i + h * pitch, h, stride=pitch), s_right * q_right)
+    def some_rows(part, first, count):
+        all_normed = []
+        for i in range(first, first + count):
+            all_normed.append(layer_norm(pair_ref[part * rows_each + i])[0].astype(BF16))
+            normed_ref[part * rows_each + i] = all_normed[-1]
+        columns = all_normed[0].shape[1]
+        q_left, s_left, q_right, s_right = project(w_ref, jnp.concatenate(all_normed, axis=1))
+        left, right = s_left * q_left, s_right * q_right
+        for n in range(count):
+            i, at = first + n, slice(n * columns, (n + 1) * columns)
+            put_lanes(rows_refs[part], pl.ds(i, h, stride=pitch), left[:, at])
+            put_lanes(rows_refs[part], pl.ds(i + h * pitch, h, stride=pitch), right[:, at])
 
     def some_channels(part, i):
         for channel in range(i * h // count, (i + 1) * h // count):
@@ -164,8 +171,8 @@
         if part < parts:
             come(part).wait()
         for i in range(count):
-            if part < parts:
-                one_row(part, i)
+            if part < parts and i % pair_of == 0:
+                some_rows(part, i, pair_of)
             if part > 0:
                 some_channels(part - 1, i)
         if part < parts:
@@ -201,6 +208,8 @@
     parts = len(rows_refs)
     count = rows // parts
     pitch = count + 1
+    rows_each = count
+    pair_of = 2 if count % 2 == 0 else 1
     stack_weights((wl, wlg, wr, wrg), w_ref)
 
     def some_channels(part, i):
@@ -210,15 +219,24 @@
                 line = d_ref[to, slot + side, pl.ds(part * count, count), :].astype(F32)
                 put_lanes(rows_refs[part], pl.ds((side * h + channel) * pitch, count), line)
 
-    def one_row(part, i):
-        normed = normed_ref[part * count + i]
+    def some_rows(part, first, count):
+        at = [part * rows_each + first + n for n in range(count)]
+        normed = jnp.concatenate([normed_ref[r] for r in at], axis=1)
         q_left, s_left, q_right, s_right = project(w_ref, normed)
-        e_left = get_lanes(rows_refs[part], pl.ds(i, h, stride=pitch)) * s_left
-        e_right = get_lanes(rows_refs[part], pl.ds(i + h * pitch, h, stride=pitch)) * s_right
+
+        def lines(start):
+            starts = [start + first + n for n in range(count)]
+            each = [get_lanes(rows_refs[part], pl.ds(n, h, stride=pitch)) for n in starts]
+            return jnp.concatenate(each, axis=1)
+
+        e_left = lines(0) * s_left
+        e_right = lines(h * pitch) * s_right
         f_left = e_left * q_left * (1.0 - s_left)
         f_right = e_right * q_right * (1.0 - s_right)
         grads = jnp.concatenate([e_left, f_left, e_right, f_right], axis=0).astype(BF16)
-        grads_ref[part * count + i] = grads
+        columns = grads_ref.shape[2]
+        for n, r in enumerate(at):
+            grads_ref[r] = grads[:, n * columns : (n + 1) * columns]
         return grads, normed
 
     together = 8 if count % 8 == 0 else count
@@ -228,11 +246,11 @@
             copy.wait()
         done = []
         for i in range(count):
-            if part > 0:
-                done.append(one_row(part - 1, i))
+            if part > 0 and i % pair_of == 0:
+                done.append(some_rows(part - 1, i, pair_of))
             if part < parts:
                 some_channels(part, i)
-            if len(done) == together:
+            if len(done) * pair_of == together:
                 all_grads, all_normed = (jnp.concatenate(x, axis=1) for x in zip(*done))
                 sums_ref[...] += dot(all_grads, all_normed, NT)
                 done = []

time: 165 us -> 165 us (level)
  no operation moved by 1% of the time
where the time goes in v20:
time: 165 us; the launch traced here: 164 us
  blocking collectives  130 us (79%)
  Pallas kernels  18.3 us (11%)
  waiting for transfers between devices  9.77 us (6%)
  starting transfers between devices  4.91 us (3%)
    all_to_all x2, blocking collectives, channel_shards(): exchange(sent)  130 us
    pallas_call x2, Pallas kernels, input_piece(): pl.pallas_call(functools.partial(input_kernel, piece * count), in_specs=[...  7.56 us
    ppermute x4, waiting for transfers between devices, channel_shards(): other = lax.ppermute(mine, axis, [(i, i ^ step) for i in range(size)])  7.29 us
    ppermute x4, starting transfers between devices, channel_shards(): other = lax.ppermute(mine, axis, [(i, i ^ step) for i in range(size)])  4.76 us
    pallas_call x1, Pallas kernels, channel_shards(): pl.pallas_call(functools.partial(before_kernel, own), in_specs=[hbm] * 6,...  4.61 us
    pallas_call x1, Pallas kernels, channel_shards(): pl.pallas_call(functools.partial(gates_kernel, own), in_specs=[hbm] + [vm...  4.18 us
  transfers between devices with their start and end apart: 6, of which 6 were waited for; matrix products, arithmetic and copies ran while one was open for 0% of the time, Pallas kernels for 5%

profile of v20, /device:TPU:0, one launch (start us, length us, event | category | flops | bytes accessed | tf_op | source)
XLA Modules:
  0.0 164.2 jit_solution(8749097966978759825)
XLA Ops:
  0.6 4.6 %before.1 = (bf16[32,6,32,256]{3,2,1,0:T(8,128)(2,1)S(1)}, bf16[32,128,256]{2,1,0:T(8,128)(2,1)}) custom-call(bf16[32,256,128]{2,1,0:T(8,128)(2,1)} %pair_hbm.5, bf16[32,2,32,256]{3,2,1,0:T(8,128)(2,1)} %bitcast.25, bf16[64,128]{1,0:T(8,128)(2,1)} %bitcast.9, bf16[64,128]{1,0:T(8,128)(2,1)} %bitcast.13, bf16[64,128]{1,0:T(8,128)(2,1)} %bitcast.17, ...), custom_call_target="tpu_custom_call" | custom-call | tf_op jit(solution)/shard_map/before/pallas_call | solution.py:332
  5.2 78.3 %all_to_all.10.in_ref = bf16[32,6,32,256]{3,2,1,0:T(8,128)(2,1)S(1)} all-to-all(bf16[32,6,32,256]{3,2,1,0:T(8,128)(2,1)S(1)} %get-tuple-element.19), channel_id=1, replica_groups=mesh['row'=16,'col'=2] {'row','col'}, dimensions={0} | all-to-all | bytes 6291456 | tf_op jit(solution)/shard_map/all_to_all | solution.py:366
  83.5 1.3 triangle.1
  84.8 0.0 copy-start
  84.8 0.0 copy-start.1
  84.8 0.0 copy-start.2
  84.8 0.0 copy-start.3
  84.9 52.2 %all_to_all.11.d_ref = bf16[32,4,32,256]{3,2,1,0:T(8,128)(2,1)S(1)} all-to-all(bf16[32,4,32,256]{3,2,1,0:T(8,128)(2,1)S(1)} %triangle.1), channel_id=1, replica_groups=mesh['row'=16,'col'=2] {'row','col'}, dimensions={0} | all-to-all | bytes 4194304 | tf_op jit(solution)/shard_map/all_to_all | solution.py:383
  137.0 0.0 copy-done
  137.0 0.0 copy-done.1
  137.0 0.0 copy-done.2
  137.0 0.0 copy-done.3
  137.0 4.2 %gates.1 = (bf16[32,256,256]{2,1,0:T(8,128)(2,1)S(1)}, f32[128,128]{1,0:T(8,128)S(1)}, f32[128,128]{1,0:T(8,128)S(1)}) custom-call(bf16[32,128,256]{2,1,0:T(8,128)(2,1)} %get-tuple-element.18.normed_hbm, bf16[32,4,32,256]{3,2,1,0:T(8,128)(2,1)S(1)} %all_to_all.11.d_ref, bf16[64,128]{1,0:T(8,128)(2,1)S(1)} %bitcast.10, bf16[64,128]{1,0:T(8,128)(2,1)S(1)} %bitcast.14, ...), custom_call_target="tpu_custom_call" | custom-call | tf_op jit(solution)/shard_map/gates/pallas_call | solution.py:369
  141.2 0.1 collective-permute-start
  141.3 1.2 collective-permute-done
  142.6 1.8 %collective-permute-start.1 = (f32[128,128]{1,0:T(8,128)S(1)}, f32[128,128]{1,0:T(8,128)S(1)}, u32[]{:S(2)}, u32[]{:S(2)}) collective-permute-start(f32[128,128]{1,0:T(8,128)S(1)} %add.15), channel_id=1, source_target_pairs={{0,16},{2,18},{4,20},{6,22},{8,24},{10,26},{12,28},{14,30},{16,0},... | collective-permute-start | bytes 196616 | tf_op jit(solution)/shard_map/ppermute | solution.py:413
  144.4 3.8 %input.2.refs_0_ = bf16[32,256,128]{2,1,0:T(8,128)(2,1)} custom-call(bf16[32,256,128]{2,1,0:T(8,128)(2,1)} %pair_hbm.5, bf16[32,256,256]{2,1,0:T(8,128)(2,1)S(1)} %get-tuple-element.22.grads_ref, bf16[64,128]{1,0:T(8,128)(2,1)S(1)} %bitcast.11, bf16[64,128]{1,0:T(8,128)(2,1)S(1)} %bitcast.15, bf16[64,128]{1,0:T(8,128)(2,1)S(1)} %bitcast.19, ...), custom_call_target="tpu_custom_call" | custom-call | flops 268435456 | bytes 2097152 | tf_op jit(solution)/shard_map/input/pallas_call | solution.py:388
  148.2 1.0 collective-permute-done.1
  149.2 0.4 collective-permute-start.2
  149.6 3.8 %input.3 = bf16[32,256,128]{2,1,0:T(8,128)(2,1)} custom-call(bf16[32,256,128]{2,1,0:T(8,128)(2,1)} %pair_hbm.5, bf16[32,256,256]{2,1,0:T(8,128)(2,1)S(1)} %get-tuple-element.22.grads_ref, bf16[64,128]{1,0:T(8,128)(2,1)S(1)} %bitcast.12, bf16[64,128]{1,0:T(8,128)(2,1)S(1)} %bitcast.16, bf16[64,128]{1,0:T(8,128)(2,1)S(1)} %bitcast.20, ...), custom_call_target="tpu_custom_call", output_to_operand_aliasing={{}: (6, {})} | custom-call | flops 268435456 | bytes 2097152 | tf_op jit(solution)/shard_map/input/pallas_call | solution.py:388
  153.4 0.2 collective-permute-done.2
  153.6 1.2 collective-permute-start.3
  154.7 3.2 %collective-permute-done.3 = f32[128,128]{1,0:T(8,128)S(1)} collective-permute-done((f32[128,128]{1,0:T(8,128)S(1)}, f32[128,128]{1,0:T(8,128)S(1)}, u32[]{:S(2)}, u32[]{:S(2)}) %collective-permute-start.3) | collective-permute-done | bytes 65568 | tf_op jit(solution)/shard_map/ppermute | solution.py:413
  157.9 1.4 collective-permute-start.4
  159.3 2.9 %collective-permute-done.4 = f32[128,128]{1,0:T(8,128)S(1)} collective-permute-done((f32[128,128]{1,0:T(8,128)S(1)}, f32[128,128]{1,0:T(8,128)S(1)}, u32[]{:S(2)}, u32[]{:S(2)}) %collective-permute-start.4) | collective-permute-done | bytes 65568 | tf_op jit(solution)/shard_map/ppermute | solution.py:413
  162.2 0.1 collective-permute-start.5
  162.3 1.2 collective-permute-done.5.other_ref
  163.6 0.7 finish.1
  (5 shorter events, 0.0 us)
Async XLA Ops:
  84.8 52.2 %copy-start = (bf16[128,64]{0,1:T(8,128)(2,1)S(1)}, bf16[128,64]{0,1:T(8,128)(2,1)}, u32[]{:S(2)}) copy-start(bf16[128,64]{0,1:T(8,128)(2,1)} %param.8) | copy-start | bytes 49156
  84.8 52.2 %copy-start.1 = (bf16[128,64]{0,1:T(8,128)(2,1)S(1)}, bf16[128,64]{0,1:T(8,128)(2,1)}, u32[]{:S(2)}) copy-start(bf16[128,64]{0,1:T(8,128)(2,1)} %param.9) | copy-start | bytes 49156
  84.8 52.2 %copy-start.2 = (bf16[128,64]{0,1:T(8,128)(2,1)S(1)}, bf16[128,64]{0,1:T(8,128)(2,1)}, u32[]{:S(2)}) copy-start(bf16[128,64]{0,1:T(8,128)(2,1)} %param.10) | copy-start | bytes 49156
  84.8 52.2 %copy-start.3 = (bf16[128,64]{0,1:T(8,128)(2,1)S(1)}, bf16[128,64]{0,1:T(8,128)(2,1)}, u32[]{:S(2)}) copy-start(bf16[128,64]{0,1:T(8,128)(2,1)} %param.11) | copy-start | bytes 49156
  141.2 1.3 collective-permute-start
  142.6 6.6 %collective-permute-start.1 = (f32[128,128]{1,0:T(8,128)S(1)}, f32[128,128]{1,0:T(8,128)S(1)}, u32[]{:S(2)}, u32[]{:S(2)}) collective-permute-start(f32[128,128]{1,0:T(8,128)S(1)} %add.15), channel_id=1, source_target_pairs={{0,16},{2,18},{4,20},{6,22},{8,24},{10,26},{12,28},{14,30},{16,0},... | collective-permute-start | bytes 196616 | tf_op jit(solution)/shard_map/ppermute | solution.py:413
  149.2 4.3 %collective-permute-start.2 = (f32[128,128]{1,0:T(8,128)S(1)}, f32[128,128]{1,0:T(8,128)S(1)}, u32[]{:S(2)}, u32[]{:S(2)}) collective-permute-start(f32[128,128]{1,0:T(8,128)S(1)} %add.16), channel_id=1, source_target_pairs={{0,8},{2,10},{4,12},{6,14},{8,0},{10,2},{12,4},{14,6},{16,24},{18,... | collective-permute-start | bytes 196616 | tf_op jit(solution)/shard_map/ppermute | solution.py:413
  153.6 4.3 %collective-permute-start.3 = (f32[128,128]{1,0:T(8,128)S(1)}, f32[128,128]{1,0:T(8,128)S(1)}, u32[]{:S(2)}, u32[]{:S(2)}) collective-permute-start(f32[128,128]{1,0:T(8,128)S(1)} %add.17), channel_id=1, source_target_pairs={{0,4},{2,6},{4,0},{6,2},{8,12},{10,14},{12,8},{14,10},{16,20},{18,... | collective-permute-start | bytes 196616 | tf_op jit(solution)/shard_map/ppermute | solution.py:413
  157.9 4.3 %collective-permute-start.4 = (f32[128,128]{1,0:T(8,128)S(1)}, f32[128,128]{1,0:T(8,128)S(1)}, u32[]{:S(2)}, u32[]{:S(2)}) collective-permute-start(f32[128,128]{1,0:T(8,128)S(1)} %add.18), channel_id=1, source_target_pairs={{0,1},{1,0},{2,3},{3,2},{4,5},{5,4},{6,7},{7,6},{8,9},{9,8},{10,11... | collective-permute-start | bytes 196616 | tf_op jit(solution)/shard_map/ppermute | solution.py:413
  162.2 1.3 collective-permute-start.5

commit v21 on v15

--- a/solution.py
+++ b/solution.py
@@ -193,14 +193,19 @@
 
 
 def gates_kernel(own, normed_hbm, d_ref, wl, wlg, wr, wrg, grads_ref, kept_ref, sent_ref, *scratch):
-    w_ref, sums_ref, *rows_refs, normed_ref, sem = scratch
-    copy = pltpu.make_async_copy(normed_hbm, normed_ref, sem)
-    copy.start()
+    w_ref, sums_ref, *rows_refs, normed_ref, sems = scratch
     h = wl.shape[0]
     rows = grads_ref.shape[0]
     parts = len(rows_refs)
     count = rows // parts
     pitch = count + 1
+
+    def come(part):
+        at = pl.ds(part * count, count)
+        return pltpu.make_async_copy(normed_hbm.at[at], normed_ref.at[at], sems.at[part])
+
+    for part in range(parts):
+        come(part).start()
     stack_weights((wl, wlg, wr, wrg), w_ref)
 
     def some_channels(part, i):
@@ -224,8 +229,8 @@
     together = 8 if count % 8 == 0 else count
     sums_ref[...] = jnp.zeros_like(sums_ref)
     for part in range(parts + 1):
-        if part == 1:
-            copy.wait()
+        if part > 0:
+            come(part - 1).wait()
         done = []
         for i in range(count):
             if part > 0:
@@ -358,7 +363,7 @@
             pltpu.VMEM((4 * hidden, dim), F32),
             *[rows_scratch] * parts,
             pltpu.VMEM(normed_shape.shape, BF16),
-            pltpu.SemaphoreType.DMA,
+            pltpu.SemaphoreType.DMA((parts,)),
         ],
         compiler_params=memory(28),
         name="gates",

time: 165 us -> 164 us (level)
  no operation moved by 1% of the time
where the time goes in v21:
time: 164 us
  blocking collectives  130 us (79%)
  Pallas kernels  18.1 us (11%)
  waiting for transfers between devices  9.76 us (6%)
  starting transfers between devices  4.92 us (3%)
    all_to_all x2, blocking collectives, channel_shards(): exchange(sent)  130 us
    pallas_call x2, Pallas kernels, input_piece(): pl.pallas_call(functools.partial(input_kernel, piece * count), in_specs=[...  7.56 us
    ppermute x4, waiting for transfers between devices, channel_shards(): other = lax.ppermute(mine, axis, [(i, i ^ step) for i in range(size)])  7.28 us
    ppermute x4, starting transfers between devices, channel_shards(): other = lax.ppermute(mine, axis, [(i, i ^ step) for i in range(size)])  4.77 us
    pallas_call x1, Pallas kernels, channel_shards(): pl.pallas_call(functools.partial(before_kernel, own), in_specs=[hbm] * 6,...  4.61 us
    pallas_call x1, Pallas kernels, channel_shards(): pl.pallas_call(functools.partial(gates_kernel, own), in_specs=[hbm] + [vm...  4 us
  transfers between devices with their start and end apart: 6, of which 6 were waited for; matrix products, arithmetic and copies ran while one was open for 0% of the time, Pallas kernels for 5%

profile of v21, /device:TPU:0, one launch (start us, length us, event | category | flops | bytes accessed | tf_op | source)
XLA Modules:
  0.0 164.0 jit_solution(5288890156633440359)
XLA Ops:
  0.6 4.6 %before.1 = (bf16[32,6,32,256]{3,2,1,0:T(8,128)(2,1)S(1)}, bf16[32,128,256]{2,1,0:T(8,128)(2,1)}) custom-call(bf16[32,256,128]{2,1,0:T(8,128)(2,1)} %pair_hbm.5, bf16[32,2,32,256]{3,2,1,0:T(8,128)(2,1)} %bitcast.25, bf16[64,128]{1,0:T(8,128)(2,1)} %bitcast.9, bf16[64,128]{1,0:T(8,128)(2,1)} %bitcast.13, bf16[64,128]{1,0:T(8,128)(2,1)} %bitcast.17, ...), custom_call_target="tpu_custom_call" | custom-call | tf_op jit(solution)/shard_map/before/pallas_call | solution.py:319
  5.2 78.3 %all_to_all.10.in_ref = bf16[32,6,32,256]{3,2,1,0:T(8,128)(2,1)S(1)} all-to-all(bf16[32,6,32,256]{3,2,1,0:T(8,128)(2,1)S(1)} %get-tuple-element.19), channel_id=1, replica_groups=mesh['row'=16,'col'=2] {'row','col'}, dimensions={0} | all-to-all | bytes 6291456 | tf_op jit(solution)/shard_map/all_to_all | solution.py:353
  83.5 1.3 triangle.1
  84.8 0.0 copy-start
  84.8 0.0 copy-start.1
  84.8 0.0 copy-start.2
  84.8 0.0 copy-start.3
  84.9 52.2 %all_to_all.11.d_ref = bf16[32,4,32,256]{3,2,1,0:T(8,128)(2,1)S(1)} all-to-all(bf16[32,4,32,256]{3,2,1,0:T(8,128)(2,1)S(1)} %triangle.1), channel_id=1, replica_groups=mesh['row'=16,'col'=2] {'row','col'}, dimensions={0} | all-to-all | bytes 4194304 | tf_op jit(solution)/shard_map/all_to_all | solution.py:370
  137.0 0.0 copy-done
  137.0 0.0 copy-done.1
  137.0 0.0 copy-done.2
  137.0 0.0 copy-done.3
  137.0 4.0 %gates.1 = (bf16[32,256,256]{2,1,0:T(8,128)(2,1)S(1)}, f32[128,128]{1,0:T(8,128)S(1)}, f32[128,128]{1,0:T(8,128)S(1)}) custom-call(bf16[32,128,256]{2,1,0:T(8,128)(2,1)} %get-tuple-element.18.normed_hbm, bf16[32,4,32,256]{3,2,1,0:T(8,128)(2,1)S(1)} %all_to_all.11.d_ref, bf16[64,128]{1,0:T(8,128)(2,1)S(1)} %bitcast.10, bf16[64,128]{1,0:T(8,128)(2,1)S(1)} %bitcast.14, ...), custom_call_target="tpu_custom_call" | custom-call | tf_op jit(solution)/shard_map/gates/pallas_call | solution.py:356
  141.1 0.1 collective-permute-start
  141.1 1.2 collective-permute-done
  142.4 1.8 %collective-permute-start.1 = (f32[128,128]{1,0:T(8,128)S(1)}, f32[128,128]{1,0:T(8,128)S(1)}, u32[]{:S(2)}, u32[]{:S(2)}) collective-permute-start(f32[128,128]{1,0:T(8,128)S(1)} %add.15), channel_id=1, source_target_pairs={{0,16},{2,18},{4,20},{6,22},{8,24},{10,26},{12,28},{14,30},{16,0},... | collective-permute-start | bytes 196616 | tf_op jit(solution)/shard_map/ppermute | solution.py:400
  144.2 3.8 %input.2.refs_0_ = bf16[32,256,128]{2,1,0:T(8,128)(2,1)} custom-call(bf16[32,256,128]{2,1,0:T(8,128)(2,1)} %pair_hbm.5, bf16[32,256,256]{2,1,0:T(8,128)(2,1)S(1)} %get-tuple-element.22.grads_ref, bf16[64,128]{1,0:T(8,128)(2,1)S(1)} %bitcast.11, bf16[64,128]{1,0:T(8,128)(2,1)S(1)} %bitcast.15, bf16[64,128]{1,0:T(8,128)(2,1)S(1)} %bitcast.19, ...), custom_call_target="tpu_custom_call" | custom-call | flops 268435456 | bytes 2097152 | tf_op jit(solution)/shard_map/input/pallas_call | solution.py:375
  148.0 1.0 collective-permute-done.1
  149.0 0.4 collective-permute-start.2
  149.4 3.8 %input.3 = bf16[32,256,128]{2,1,0:T(8,128)(2,1)} custom-call(bf16[32,256,128]{2,1,0:T(8,128)(2,1)} %pair_hbm.5, bf16[32,256,256]{2,1,0:T(8,128)(2,1)S(1)} %get-tuple-element.22.grads_ref, bf16[64,128]{1,0:T(8,128)(2,1)S(1)} %bitcast.12, bf16[64,128]{1,0:T(8,128)(2,1)S(1)} %bitcast.16, bf16[64,128]{1,0:T(8,128)(2,1)S(1)} %bitcast.20, ...), custom_call_target="tpu_custom_call", output_to_operand_aliasing={{}: (6, {})} | custom-call | flops 268435456 | bytes 2097152 | tf_op jit(solution)/shard_map/input/pallas_call | solution.py:375
  153.2 0.2 collective-permute-done.2
  153.4 1.2 collective-permute-start.3
  154.5 3.2 %collective-permute-done.3 = f32[128,128]{1,0:T(8,128)S(1)} collective-permute-done((f32[128,128]{1,0:T(8,128)S(1)}, f32[128,128]{1,0:T(8,128)S(1)}, u32[]{:S(2)}, u32[]{:S(2)}) %collective-permute-start.3) | collective-permute-done | bytes 65568 | tf_op jit(solution)/shard_map/ppermute | solution.py:400
  157.7 1.4 collective-permute-start.4
  159.2 2.9 %collective-permute-done.4 = f32[128,128]{1,0:T(8,128)S(1)} collective-permute-done((f32[128,128]{1,0:T(8,128)S(1)}, f32[128,128]{1,0:T(8,128)S(1)}, u32[]{:S(2)}, u32[]{:S(2)}) %collective-permute-start.4) | collective-permute-done | bytes 65568 | tf_op jit(solution)/shard_map/ppermute | solution.py:400
  162.1 0.1 collective-permute-start.5
  162.1 1.2 collective-permute-done.5.other_ref
  163.4 0.7 finish.1
  (5 shorter events, 0.0 us)
Async XLA Ops:
  84.8 52.2 %copy-start = (bf16[128,64]{0,1:T(8,128)(2,1)S(1)}, bf16[128,64]{0,1:T(8,128)(2,1)}, u32[]{:S(2)}) copy-start(bf16[128,64]{0,1:T(8,128)(2,1)} %param.8) | copy-start | bytes 49156
  84.8 52.2 %copy-start.1 = (bf16[128,64]{0,1:T(8,128)(2,1)S(1)}, bf16[128,64]{0,1:T(8,128)(2,1)}, u32[]{:S(2)}) copy-start(bf16[128,64]{0,1:T(8,128)(2,1)} %param.9) | copy-start | bytes 49156
  84.8 52.2 %copy-start.2 = (bf16[128,64]{0,1:T(8,128)(2,1)S(1)}, bf16[128,64]{0,1:T(8,128)(2,1)}, u32[]{:S(2)}) copy-start(bf16[128,64]{0,1:T(8,128)(2,1)} %param.10) | copy-start | bytes 49156
  84.8 52.2 %copy-start.3 = (bf16[128,64]{0,1:T(8,128)(2,1)S(1)}, bf16[128,64]{0,1:T(8,128)(2,1)}, u32[]{:S(2)}) copy-start(bf16[128,64]{0,1:T(8,128)(2,1)} %param.11) | copy-start | bytes 49156
  141.1 1.3 collective-permute-start
  142.4 6.6 %collective-permute-start.1 = (f32[128,128]{1,0:T(8,128)S(1)}, f32[128,128]{1,0:T(8,128)S(1)}, u32[]{:S(2)}, u32[]{:S(2)}) collective-permute-start(f32[128,128]{1,0:T(8,128)S(1)} %add.15), channel_id=1, source_target_pairs={{0,16},{2,18},{4,20},{6,22},{8,24},{10,26},{12,28},{14,30},{16,0},... | collective-permute-start | bytes 196616 | tf_op jit(solution)/shard_map/ppermute | solution.py:400
  149.0 4.3 %collective-permute-start.2 = (f32[128,128]{1,0:T(8,128)S(1)}, f32[128,128]{1,0:T(8,128)S(1)}, u32[]{:S(2)}, u32[]{:S(2)}) collective-permute-start(f32[128,128]{1,0:T(8,128)S(1)} %add.16), channel_id=1, source_target_pairs={{0,8},{2,10},{4,12},{6,14},{8,0},{10,2},{12,4},{14,6},{16,24},{18,... | collective-permute-start | bytes 196616 | tf_op jit(solution)/shard_map/ppermute | solution.py:400
  153.4 4.3 %collective-permute-start.3 = (f32[128,128]{1,0:T(8,128)S(1)}, f32[128,128]{1,0:T(8,128)S(1)}, u32[]{:S(2)}, u32[]{:S(2)}) collective-permute-start(f32[128,128]{1,0:T(8,128)S(1)} %add.17), channel_id=1, source_target_pairs={{0,4},{2,6},{4,0},{6,2},{8,12},{10,14},{12,8},{14,10},{16,20},{18,... | collective-permute-start | bytes 196616 | tf_op jit(solution)/shard_map/ppermute | solution.py:400
  157.7 4.3 %collective-permute-start.4 = (f32[128,128]{1,0:T(8,128)S(1)}, f32[128,128]{1,0:T(8,128)S(1)}, u32[]{:S(2)}, u32[]{:S(2)}) collective-permute-start(f32[128,128]{1,0:T(8,128)S(1)} %add.18), channel_id=1, source_target_pairs={{0,1},{1,0},{2,3},{3,2},{4,5},{5,4},{6,7},{7,6},{8,9},{9,8},{10,11... | collective-permute-start | bytes 196616 | tf_op jit(solution)/shard_map/ppermute | solution.py:400
  162.1 1.3 collective-permute-start.5
